TPU v7x, 128 devices: a whole 4x4x4 slice. The times are simulated.
128 devices in a mesh: row: 8 (over z, core), col: 16 (over x, y).
Axes of the slice: x: 4, y: 4, z: 4, core: 2. Of those that a mesh axis runs over, the one named last changes fastest.
Arguments:
- leaf_rhs: bfloat16 [6144, 512, 128], P(('row', 'col')), may hold values from -6 to 6
- leaf_inv: bfloat16 [6144, 128, 128], P(('row', 'col')), as said below
- leaf_off: bfloat16 [6144, 3, 128, 128], P(('row', 'col')), may hold values from -0.0234375 to 0.0234375
- blocks: int32 [6144, 3], P(('row', 'col')), may hold values from 0 to 31, all different within a row
- par_rhs: bfloat16 [32, 512, 128], P('col', 'row'), may hold values from -6 to 6
- par_inv: bfloat16 [32, 128, 128], P('col', 'row'), as said below
Outputs:
- leaf_x: bfloat16 [6144, 512, 128], P(('row', 'col'))
- par_x: bfloat16 [32, 512, 128], P('col', 'row')
Inputs may be any that keep to these rules, and one draw needn't show every extreme that they name: `blocks`: each row names 3 different parent supernodes, and every parent supernode is named by some row. `leaf_inv`: each block is lower triangular with a diagonal between 0.8 and 1.25. `par_inv`: each block is lower triangular with a diagonal between 0.8 and 1.25.
All inputs are finite; a program needn't handle non-finite values.
Results may differ from a plain program's by a relative error of at most 0.0053.
Values may be sent and summed in bfloat16 or wider, within the bound.
No kernel may reach another device: no remote copies, remote signals or barrier semaphores. Data moves between devices by JAX's collectives and lax.ppermute only.
A program may use at most 192 MiB of HBM per device.

v0:
```python
import jax
import jax.numpy as jnp
from jax import lax
from jax.sharding import PartitionSpec as P


def owner_term(contrib, parent_ids, length):
    targets = lax.broadcasted_iota(jnp.int32, (1, 1, length), 2)
    onehot = (parent_ids[:, :, None] == targets).astype(jnp.float32)
    return jnp.einsum("jkp,jkrc->prc", onehot, contrib, precision=lax.Precision.HIGHEST)


def on_device(leaf_rhs, leaf_inv, leaf_off, blocks, par_rhs, par_inv):
    highest = lax.Precision.HIGHEST
    leaf_y = jnp.einsum(
        "jrc,jbc->jrb", leaf_rhs, leaf_inv, preferred_element_type=jnp.float32
    ).astype(jnp.bfloat16)
    contrib = jnp.einsum("jrb,jkcb->jkrc", leaf_y, leaf_off, preferred_element_type=jnp.float32)
    keep_rows = par_rhs.shape[0]
    width = par_rhs.shape[2]
    owned = lax.psum_scatter(
        owner_term(contrib, blocks, lax.axis_size("col") * keep_rows),
        "col",
        scatter_dimension=0,
        tiled=True,
    )
    updates = lax.psum_scatter(owned, "row", scatter_dimension=1, tiled=True)
    inverse = lax.all_gather(par_inv, "row", axis=1, tiled=True)
    remainder = par_rhs.astype(jnp.float32) - updates
    par_y = jnp.einsum(
        "prc,pbc->prb", remainder, inverse.astype(jnp.float32), precision=highest
    ).astype(jnp.bfloat16)
    par_x = jnp.einsum("prb,pbc->prc", par_y, inverse, preferred_element_type=jnp.float32).astype(
        jnp.bfloat16
    )
    solved_rows = lax.all_gather(par_x, "row", axis=1, tiled=True)
    every_x = lax.all_gather(solved_rows, "col", axis=0, tiled=True)
    leaf_count = blocks.shape[0]
    fanout = blocks.shape[1]
    chosen = jnp.take(every_x, blocks.reshape(-1), axis=0).reshape(
        leaf_count, fanout, every_x.shape[1], width
    )
    back = jnp.einsum("jkrc,jkcb->jrb", chosen, leaf_off, preferred_element_type=jnp.float32)
    leaf_x = jnp.einsum(
        "jrb,jbc->jrc",
        leaf_y.astype(jnp.float32) - back,
        leaf_inv.astype(jnp.float32),
        precision=highest,
    ).astype(jnp.bfloat16)
    return (leaf_x, par_x)


def solution(mesh):
    return jax.shard_map(
        on_device,
        mesh=mesh,
        in_specs=(
            P(("row", "col"), None, None),
            P(("row", "col"), None, None),
            P(("row", "col"), None, None, None),
            P(("row", "col"), None),
            P("col", "row", None),
            P("col", "row", None),
        ),
        out_specs=(P(("row", "col"), None, None), P("col", "row", None)),
        check_vma=False,
    )
```

profile of v0, /device:TPU:1, one launch (start us, length us, event | category | flops | bytes accessed | tf_op | source)
XLA Modules:
  0.0 345.3 jit_solution(4750256746784526357)
XLA Ops:
  7.2 0.0 copy-start
  7.2 0.0 reduce-scatter.2.cloned.1.call-start
  7.2 1.4 copy-done
  8.6 7.2 %convolution_convert_fusion = bf16[48,512,128]{2,1,0:T(8,128)(2,1)} fusion(bf16[48,512,128]{2,1,0:T(8,128)(2,1)} %param.6, bf16[48,128,128]{2,1,0:T(8,128)(2,1)S(1)} %copy-done), kind=kOutput, calls=%fused_computation.12 | convolution fusion | flops 808452096 | bytes 14155776 | tf_op jit(solution)/shard_map/jrc,jbc->jrb/dot_general | solution.py:15
  15.8 0.0 copy-start.3
  15.8 18.0 %convolution_bitcast_fusion = f32[48,3,512,128]{3,2,1,0:T(8,128)} fusion(bf16[48,3,128,128]{3,2,1,0:T(8,128)(2,1)} %param.8, bf16[48,512,128]{2,1,0:T(8,128)(2,1)} %convolution_convert_fusion), kind=kOutput, calls=%fused_computation.6 | convolution fusion | flops 2415919104 | bytes 48758784 | tf_op jit(solution)/shard_map/jrb,jkcb->jkrc/dot_general | solution.py:18
  33.8 0.0 copy-done.3
  33.8 42.0 %fusion.10 = f32[32,512,128]{2,0,1:T(8,128)S(1)} fusion(f32[48,3,512,128]{3,2,1,0:T(8,128)} %convolution_bitcast_fusion, s32[48,3]{0,1:T(4,128)S(1)} %copy-done.3), kind=kOutput, calls=%fused_computation.14 | convolution fusion | flops 3623883264 | bytes 46137920 | tf_op jit(solution)/shard_map/jkp,jkrc->prc/dot_general | solution.py:10
  75.7 8.1 %copy.27 = f32[32,512,128]{2,1,0:T(8,128)} copy(f32[32,512,128]{2,0,1:T(8,128)S(1)} %fusion.10) | data formatting | bytes 16777216 | tf_op jit(solution)/shard_map/jkp,jkrc->prc/dot_general | solution.py:10
  83.8 0.0 copy-start.5
  83.8 0.0 copy-start.4
  83.8 0.0 copy-start.2
  83.8 0.0 reduce-scatter.2.cloned.1.call-update
  83.8 0.0 all-reduce.3.cloned.1.call-start
  83.9 87.2 %reduce-scatter.2.cloned.1.call-done = f32[2,512,128]{2,1,0:T(8,128)} async-done(((f32[32,512,128]{2,1,0:T(8,128)}), f32[2,512,128]{2,1,0:T(8,128)}) %reduce-scatter.2.cloned.1.call-update) | async-done | bytes 524304 | tf_op jit(solution)/shard_map/reduce_scatter | solution.py:21
  171.1 2.2 copy.28
  173.3 0.0 all-reduce.3.cloned.1.call-update
  173.3 0.0 all-gather.2.cloned.1.call-start
  173.4 0.0 copy-done.5
  173.4 0.6 dynamic-slice
  174.6 0.0 copy-done.4
  174.6 14.9 %all_gather.9 = bf16[2,128,128]{2,1,0:T(8,128)(2,1)S(1)} all-gather(bf16[2,16,128]{2,1,0:T(8,128)(2,1)S(1)} %copy-done.4), channel_id=1, replica_groups=mesh['row'=8,'col'=16] {'row'}, dimensions={1}, use_global_device_ids=true | all-gather | bytes 73728 | tf_op jit(solution)/shard_map/all_gather | solution.py:28
  189.6 43.9 %all-reduce.3.cloned.1.call-done = f32[2,512,128]{2,0,1:T(2,128)} async-done(((f32[2,512,128]{2,0,1:T(2,128)}), f32[2,512,128]{2,0,1:T(2,128)}) %all-reduce.3.cloned.1.call-update) | async-done | bytes 524304
  233.5 0.8 constant_dynamic-slice_fusion
  234.3 0.0 copy-done.2
  234.3 0.2 convolution_convert_fusion.2
  234.6 0.1 convolution_convert_fusion.1
  234.7 0.0 copy-start.1
  234.7 16.5 %all_gather.10 = bf16[2,512,128]{2,1,0:T(8,128)(2,1)} all-gather(bf16[2,64,128]{2,1,0:T(8,128)(2,1)S(1)} %convolution_convert_fusion.1), channel_id=1, replica_groups=mesh['row'=8,'col'=16] {'row'}, dimensions={1}, use_global_device_ids=true | all-gather | bytes 294912 | tf_op jit(solution)/shard_map/all_gather | solution.py:36
  251.2 0.0 all-gather.2.cloned.1.call-update
  251.3 0.1 copy.30
  251.4 0.1 reshape.45
  251.5 0.1 copy.25
  251.6 50.3 %all-gather.2.cloned.1.call-done = bf16[32,512,128]{2,1,0:T(8,128)(2,1)} async-done(((bf16[2,512,128]{2,1,0:T(8,128)(2,1)}), bf16[32,512,128]{2,1,0:T(8,128)(2,1)}) %all-gather.2.cloned.1.call-update) | async-done | bytes 4194320 | tf_op jit(solution)/shard_map/all_gather | solution.py:37
  301.9 11.5 %gather_fusion = bf16[144,512,128]{2,1,0:T(8,128)(2,1)} fusion(bf16[32,512,128]{2,1,0:T(8,128)(2,1)} %all-gather.2.cloned.1.call-done, s32[1024]{0:T(1024)S(1)} %pad_clamp_fusion), kind=kCustom, calls=%fused_computation | custom fusion | bytes 37749312 | tf_op jit(solution)/shard_map/jit(_take)/gather | solution.py:40
  313.4 0.0 copy-done.1
  313.4 13.0 %fusion.2 = f32[48,512,128,1]{2,1,3,0:T(8,128)} fusion(bf16[48,3,128,128]{3,2,1,0:T(8,128)(2,1)} %param.8, bf16[48,3,512,128]{3,2,1,0:T(8,128)(2,1)} %bitcast.30, pred[48,3]{1,0:T(8,128)(4,1)S(1)} %copy.25), kind=kOutput, calls=%fused_computation.3 | convolution fusion | flops 2425356288 | bytes 36176016 | tf_op jit(solution)/shard_map/jkrc,jkcb->jrb/dot_general | solution.py:43
  326.5 12.3 %fusion.9 = bf16[48,512,128]{2,1,0:T(8,128)(2,1)} fusion(bf16[48,128,128]{2,1,0:T(8,128)(2,1)S(1)} %copy-done, f32[48,512,128,1]{2,1,3,0:T(8,128)} %fusion.2, bf16[48,512,128]{2,1,0:T(8,128)(2,1)} %convolution_convert_fusion), kind=kOutput, calls=%fused_computation.13 | convolution fusion | flops 4841275392 | bytes 26738688 | tf_op jit(solution)/shard_map/jrb,jbc->jrc/dot_general | solution.py:44
  (3 shorter events, 0.0 us)
Async XLA Ops:
  7.2 1.4 copy-start
  7.2 163.9 %reduce-scatter.2.cloned.1.call-start = ((), (), s32[]{:S(2)}) async-start(), calls=%async_computation.1 | async-start | bytes 8912896 | tf_op jit(solution)/shard_map/reduce_scatter | solution.py:21
  15.8 18.0 %copy-start.3 = (s32[48,3]{0,1:T(4,128)S(1)}, s32[48,3]{0,1:T(4,128)}, u32[]{:S(2)}) copy-start(s32[48,3]{0,1:T(4,128)} %param.9) | copy-start | bytes 1732
  83.8 89.6 %copy-start.5 = (u32[128]{0:T(128)S(1)}, u32[128]{0:T(128)}, u32[]{:S(2)}) copy-start(u32[128]{0:T(128)} %constant.24) | copy-start | bytes 1540
  83.8 90.8 %copy-start.4 = (bf16[2,16,128]{2,1,0:T(8,128)(2,1)S(1)}, bf16[2,16,128]{2,1,0:T(8,128)(2,1)}, u32[]{:S(2)}) copy-start(bf16[2,16,128]{2,1,0:T(8,128)(2,1)} %param.11) | copy-start | bytes 24580
  83.8 150.5 %copy-start.2 = (bf16[2,64,128]{2,1,0:T(8,128)(2,1)S(1)}, bf16[2,64,128]{2,1,0:T(8,128)(2,1)}, u32[]{:S(2)}) copy-start(bf16[2,64,128]{2,1,0:T(8,128)(2,1)} %param.10) | copy-start | bytes 98308
  83.8 149.6 %all-reduce.3.cloned.1.call-start = ((), (), s32[]{:S(2)}) async-start(), calls=%async_computation.3 | async-start | bytes 1048576
  173.3 128.6 %all-gather.2.cloned.1.call-start = ((), (), s32[]{:S(2)}) async-start(), calls=%async_computation.2 | async-start | bytes 4456448 | tf_op jit(solution)/shard_map/all_gather | solution.py:37
  234.7 78.7 %copy-start.1 = (bf16[2,64,128]{2,1,0:T(8,128)(2,1)}, bf16[2,64,128]{2,1,0:T(8,128)(2,1)S(1)}, u32[]{:S(2)}) copy-start(bf16[2,64,128]{2,1,0:T(8,128)(2,1)S(1)} %convolution_convert_fusion.1) | copy-start | bytes 98308
Sparse Core Ops, SparseCore 0:
  84.0 87.0 reduce-scatter.1
  174.0 59.4 all-reduce.2
  251.4 50.4 all-gather.1
where the time goes:
time: 346 us; the launch traced here: 345 us
  waiting for transfers between devices  181 us (52%)
  matrix products  92.8 us (27%)
  blocking collectives  31.5 us (9%)
  local copies, waits for them, and re-layouts  25 us (7%)
  between operations  14.5 us (4%)
    reduce_scatter x1, waiting for transfers between devices, on_device(): lax.psum_scatter(owner_term(contrib, blocks, lax.axis_size('col') * keep_...  87.2 us
    all_gather x1, waiting for transfers between devices, on_device(): every_x = lax.all_gather(solved_rows, 'col', axis=0, tiled=True)  50.3 us
    unnamed x4, waiting for transfers between devices  44 us
    dot_general x1, matrix products, owner_term(): jnp.einsum('jkp,jkrc->prc', onehot, contrib, precision=lax.Precision.HIGH...  42 us
    dot_general x1, matrix products, on_device(): jnp.einsum('jrb,jkcb->jkrc', leaf_y, leaf_off, preferred_element_type=jnp...  18 us
    all_gather x1, blocking collectives, on_device(): solved_rows = lax.all_gather(par_x, 'row', axis=1, tiled=True)  16.5 us
    all_gather x1, blocking collectives, on_device(): inverse = lax.all_gather(par_inv, 'row', axis=1, tiled=True)  14.9 us
    dot_general x1, matrix products, on_device(): jnp.einsum('jkrc,jkcb->jrb', chosen, leaf_off, preferred_element_type=jnp...  13 us
  transfers between devices with their start and end apart: 3, of which 3 were waited for; matrix products, arithmetic and copies ran while one was open for 0% of the time, Pallas kernels for 0%

commit v1 on v0

v1 whole, which is shorter than its diff:
```python
import functools

import jax
import jax.numpy as jnp
from jax import lax
from jax.experimental import pallas as pl
from jax.experimental.pallas import tpu as pltpu
from jax.sharding import PartitionSpec as P

F32, BF16 = jnp.float32, jnp.bfloat16
VMEM_LIMIT = 56 * 1024 * 1024
CORES = 2


def params(n=1):
    return pltpu.CompilerParams(
        vmem_limit_bytes=VMEM_LIMIT, dimension_semantics=("arbitrary",) * n
    )


def mm_t(a, b):
    return lax.dot_general(a, b, (((1,), (1,)), ((), ())), preferred_element_type=F32)


def mm(a, b):
    return jnp.dot(a, b, preferred_element_type=F32)


def forward_kernel(step_leaves, fanout, heights, blocks, core, rhs, inv, off, y_out, keep, send, acc):
    step = pl.program_id(0)
    parents, block_rows, width = acc.shape[2:]

    @pl.when(step == 0)
    def _():
        acc[...] = jnp.zeros_like(acc)

    for i in range(step_leaves):
        y = mm_t(rhs[i], inv[i]).astype(BF16)
        y_out[i] = y
        for k in range(fanout):
            parent = blocks[(step * step_leaves + i) * fanout + k]
            part = mm_t(y, off[i, k])
            for z in range(heights):
                for c in range(CORES):
                    at = (z * CORES + c) * block_rows
                    acc[c, z, parent] += part[at : at + block_rows]

    @pl.when(step == pl.num_programs(0) - 1)
    def _():
        me = core[0]
        keep[...] = acc[me]
        send[...] = acc[1 - me].astype(BF16)


def forward(blocks, core, rhs, inv, off, parents, rows):
    leaves, nrhs, width = rhs.shape
    fanout = off.shape[1]
    heights = rows // CORES
    block_rows = nrhs // rows
    g = 4
    half = (heights, parents, block_rows, width)
    return pl.pallas_call(
        functools.partial(forward_kernel, g, fanout, heights),
        grid_spec=pltpu.PrefetchScalarGridSpec(
            num_scalar_prefetch=2,
            grid=(leaves // g,),
            in_specs=[
                pl.BlockSpec((g, nrhs, width), lambda s, *_: (s, 0, 0)),
                pl.BlockSpec((g, width, width), lambda s, *_: (s, 0, 0)),
                pl.BlockSpec((g, fanout, width, width), lambda s, *_: (s, 0, 0, 0)),
            ],
            out_specs=[
                pl.BlockSpec((g, nrhs, width), lambda s, *_: (s, 0, 0)),
                pl.BlockSpec(half, lambda s, *_: (0, 0, 0, 0)),
                pl.BlockSpec(half, lambda s, *_: (0, 0, 0, 0)),
            ],
            scratch_shapes=[pltpu.VMEM((CORES,) + half, F32)],
        ),
        out_shape=[
            jax.ShapeDtypeStruct(rhs.shape, BF16),
            jax.ShapeDtypeStruct(half, F32),
            jax.ShapeDtypeStruct(half, BF16),
        ],
        compiler_params=params(),
        name="forward",
        cost_estimate=pl.CostEstimate(
            flops=2 * leaves * nrhs * width * width * (1 + fanout),
            bytes_accessed=26_000_000,
            transcendentals=0,
        ),
    )(blocks, core, rhs, inv, off)


def fold_kernel(step_leaves, fanout, inv, off, out):
    for i in range(step_leaves):
        for k in range(fanout):
            out[i, k] = mm(off[i, k], inv[i]).astype(BF16)


def fold(inv, off):
    leaves, fanout, width, _ = off.shape
    g = 8
    return pl.pallas_call(
        functools.partial(fold_kernel, g, fanout),
        grid=(leaves // g,),
        in_specs=[
            pl.BlockSpec((g, width, width), lambda s: (s, 0, 0)),
            pl.BlockSpec((g, fanout, width, width), lambda s: (s, 0, 0, 0)),
        ],
        out_specs=pl.BlockSpec((g, fanout, width, width), lambda s: (s, 0, 0, 0)),
        out_shape=jax.ShapeDtypeStruct(off.shape, BF16),
        compiler_params=params(),
        name="fold",
        cost_estimate=pl.CostEstimate(
            flops=2 * leaves * fanout * width**3,
            bytes_accessed=11_000_000,
            transcendentals=0,
        ),
    )(inv, off)


def parent_kernel(sources, got, rhs, inv, x_out, x_every):
    own, block_rows, width = rhs.shape
    total = got[0].astype(F32)
    for s in range(1, sources):
        total += got[s].astype(F32)
    for p in range(own):
        rest = rhs[p].astype(F32) - total[p]
        high = rest.astype(BF16)
        left = rest - high.astype(F32)
        mid = left.astype(BF16)
        low = (left - mid.astype(F32)).astype(BF16)
        w = inv[p]
        y = (mm_t(low, w) + mm_t(mid, w)) + mm_t(high, w)
        x = mm(y.astype(BF16), w).astype(BF16)
        x_out[p] = x
        for s in range(sources):
            x_every[s, p] = x


def parent(got, rhs, inv):
    sources = got.shape[0]
    return pl.pallas_call(
        functools.partial(parent_kernel, sources),
        out_shape=[
            jax.ShapeDtypeStruct(rhs.shape, BF16),
            jax.ShapeDtypeStruct(got.shape, BF16),
        ],
        compiler_params=params(0),
        name="parent",
        cost_estimate=pl.CostEstimate(
            flops=30_000_000, bytes_accessed=4_500_000, transcendentals=0
        ),
    )(got, rhs, inv)


def backward_kernel(step_leaves, fanout, heights, blocks, core, y, inv, folded, mine, other, out, xs, lhs):
    step = pl.program_id(0)
    block_rows, width = mine.shape[2:]

    @pl.when(step == 0)
    def _():
        me = core[0]
        xs[me] = mine[...]
        xs[1 - me] = other[...]

    for i in range(step_leaves):
        for k in range(fanout):
            p = blocks[(step * step_leaves + i) * fanout + k]
            for z in range(heights):
                for c in range(CORES):
                    at = (z * CORES + c) * block_rows
                    lhs[i, at : at + block_rows, k * width : (k + 1) * width] = xs[c, z, p]
        back = mm(lhs[i], folded[i].reshape(fanout * width, width))
        out[i] = (mm(y[i], inv[i]) - back).astype(BF16)


def backward(blocks, core, y, inv, folded, mine, other):
    leaves, nrhs, width = y.shape
    fanout = folded.shape[1]
    heights = mine.shape[0]
    g = 4
    return pl.pallas_call(
        functools.partial(backward_kernel, g, fanout, heights),
        grid_spec=pltpu.PrefetchScalarGridSpec(
            num_scalar_prefetch=2,
            grid=(leaves // g,),
            in_specs=[
                pl.BlockSpec((g, nrhs, width), lambda s, *_: (s, 0, 0)),
                pl.BlockSpec((g, width, width), lambda s, *_: (s, 0, 0)),
                pl.BlockSpec((g, fanout, width, width), lambda s, *_: (s, 0, 0, 0)),
                pl.BlockSpec(mine.shape, lambda s, *_: (0, 0, 0, 0)),
                pl.BlockSpec(mine.shape, lambda s, *_: (0, 0, 0, 0)),
            ],
            out_specs=pl.BlockSpec((g, nrhs, width), lambda s, *_: (s, 0, 0)),
            scratch_shapes=[
                pltpu.VMEM((CORES,) + mine.shape, BF16),
                pltpu.VMEM((g, nrhs, fanout * width), BF16),
            ],
        ),
        out_shape=jax.ShapeDtypeStruct(y.shape, BF16),
        compiler_params=params(),
        name="backward",
        cost_estimate=pl.CostEstimate(
            flops=2 * leaves * nrhs * width * width * (1 + fanout),
            bytes_accessed=23_000_000,
            transcendentals=0,
        ),
    )(blocks, core, y, inv, folded, mine, other)


def gather_inverse(par_inv, rows):
    own, part, width = par_inv.shape
    heights = rows // CORES
    place = lax.axis_index("row")
    across = lax.ppermute(par_inv, "row", [(r, r ^ 1) for r in range(rows)])
    pair = jnp.where(
        place % CORES == 0, jnp.stack([par_inv, across]), jnp.stack([across, par_inv])
    )
    parts = [pair] + [
        lax.ppermute(pair, "row", [(r, (r + CORES * s) % rows) for r in range(rows)])
        for s in range(1, heights)
    ]
    z = place // CORES
    stacked = jnp.stack(parts)
    whole = jnp.zeros_like(stacked)
    for h in range(heights):
        pick = sum(
            jnp.where((z - h) % heights == s, parts[s].astype(F32), 0.0) for s in range(heights)
        )
        whole = whole.at[h].set(pick.astype(BF16))
    return whole.transpose(2, 0, 1, 3, 4).reshape(own, rows * part, width)


def on_device(rows, cols, leaf_rhs, leaf_inv, leaf_off, blocks, par_rhs, par_inv):
    own, block_rows, width = par_rhs.shape
    parents = own * cols
    heights = rows // CORES
    chips = heights * cols
    core = (lax.axis_index("row") % CORES).astype(jnp.int32).reshape(1)
    flat = blocks.reshape(-1)
    swap = [(r, r ^ 1) for r in range(rows)]
    groups = [
        [(z * CORES + c) * cols + k for z in range(heights) for k in range(cols)]
        for c in range(CORES)
    ]
    spread = functools.partial(
        lax.all_to_all,
        axis_name=("row", "col"),
        split_axis=0,
        concat_axis=0,
        axis_index_groups=groups,
        tiled=True,
    )

    inverse = gather_inverse(par_inv, rows)
    leaf_y, keep, send = forward(flat, core, leaf_rhs, leaf_inv, leaf_off, parents, rows)
    chip = (keep + lax.ppermute(send, "row", swap).astype(F32)).astype(BF16)
    got = spread(chip.reshape(chips, own, block_rows, width))
    folded = fold(leaf_inv, leaf_off)
    par_x, every = parent(got, par_rhs, inverse)
    mine = spread(every).reshape(heights, parents, block_rows, width)
    other = lax.ppermute(mine, "row", swap)
    leaf_x = backward(flat, core, leaf_y, leaf_inv, folded, mine, other)
    return (leaf_x, par_x)


def solution(mesh):
    rows, cols = mesh.shape["row"], mesh.shape["col"]
    return jax.shard_map(
        functools.partial(on_device, rows, cols),
        mesh=mesh,
        in_specs=(
            P(("row", "col"), None, None),
            P(("row", "col"), None, None),
            P(("row", "col"), None, None, None),
            P(("row", "col"), None),
            P("col", "row", None),
            P("col", "row", None),
        ),
        out_specs=(P(("row", "col"), None, None), P("col", "row", None)),
        check_vma=False,
    )
```

time: 346 us -> 141 us (0.41)
  waiting for transfers between devices: 181 us -> 24.9 us
  matrix products: 92.8 us -> 0 us
  Pallas kernels: 0 us -> 48.8 us
  starting transfers between devices: 0.12 us -> 22.5 us
  local copies, waits for them, and re-layouts: 25 us -> 4.66 us
  between operations: 14.5 us -> 0.7 us
  other arithmetic: 0.02 us -> 4.37 us
    dot_general x7 -> x0, matrix products: 92.8 us -> none  [the longest x1 42 us: owner_term(): jnp.einsum('jkp,jkrc->prc', onehot, contrib, precision=lax.Precision.HIGH...]
    reduce_scatter x1 -> x0, waiting for transfers between devices: 87.2 us -> none  [on_device(): lax.psum_scatter(owner_term(contrib, blocks, lax.axis_size('col') * keep_...]
    all_gather x1 -> x0, waiting for transfers between devices: 50.3 us -> none  [on_device(): every_x = lax.all_gather(solved_rows, 'col', axis=0, tiled=True)]
    pallas_call x0 -> x4, Pallas kernels: none -> 48.8 us  [the longest x1 20.8 us: forward(): pl.pallas_call(functools.partial(forward_kernel, g, fanout, heights), gri...]
    unnamed x4 -> x0, waiting for transfers between devices: 44 us -> none
    all_to_all x0 -> x1, blocking collectives: none -> 34.1 us  [on_device(): mine = spread(every).reshape(heights, parents, block_rows, width)]
    all_gather x2 -> x0, blocking collectives: 31.5 us -> none  [the longest x1 16.5 us: on_device(): solved_rows = lax.all_gather(par_x, 'row', axis=1, tiled=True)]
    all_to_all x0 -> x1, waiting for transfers between devices: none -> 17.1 us  [on_device(): got = spread(chip.reshape(chips, own, block_rows, width))]
  transfers between devices with their start and end apart: 3 -> 7, of which waited for: 3 -> 4; matrix products, arithmetic and copies ran while one was open for 0% -> 1% of each run, Pallas kernels for 0% -> 5%
where the time goes in v1:
time: 141 us; the launch traced here: 140 us
  Pallas kernels  48.8 us (35%)
  blocking collectives  34.1 us (24%)
  waiting for transfers between devices  24.9 us (18%)
  starting transfers between devices  22.5 us (16%)
  local copies, waits for them, and re-layouts  4.66 us (3%)
  other arithmetic  4.37 us (3%)
    all_to_all x1, blocking collectives, on_device(): mine = spread(every).reshape(heights, parents, block_rows, width)  34.1 us
    pallas_call x1, Pallas kernels, forward(): pl.pallas_call(functools.partial(forward_kernel, g, fanout, heights), gri...  20.8 us
    all_to_all x1, waiting for transfers between devices, on_device(): got = spread(chip.reshape(chips, own, block_rows, width))  17.1 us
    pallas_call x1, Pallas kernels, backward(): pl.pallas_call(functools.partial(backward_kernel, g, fanout, heights), gr...  16.9 us
    all_to_all x1, starting transfers between devices, on_device(): got = spread(chip.reshape(chips, own, block_rows, width))  11.3 us
    pallas_call x1, Pallas kernels, fold(): pl.pallas_call(functools.partial(fold_kernel, g, fanout), grid=(leaves //...  7.26 us
    ppermute x3, starting transfers between devices, gather_inverse(): lax.ppermute(pair, 'row', [(r, (r + CORES * s) % rows) for r in range(row...  5.57 us
    convert_element_type x1, other arithmetic, on_device(): chip = (keep + lax.ppermute(send, 'row', swap).astype(F32)).astype(BF16)  4.25 us
  transfers between devices with their start and end apart: 7, of which 4 were waited for; matrix products, arithmetic and copies ran while one was open for 1% of the time, Pallas kernels for 5%

profile of v1, /device:TPU:1, one launch (start us, length us, event | category | flops | bytes accessed | tf_op | source)
XLA Modules:
  0.0 140.1 jit_solution(1030193551436875825)
XLA Ops:
  0.6 0.8 copy.9
  1.4 0.6 reshape.180.blocks
  2.0 20.8 %forward.1 = (bf16[48,512,128]{2,1,0:T(8,128)(2,1)}, f32[4,32,64,128]{3,2,1,0:T(8,128)}, bf16[4,32,64,128]{3,2,1,0:T(8,128)(2,1)}) custom-call(s32[144]{0:T(256)} %reshape.180.blocks, s32[1]{0:T(128)} %bitcast.core, bf16[48,512,128]{2,1,0:T(8,128)(2,1)} %rhs.6, bf16[48,128,128]{2,1,0:T(8,128)(2,1)} %inv.5, bf16[48,3,128,128]{3,2,1,0:T(8,128)(2,1)} %off.3), custom_call_target="tpu_custom_call" | custom-call | flops 3221225472 | bytes 26000000 | tf_op jit(solution)/shard_map/forward/pallas_call | solution.py:62
  22.8 1.4 %collective-permute-start = (bf16[4,32,64,128]{3,2,1,0:T(8,128)(2,1)}, bf16[4,32,64,128]{3,2,1,0:T(8,128)(2,1)S(1)}, u32[]{:S(2)}, u32[]{:S(2)}) collective-permute-start(bf16[4,32,64,128]{3,2,1,0:T(8,128)(2,1)} %get-tuple-element.57), channel_id=1, source_target_pairs={{0,16},{16,0},{32,48},{48,32},{64,80},{80,64},{96,112},{112,96},{1... | collective-permute-start | bytes 6291464 | tf_op jit(solution)/shard_map/ppermute | solution.py:258
  24.3 4.0 %collective-permute-done = bf16[4,32,64,128]{3,2,1,0:T(8,128)(2,1)S(1)} collective-permute-done((bf16[4,32,64,128]{3,2,1,0:T(8,128)(2,1)}, bf16[4,32,64,128]{3,2,1,0:T(8,128)(2,1)S(1)}, u32[]{:S(2)}, u32[]{:S(2)}) %collective-permute-start) | collective-permute-done | bytes 2097184 | tf_op jit(solution)/shard_map/ppermute | solution.py:258
  28.3 4.2 %add_convert_fusion = bf16[4,32,64,128]{3,2,1,0:T(8,128)(2,1)} fusion(f32[4,32,64,128]{3,2,1,0:T(8,128)} %get-tuple-element.56, bf16[4,32,64,128]{3,2,1,0:T(8,128)(2,1)S(1)} %collective-permute-done), kind=kLoop, calls=%fused_computation | loop fusion | flops 3145728 | bytes 8388608 | tf_op jit(solution)/shard_map/convert_element_type | solution.py:258
  32.5 0.0 copy-start.3
  32.5 11.3 %all-to-all-start = ((bf16[64,2,64,128]{3,2,1,0:T(8,128)(2,1)}), bf16[64,2,64,128]{3,2,1,0:T(8,128)(2,1)S(1)}, u32[]{:S(2)}, u32[]{:S(2)}) async-start(bf16[64,2,64,128]{3,2,1,0:T(8,128)(2,1)} %bitcast.23), calls=%async_computation | async-start | bytes 4194304 | tf_op jit(solution)/shard_map/all_to_all | solution.py:259
  43.9 0.0 copy-done.3
  43.9 0.7 collective-permute-start.1
  44.6 0.8 collective-permute-done.1
  45.5 2.9 %collective-permute-start.3 = (bf16[2,2,16,128]{3,2,1,0:T(8,128)(2,1)S(1)}, bf16[2,2,16,128]{3,2,1,0:T(8,128)(2,1)S(1)}, u32[]{:S(2)}, u32[]{:S(2)}) collective-permute-start(bf16[2,2,16,128]{3,2,1,0:T(8,128)(2,1)S(1)} %maximum_select_fusion), channel_id=1, source_target_pairs={{0,64},{16,80},{32,96},{48,112},{64,0},{80,16},{96,32},{112,48},{1... | collective-permute-start | bytes 49160 | tf_op jit(solution)/shard_map/ppermute | solution.py:221
  48.3 0.4 collective-permute-start.2
  48.7 2.3 %collective-permute-start.4 = (bf16[2,2,16,128]{3,2,1,0:T(8,128)(2,1)S(1)}, bf16[2,2,16,128]{3,2,1,0:T(8,128)(2,1)S(1)}, u32[]{:S(2)}, u32[]{:S(2)}) collective-permute-start(bf16[2,2,16,128]{3,2,1,0:T(8,128)(2,1)S(1)} %maximum_select_fusion), channel_id=1, source_target_pairs={{0,96},{16,112},{32,0},{48,16},{64,32},{80,48},{96,64},{112,80},{1... | collective-permute-start | bytes 49160 | tf_op jit(solution)/shard_map/ppermute | solution.py:221
  51.0 0.0 collective-permute-done.3
  51.0 3.0 %collective-permute-done.2 = bf16[2,2,16,128]{3,2,1,0:T(8,128)(2,1)S(1)} collective-permute-done((bf16[2,2,16,128]{3,2,1,0:T(8,128)(2,1)S(1)}, bf16[2,2,16,128]{3,2,1,0:T(8,128)(2,1)S(1)}, u32[]{:S(2)}, u32[]{:S(2)}) %collective-permute-start.2) | collective-permute-done | bytes 16416 | tf_op jit(solution)/shard_map/ppermute | solution.py:221
  54.0 0.0 collective-permute-done.4
  54.2 0.6 copy.10
  54.8 17.1 %all-to-all-done.got = bf16[64,2,64,128]{3,2,1,0:T(8,128)(2,1)S(1)} async-done(((bf16[64,2,64,128]{3,2,1,0:T(8,128)(2,1)}), bf16[64,2,64,128]{3,2,1,0:T(8,128)(2,1)S(1)}, u32[]{:S(2)}, u32[]{:S(2)}) %all-to-all-start) | async-done | bytes 2097184 | tf_op jit(solution)/shard_map/all_to_all | solution.py:259
  71.9 0.0 copy-start.1
  71.9 1.3 copy-done.1
  73.2 3.8 %parent.1 = (bf16[2,64,128]{2,1,0:T(8,128)(2,1)}, bf16[64,2,64,128]{3,2,1,0:T(8,128)(2,1)}) custom-call(bf16[64,2,64,128]{3,2,1,0:T(8,128)(2,1)} %copy-done.1, bf16[2,64,128]{2,1,0:T(8,128)(2,1)} %rhs.7, bf16[2,128,128]{2,1,0:T(8,128)(2,1)} %bitcast.24), custom_call_target="tpu_custom_call" | custom-call | flops 30000000 | bytes 4500000 | tf_op jit(solution)/shard_map/parent/pallas_call | solution.py:143
  77.0 34.1 %all_to_all.10 = bf16[64,2,64,128]{3,2,1,0:T(8,128)(2,1)S(1)} all-to-all(bf16[64,2,64,128]{3,2,1,0:T(8,128)(2,1)} %get-tuple-element.58), channel_id=1, replica_groups={{0,1,2,3,4,5,6,7,8,9,10,11,12,13,14,15,32,33,34,35,36,37,38,39,40,41,42..., dimensions={0} | all-to-all | bytes 4194304 | tf_op jit(solution)/shard_map/all_to_all | solution.py:262
  111.1 0.0 copy-start
  111.1 3.5 %collective-permute-start.5 = (bf16[4,32,64,128]{3,2,1,0:T(8,128)(2,1)S(1)}, bf16[4,32,64,128]{3,2,1,0:T(8,128)(2,1)S(1)}, u32[]{:S(2)}, u32[]{:S(2)}) collective-permute-start(bf16[4,32,64,128]{3,2,1,0:T(8,128)(2,1)S(1)} %bitcast.21), channel_id=1, source_target_pairs={{0,16},{16,0},{32,48},{48,32},{64,80},{80,64},{96,112},{112,96},{1... | collective-permute-start | bytes 6291464 | tf_op jit(solution)/shard_map/ppermute | solution.py:263
  114.6 7.3 %fold.1.folded = bf16[48,3,128,128]{3,2,1,0:T(8,128)(2,1)} custom-call(bf16[48,128,128]{2,1,0:T(8,128)(2,1)} %inv.5, bf16[48,3,128,128]{3,2,1,0:T(8,128)(2,1)} %off.3), custom_call_target="tpu_custom_call" | custom-call | flops 603979776 | bytes 11000000 | tf_op jit(solution)/shard_map/fold/pallas_call | solution.py:103
  121.9 0.0 copy-done
  121.9 0.0 collective-permute-done.5.other
  121.9 0.0 copy-start.2
  121.9 1.3 copy-done.2
  123.2 16.9 %backward.1 = bf16[48,512,128]{2,1,0:T(8,128)(2,1)} custom-call(s32[144]{0:T(256)} %reshape.180.blocks, s32[1]{0:T(128)} %bitcast.core, bf16[48,512,128]{2,1,0:T(8,128)(2,1)} %get-tuple-element.55.y, bf16[48,128,128]{2,1,0:T(8,128)(2,1)} %inv.5, bf16[48,3,128,128]{3,2,1,0:T(8,128)(2,1)} %fold.1.folded, bf16[4,32,64,128]{3,2,1,0:T(8,128)(2,1)} %bitcast.22, ...), custom_call_target="tpu_custom_call" | custom-call | flops 3221225472 | bytes 23000000 | tf_op jit(solution)/shard_map/backward/pallas_call | solution.py:183
  (6 shorter events, 0.1 us)
Async XLA Ops:
  22.8 5.4 %collective-permute-start = (bf16[4,32,64,128]{3,2,1,0:T(8,128)(2,1)}, bf16[4,32,64,128]{3,2,1,0:T(8,128)(2,1)S(1)}, u32[]{:S(2)}, u32[]{:S(2)}) collective-permute-start(bf16[4,32,64,128]{3,2,1,0:T(8,128)(2,1)} %get-tuple-element.57), channel_id=1, source_target_pairs={{0,16},{16,0},{32,48},{48,32},{64,80},{80,64},{96,112},{112,96},{1... | collective-permute-start | bytes 6291464 | tf_op jit(solution)/shard_map/ppermute | solution.py:258
  32.5 11.4 %copy-start.3 = (bf16[2,16,128]{2,1,0:T(8,128)(2,1)S(1)}, bf16[2,16,128]{2,1,0:T(8,128)(2,1)}, u32[]{:S(2)}) copy-start(bf16[2,16,128]{2,1,0:T(8,128)(2,1)} %param.19) | copy-start | bytes 24580
  32.5 39.4 %all-to-all-start = ((bf16[64,2,64,128]{3,2,1,0:T(8,128)(2,1)}), bf16[64,2,64,128]{3,2,1,0:T(8,128)(2,1)S(1)}, u32[]{:S(2)}, u32[]{:S(2)}) async-start(bf16[64,2,64,128]{3,2,1,0:T(8,128)(2,1)} %bitcast.23), calls=%async_computation | async-start | bytes 4194304 | tf_op jit(solution)/shard_map/all_to_all | solution.py:259
  43.9 1.6 %collective-permute-start.1 = (bf16[2,16,128]{2,1,0:T(8,128)(2,1)S(1)}, bf16[2,16,128]{2,1,0:T(8,128)(2,1)S(1)}, u32[]{:S(2)}, u32[]{:S(2)}) collective-permute-start(bf16[2,16,128]{2,1,0:T(8,128)(2,1)S(1)} %copy-done.3), channel_id=1, source_target_pairs={{0,16},{16,0},{32,48},{48,32},{64,80},{80,64},{96,112},{112,96},{1... | collective-permute-start | bytes 24584 | tf_op jit(solution)/shard_map/ppermute | solution.py:216
  45.5 5.6 %collective-permute-start.3 = (bf16[2,2,16,128]{3,2,1,0:T(8,128)(2,1)S(1)}, bf16[2,2,16,128]{3,2,1,0:T(8,128)(2,1)S(1)}, u32[]{:S(2)}, u32[]{:S(2)}) collective-permute-start(bf16[2,2,16,128]{3,2,1,0:T(8,128)(2,1)S(1)} %maximum_select_fusion), channel_id=1, source_target_pairs={{0,64},{16,80},{32,96},{48,112},{64,0},{80,16},{96,32},{112,48},{1... | collective-permute-start | bytes 49160 | tf_op jit(solution)/shard_map/ppermute | solution.py:221
  48.3 5.7 %collective-permute-start.2 = (bf16[2,2,16,128]{3,2,1,0:T(8,128)(2,1)S(1)}, bf16[2,2,16,128]{3,2,1,0:T(8,128)(2,1)S(1)}, u32[]{:S(2)}, u32[]{:S(2)}) collective-permute-start(bf16[2,2,16,128]{3,2,1,0:T(8,128)(2,1)S(1)} %maximum_select_fusion), channel_id=1, source_target_pairs={{0,32},{16,48},{32,64},{48,80},{64,96},{80,112},{96,0},{112,16},{1... | collective-permute-start | bytes 49160 | tf_op jit(solution)/shard_map/ppermute | solution.py:221
  48.7 5.3 %collective-permute-start.4 = (bf16[2,2,16,128]{3,2,1,0:T(8,128)(2,1)S(1)}, bf16[2,2,16,128]{3,2,1,0:T(8,128)(2,1)S(1)}, u32[]{:S(2)}, u32[]{:S(2)}) collective-permute-start(bf16[2,2,16,128]{3,2,1,0:T(8,128)(2,1)S(1)} %maximum_select_fusion), channel_id=1, source_target_pairs={{0,96},{16,112},{32,0},{48,16},{64,32},{80,48},{96,64},{112,80},{1... | collective-permute-start | bytes 49160 | tf_op jit(solution)/shard_map/ppermute | solution.py:221
  71.9 1.3 copy-start.1
  111.1 10.7 %copy-start = (bf16[64,2,64,128]{3,2,1,0:T(8,128)(2,1)}, bf16[64,2,64,128]{3,2,1,0:T(8,128)(2,1)S(1)}, u32[]{:S(2)}) copy-start(bf16[64,2,64,128]{3,2,1,0:T(8,128)(2,1)S(1)} %all_to_all.10) | copy-start | bytes 6291460
  111.1 10.7 %collective-permute-start.5 = (bf16[4,32,64,128]{3,2,1,0:T(8,128)(2,1)S(1)}, bf16[4,32,64,128]{3,2,1,0:T(8,128)(2,1)S(1)}, u32[]{:S(2)}, u32[]{:S(2)}) collective-permute-start(bf16[4,32,64,128]{3,2,1,0:T(8,128)(2,1)S(1)} %bitcast.21), channel_id=1, source_target_pairs={{0,16},{16,0},{32,48},{48,32},{64,80},{80,64},{96,112},{112,96},{1... | collective-permute-start | bytes 6291464 | tf_op jit(solution)/shard_map/ppermute | solution.py:263
  121.9 1.3 copy-start.2

commit v2 on v1

v2 whole, which is shorter than its diff:
```python
import functools

import jax
import jax.numpy as jnp
from jax import lax
from jax.experimental import pallas as pl
from jax.experimental.pallas import tpu as pltpu
from jax.sharding import PartitionSpec as P

F32, BF16 = jnp.float32, jnp.bfloat16
F_G, F_S, B_G, B_S = 12, 2, 12, 2
CORES = 2


def params(mib):
    return pltpu.CompilerParams(vmem_limit_bytes=mib * 1024 * 1024)


def in_hbm(*arrays):
    return [pltpu.with_memory_space_constraint(a, pltpu.HBM) for a in arrays]


def cost(flops, moved):
    return pl.CostEstimate(flops=flops, bytes_accessed=moved, transcendentals=0)


def mm_t(a, b):
    return lax.dot_general(a, b, (((1,), (1,)), ((), ())), preferred_element_type=F32)


def mm(a, b):
    return jnp.dot(a, b, preferred_element_type=F32)


def diagonal(ref, slot, blocks):
    row = col = 0
    for b in blocks:
        ref[slot, row : row + b.shape[0], col : col + b.shape[1]] = b
        row, col = row + b.shape[0], col + b.shape[1]


def forward_kernel(
    g, fanout, blocks, core, rhs_hbm, inv_hbm, off_hbm, keep_hbm, send_hbm,
    rhs, inv, off, acc, staged, w_inv, w_off, in_sems, out_sems,
):
    leaves = rhs.shape[0]
    _, heights, parents, block_rows, width = acc.shape
    half = heights * block_rows
    me = core[0]

    def fetches(i):
        some = pl.ds(g * i, g)
        return [
            pltpu.make_async_copy(hbm.at[some], vmem.at[some], in_sems.at[n, i])
            for n, (hbm, vmem) in enumerate(((inv_hbm, inv), (rhs_hbm, rhs), (off_hbm, off)))
        ]

    for i in range(leaves // g):
        for copy in fetches(i):
            copy.start()

    w_inv[...] = jnp.zeros_like(w_inv)
    w_off[...] = jnp.zeros_like(w_off)
    acc[...] = jnp.zeros_like(acc)

    def pair(j, slot):
        diagonal(w_inv, slot, [inv[j], inv[j + 1]])
        diagonal(w_off, slot, [off[j + h].reshape(fanout * width, width) for h in range(2)])
        x = jnp.concatenate(
            [
                jnp.concatenate(
                    [rhs[j + h, z, c] for c in (me, 1 - me) for z in range(heights)], axis=0
                )
                for h in range(2)
            ],
            axis=1,
        )
        y = mm_t(x, w_inv[slot]).astype(BF16)
        part = mm_t(y, w_off[slot])
        for h in range(2):
            for k in range(fanout):
                p = blocks[(j + h) * fanout + k]
                at = (h * fanout + k) * width
                for c in range(CORES):
                    for z in range(heights):
                        row = c * half + z * block_rows
                        acc[c, z, p] += part[row : row + block_rows, at : at + width]

    @pl.loop(0, leaves // g)
    def _(i):
        for copy in fetches(i):
            copy.wait()
        for u in range(0, g, 2):
            pair(i * g + u, (u // 2) % w_inv.shape[0])

    copies = []
    for z in range(heights):
        for c, out in ((1, send_hbm), (0, keep_hbm)):
            staged[c, z] = acc[c, z].astype(BF16)
            copies.append(pltpu.make_async_copy(staged.at[c, z], out.at[z], out_sems.at[c, z]))
            copies[-1].start()
    for copy in copies:
        copy.wait()


def forward(blocks, core, rhs, inv, off, parents):
    leaves, heights, _, block_rows, width = rhs.shape
    fanout = off.shape[1]
    half = (heights, parents, block_rows, width)
    g, slots = F_G, F_S
    smem, hbm = pl.BlockSpec(memory_space=pltpu.SMEM), pl.BlockSpec(memory_space=pltpu.HBM)
    return pl.pallas_call(
        functools.partial(forward_kernel, g, fanout),
        in_specs=[smem, smem, hbm, hbm, hbm],
        out_specs=[hbm, hbm],
        scratch_shapes=[
            pltpu.VMEM(rhs.shape, BF16),
            pltpu.VMEM(inv.shape, BF16),
            pltpu.VMEM(off.shape, BF16),
            pltpu.VMEM((CORES,) + half, F32),
            pltpu.VMEM((CORES,) + half, BF16),
            pltpu.VMEM((slots, 2 * width, 2 * width), BF16),
            pltpu.VMEM((slots, 2 * fanout * width, 2 * width), BF16),
            pltpu.SemaphoreType.DMA((3, leaves // g)),
            pltpu.SemaphoreType.DMA((CORES, heights)),
        ],
        out_shape=[jax.ShapeDtypeStruct(half, BF16)] * 2,
        compiler_params=params(48),
        name="forward",
        cost_estimate=cost(7_000_000_000, 19_000_000),
    )(blocks, core, *in_hbm(rhs, inv, off))


def fold_kernel(g, fanout, inv, off, out, w_inv):
    width = inv.shape[-1]

    @pl.when(pl.program_id(0) == 0)
    def _():
        w_inv[...] = jnp.zeros_like(w_inv)

    for i in range(0, g, 2):
        slot = (i // 2) % 2
        diagonal(w_inv, slot, [inv[i], inv[i + 1]])
        x = jnp.concatenate([off[i + h].reshape(fanout * width, width) for h in range(2)], axis=1)
        m = mm(x, w_inv[slot]).astype(BF16)
        for h in range(2):
            out[i + h] = m[:, h * width : (h + 1) * width]


def fold(inv, off):
    leaves, fanout, width, _ = off.shape
    g = 8
    return pl.pallas_call(
        functools.partial(fold_kernel, g, fanout),
        grid=(leaves // g,),
        in_specs=[
            pl.BlockSpec((g, width, width), lambda s: (s, 0, 0)),
            pl.BlockSpec((g, fanout, width, width), lambda s: (s, 0, 0, 0)),
        ],
        out_specs=pl.BlockSpec((g, fanout * width, width), lambda s: (s, 0, 0)),
        out_shape=jax.ShapeDtypeStruct((leaves, fanout * width, width), BF16),
        scratch_shapes=[pltpu.VMEM((2, 2 * width, 2 * width), BF16)],
        compiler_params=params(10),
        name="fold",
        cost_estimate=cost(4_000_000_000, 15_000_000),
    )(inv, off)


def leaf_kernel(g, rhs, inv, after, out, w_inv):
    width = inv.shape[-1]

    @pl.when(pl.program_id(0) == 0)
    def _():
        w_inv[...] = jnp.zeros_like(w_inv)

    for i in range(0, g, 2):
        slot = (i // 2) % 2
        diagonal(w_inv, slot, [inv[i], inv[i + 1]])
        x = jnp.concatenate([rhs[i], rhs[i + 1]], axis=1)
        y = mm_t(x, w_inv[slot]).astype(BF16)
        z = mm(y, w_inv[slot]).astype(BF16)
        for h in range(2):
            out[i + h] = z[:, h * width : (h + 1) * width]


def leaf(rhs, inv, after):
    leaves, nrhs, width = rhs.shape
    g = 8
    return pl.pallas_call(
        functools.partial(leaf_kernel, g),
        grid=(leaves // g,),
        in_specs=[
            pl.BlockSpec((g, nrhs, width), lambda s: (s, 0, 0)),
            pl.BlockSpec((g, width, width), lambda s: (s, 0, 0)),
            pl.BlockSpec(memory_space=pl.ANY),
        ],
        out_specs=pl.BlockSpec((g, nrhs, width), lambda s: (s, 0, 0)),
        out_shape=jax.ShapeDtypeStruct(rhs.shape, BF16),
        scratch_shapes=[pltpu.VMEM((2, 2 * width, 2 * width), BF16)],
        compiler_params=params(10),
        name="leaf",
        cost_estimate=cost(6_000_000_000, 20_000_000),
    )(rhs, inv, after)


def parent_kernel(sources, got, rhs, inv, after, x_out, x_every):
    own, block_rows, width = rhs.shape
    total = got[0].astype(F32)
    for s in range(1, sources):
        total += got[s].astype(F32)
    for p in range(own):
        rest = rhs[p].astype(F32) - total[p]
        high = rest.astype(BF16)
        left = rest - high.astype(F32)
        mid = left.astype(BF16)
        low = (left - mid.astype(F32)).astype(BF16)
        w = inv[p]
        y = (mm_t(low, w) + mm_t(mid, w)) + mm_t(high, w)
        x = mm(y.astype(BF16), w).astype(BF16)
        x_out[p] = x
        for s in range(sources):
            x_every[s, p] = x


def parent(got, rhs, inv, after):
    sources = got.shape[0]
    return pl.pallas_call(
        functools.partial(parent_kernel, sources),
        in_specs=[pl.BlockSpec(memory_space=pltpu.VMEM)] * 3 + [pl.BlockSpec(memory_space=pl.ANY)],
        out_shape=[
            jax.ShapeDtypeStruct(rhs.shape, BF16),
            jax.ShapeDtypeStruct(got.shape, BF16),
        ],
        compiler_params=params(16),
        name="parent",
        cost_estimate=cost(30_000_000, 4_500_000),
    )(got, rhs, inv, after)


def backward_kernel(g, fanout, blocks, which, base_hbm, folded_hbm, xs, *rest):
    out_hbm, base, folded, out, w, in_sems, out_sems = rest[-7:]
    leaves, heights, block_rows, width = base.shape
    c = which[0]

    def fetches(i):
        some = pl.ds(g * i, g)
        return [
            pltpu.make_async_copy(folded_hbm.at[some], folded.at[some], in_sems.at[0, i]),
            pltpu.make_async_copy(base_hbm.at[some, :, c], base.at[some], in_sems.at[1, i]),
        ]

    def store(i):
        some = pl.ds(g * i, g)
        return pltpu.make_async_copy(out.at[some], out_hbm.at[some, :, c], out_sems.at[i])

    for i in range(leaves // g):
        for copy in fetches(i):
            copy.start()

    w[...] = jnp.zeros_like(w)

    def pair(j, slot):
        diagonal(w, slot, [folded[j], folded[j + 1]])
        x = jnp.concatenate(
            [
                jnp.concatenate(
                    [xs[z, blocks[(j + h) * fanout + k]] for z in range(heights)], axis=0
                )
                for h in range(2)
                for k in range(fanout)
            ],
            axis=1,
        )
        back = mm(x, w[slot])
        for h in range(2):
            for z in range(heights):
                row = z * block_rows
                part = back[row : row + block_rows, h * width : (h + 1) * width]
                out[j + h, z] = (base[j + h, z].astype(F32) - part).astype(BF16)

    @pl.loop(0, leaves // g)
    def _(i):
        for copy in fetches(i):
            copy.wait()
        for u in range(0, g, 2):
            pair(i * g + u, (u // 2) % w.shape[0])
        store(i).start()

    for i in range(leaves // g):
        store(i).wait()


def backward(blocks, which, base, folded, xs, so_far=None):
    leaves, heights, _, block_rows, width = base.shape
    fanout = folded.shape[1] // width
    half = (leaves, heights, block_rows, width)
    g, slots = B_G, B_S
    more = [] if so_far is None else [so_far]
    smem, hbm = pl.BlockSpec(memory_space=pltpu.SMEM), pl.BlockSpec(memory_space=pltpu.HBM)
    return pl.pallas_call(
        functools.partial(backward_kernel, g, fanout),
        in_specs=[smem, smem, hbm, hbm, pl.BlockSpec(memory_space=pltpu.VMEM)] + [hbm] * len(more),
        out_specs=hbm,
        scratch_shapes=[
            pltpu.VMEM(half, BF16),
            pltpu.VMEM(folded.shape, BF16),
            pltpu.VMEM(half, BF16),
            pltpu.VMEM((slots, 2 * fanout * width, 2 * width), BF16),
            pltpu.SemaphoreType.DMA((2, leaves // g)),
            pltpu.SemaphoreType.DMA((leaves // g,)),
        ],
        out_shape=jax.ShapeDtypeStruct(base.shape, BF16),
        input_output_aliases={5: 0} if more else {},
        compiler_params=params(24),
        name="backward",
        cost_estimate=cost(5_000_000_000, 13_000_000),
    )(blocks, which, *in_hbm(base, folded), xs, *more)


def gather_inverse(par_inv, rows):
    own, part, width = par_inv.shape
    heights = rows // CORES
    place = lax.axis_index("row")
    across = lax.ppermute(par_inv, "row", [(r, r ^ 1) for r in range(rows)])
    pair = jnp.where(
        place % CORES == 0, jnp.stack([par_inv, across]), jnp.stack([across, par_inv])
    )
    parts = [pair] + [
        lax.ppermute(pair, "row", [(r, (r + CORES * s) % rows) for r in range(rows)])
        for s in range(1, heights)
    ]
    z = place // CORES
    stacked = jnp.stack(parts)
    whole = jnp.zeros_like(stacked)
    for h in range(heights):
        pick = sum(
            jnp.where((z - h) % heights == s, parts[s].astype(F32), 0.0) for s in range(heights)
        )
        whole = whole.at[h].set(pick.astype(BF16))
    return whole.transpose(2, 0, 1, 3, 4).reshape(own, rows * part, width)


def on_device(rows, cols, leaf_rhs, leaf_inv, leaf_off, blocks, par_rhs, par_inv):
    own, block_rows, width = par_rhs.shape
    parents = own * cols
    heights = rows // CORES
    chips = heights * cols
    core = (lax.axis_index("row") % CORES).astype(jnp.int32).reshape(1)
    flat = blocks.reshape(-1)
    swap = [(r, r ^ 1) for r in range(rows)]
    groups = [
        [(z * CORES + c) * cols + k for z in range(heights) for k in range(cols)]
        for c in range(CORES)
    ]
    spread = functools.partial(
        lax.all_to_all,
        axis_name=("row", "col"),
        split_axis=0,
        concat_axis=0,
        axis_index_groups=groups,
        tiled=True,
    )

    inverse = gather_inverse(par_inv, rows)
    by_core = (leaf_rhs.shape[0], heights, CORES, block_rows, width)
    keep, send = forward(flat, core, leaf_rhs.reshape(by_core), leaf_inv, leaf_off, parents)
    chip = (keep.astype(F32) + lax.ppermute(send, "row", swap).astype(F32)).astype(BF16)
    got = spread(chip.reshape(chips, own, block_rows, width))
    folded = fold(leaf_inv, leaf_off)
    par_x, every = parent(got, par_rhs, inverse, folded[0, :16])
    mine = spread(every).reshape(heights, parents, block_rows, width)
    base = leaf(leaf_rhs, leaf_inv, par_x).reshape(by_core)
    mine, base = lax.optimization_barrier((mine, base))
    other = lax.ppermute(mine, "row", swap)
    half = backward(flat, core, base, folded, mine)
    leaf_x = backward(flat, 1 - core, base, folded, other, half)
    return (leaf_x.reshape(leaf_rhs.shape), par_x)


def solution(mesh):
    rows, cols = mesh.shape["row"], mesh.shape["col"]
    return jax.shard_map(
        functools.partial(on_device, rows, cols),
        mesh=mesh,
        in_specs=(
            P(("row", "col"), None, None),
            P(("row", "col"), None, None),
            P(("row", "col"), None, None, None),
            P(("row", "col"), None),
            P("col", "row", None),
            P("col", "row", None),
        ),
        out_specs=(P(("row", "col"), None, None), P("col", "row", None)),
        check_vma=False,
    )
```

time: 141 us -> 119 us (0.84)
  blocking collectives: 34.1 us -> 0 us
  Pallas kernels: 48.8 us -> 37.5 us
  local copies, waits for them, and re-layouts: 4.66 us -> 15.7 us
  starting transfers between devices: 22.5 us -> 30.7 us
  waiting for transfers between devices: 24.9 us -> 31 us
  other arithmetic: 4.37 us -> 2.37 us
    all_to_all x1 -> x0, blocking collectives: 34.1 us -> none  [on_device(): mine = spread(every).reshape(heights, parents, block_rows, width)]
    all_to_all x0 -> x1, waiting for transfers between devices: none -> 15.1 us  [on_device(): mine = spread(every).reshape(heights, parents, block_rows, width)]
    all_to_all x1, waiting for transfers between devices: 17.1 us -> 2.07 us  [on_device(): got = spread(chip.reshape(chips, own, block_rows, width))]
    unnamed x9 -> x21, local copies, waits for them, and re-layouts: 3.38 us -> 14.9 us
    all_to_all x0 -> x1, starting transfers between devices: none -> 8.87 us  [on_device(): mine = spread(every).reshape(heights, parents, block_rows, width)]
    ppermute x3, waiting for transfers between devices: 3.01 us -> 10.1 us  [gather_inverse(): lax.ppermute(pair, 'row', [(r, (r + CORES * s) % rows) for r in range(row...]
    pallas_call x3 -> x5, Pallas kernels: 41.5 us -> 34.8 us  [the longest x1 13.7 us: forward(): pl.pallas_call(functools.partial(forward_kernel, g, fanout), in_specs=[sm...]
    pallas_call x1, Pallas kernels: 7.26 us -> 2.62 us  [fold(): pl.pallas_call(functools.partial(fold_kernel, g, fanout), grid=(leaves //...]
  transfers between devices with their start and end apart: 7 -> 8, of which waited for: 4 -> 5; matrix products, arithmetic and copies ran while one was open for 1% -> 1% of each run, Pallas kernels for 5% -> 13%
where the time goes in v2:
time: 119 us; the launch traced here: 118 us
  Pallas kernels  37.5 us (32%)
  waiting for transfers between devices  31 us (26%)
  starting transfers between devices  30.7 us (26%)
  local copies, waits for them, and re-layouts  15.7 us (13%)
  other arithmetic  2.37 us (2%)
    all_to_all x1, waiting for transfers between devices, on_device(): mine = spread(every).reshape(heights, parents, block_rows, width)  15.1 us
    unnamed x21, local copies, waits for them, and re-layouts  14.9 us
    pallas_call x1, Pallas kernels, forward(): pl.pallas_call(functools.partial(forward_kernel, g, fanout), in_specs=[sm...  13.7 us
    pallas_call x2, Pallas kernels, backward(): pl.pallas_call(functools.partial(backward_kernel, g, fanout), in_specs=[s...  13.6 us
    all_to_all x1, starting transfers between devices, on_device(): got = spread(chip.reshape(chips, own, block_rows, width))  11.4 us
    ppermute x3, waiting for transfers between devices, gather_inverse(): lax.ppermute(pair, 'row', [(r, (r + CORES * s) % rows) for r in range(row...  10.1 us
    all_to_all x1, starting transfers between devices, on_device(): mine = spread(every).reshape(heights, parents, block_rows, width)  8.87 us
    pallas_call x1, Pallas kernels, leaf(): pl.pallas_call(functools.partial(leaf_kernel, g), grid=(leaves // g,), in...  6.03 us
  transfers between devices with their start and end apart: 8, of which 5 were waited for; matrix products, arithmetic and copies ran while one was open for 1% of the time, Pallas kernels for 13%

profile of v2, /device:TPU:1, one launch (start us, length us, event | category | flops | bytes accessed | tf_op | source)
XLA Modules:
  0.0 118.1 jit_solution(10145767903829880674)
XLA Ops:
  0.6 0.8 copy.10
  1.4 0.1 reshape.189.blocks
  1.5 13.7 %forward.1 = (bf16[4,32,64,128]{3,2,1,0:T(8,128)(2,1)S(1)}, bf16[4,32,64,128]{3,2,1,0:T(8,128)(2,1)S(1)}) custom-call(s32[144]{0:T(256)S(1)} %reshape.189.blocks, s32[1]{0:T(128)} %bitcast.core.which, bf16[48,4,2,64,128]{4,3,2,1,0:T(8,128)(2,1)} %bitcast.31, bf16[48,128,128]{2,1,0:T(8,128)(2,1)} %inv.3, bf16[48,3,128,128]{3,2,1,0:T(8,128)(2,1)} %off.1), custom_call_target="tpu_custom_call" | custom-call | flops 7000000000 | bytes 19000000 | tf_op jit(solution)/shard_map/forward/pallas_call | solution.py:112
  15.3 1.5 %collective-permute-start = (bf16[4,32,64,128]{3,2,1,0:T(8,128)(2,1)S(1)}, bf16[4,32,64,128]{3,2,1,0:T(8,128)(2,1)S(1)}, u32[]{:S(2)}, u32[]{:S(2)}) collective-permute-start(bf16[4,32,64,128]{3,2,1,0:T(8,128)(2,1)S(1)} %get-tuple-element.57), channel_id=1, source_target_pairs={{0,16},{16,0},{32,48},{48,32},{64,80},{80,64},{96,112},{112,96},{1... | collective-permute-start | bytes 6291464 | tf_op jit(solution)/shard_map/ppermute | solution.py:367
  16.8 3.8 %collective-permute-done = bf16[4,32,64,128]{3,2,1,0:T(8,128)(2,1)S(1)} collective-permute-done((bf16[4,32,64,128]{3,2,1,0:T(8,128)(2,1)S(1)}, bf16[4,32,64,128]{3,2,1,0:T(8,128)(2,1)S(1)}, u32[]{:S(2)}, u32[]{:S(2)}) %collective-permute-start) | collective-permute-done | bytes 2097184 | tf_op jit(solution)/shard_map/ppermute | solution.py:367
  20.6 2.3 %add_convert_fusion = bf16[4,32,64,128]{3,2,1,0:T(8,128)(2,1)} fusion(bf16[4,32,64,128]{3,2,1,0:T(8,128)(2,1)S(1)} %collective-permute-done, bf16[4,32,64,128]{3,2,1,0:T(8,128)(2,1)S(1)} %get-tuple-element.56), kind=kLoop, calls=%fused_computation | loop fusion | flops 4194304 | bytes 6291456 | tf_op jit(solution)/shard_map/convert_element_type | solution.py:367
  22.8 0.0 copy-start.9
  22.8 11.4 %all-to-all-start = ((bf16[64,2,64,128]{3,2,1,0:T(8,128)(2,1)}), bf16[64,2,64,128]{3,2,1,0:T(8,128)(2,1)S(1)}, u32[]{:S(2)}, u32[]{:S(2)}) async-start(bf16[64,2,64,128]{3,2,1,0:T(8,128)(2,1)} %bitcast.33), calls=%async_computation | async-start | bytes 4194304 | tf_op jit(solution)/shard_map/all_to_all | solution.py:368
  34.2 0.0 copy-done.9
  34.2 0.0 copy-start.3
  34.2 0.7 collective-permute-start.1
  34.9 0.0 copy-start.5
  34.9 2.3 %copy-done.5 = bf16[48,3,128,128]{3,2,1,0:T(8,128)(2,1)S(1)} copy-done((bf16[48,3,128,128]{3,2,1,0:T(8,128)(2,1)S(1)}, bf16[48,3,128,128]{3,2,1,0:T(8,128)(2,1)}, u32[]{:S(2)}) %copy-start.5) | copy-done | bytes 4718616
  37.3 0.0 copy-start.6
  37.3 1.4 %copy-done.6 = bf16[48,128,128]{2,1,0:T(8,128)(2,1)S(1)} copy-done((bf16[48,128,128]{2,1,0:T(8,128)(2,1)S(1)}, bf16[48,128,128]{2,1,0:T(8,128)(2,1)}, u32[]{:S(2)}) %copy-start.6) | copy-done | bytes 1572888
  38.7 2.6 %fold.1.folded_hbm = bf16[48,384,128]{2,1,0:T(8,128)(2,1)S(1)} custom-call(bf16[48,128,128]{2,1,0:T(8,128)(2,1)S(1)} %copy-done.6, bf16[48,3,128,128]{3,2,1,0:T(8,128)(2,1)S(1)} %copy-done.5), custom_call_target="tpu_custom_call" | custom-call | flops 4000000000 | bytes 15000000 | tf_op jit(solution)/shard_map/fold/pallas_call | solution.py:153
  41.3 0.0 copy-start.1
  41.3 2.2 %copy-done.1 = bf16[48,384,128]{2,1,0:T(8,128)(2,1)} copy-done((bf16[48,384,128]{2,1,0:T(8,128)(2,1)}, bf16[48,384,128]{2,1,0:T(8,128)(2,1)S(1)}, u32[]{:S(2)}) %copy-start.1) | copy-done | bytes 4718616
  43.5 0.0 collective-permute-done.1
  43.5 3.0 %collective-permute-start.3 = (bf16[2,2,16,128]{3,2,1,0:T(8,128)(2,1)S(1)}, bf16[2,2,16,128]{3,2,1,0:T(8,128)(2,1)S(1)}, u32[]{:S(2)}, u32[]{:S(2)}) collective-permute-start(bf16[2,2,16,128]{3,2,1,0:T(8,128)(2,1)S(1)} %maximum_select_fusion), channel_id=1, source_target_pairs={{0,64},{16,80},{32,96},{48,112},{64,0},{80,16},{96,32},{112,48},{1... | collective-permute-start | bytes 49160 | tf_op jit(solution)/shard_map/ppermute | solution.py:329
  46.5 0.4 collective-permute-start.2
  46.9 2.3 %collective-permute-start.4 = (bf16[2,2,16,128]{3,2,1,0:T(8,128)(2,1)S(1)}, bf16[2,2,16,128]{3,2,1,0:T(8,128)(2,1)S(1)}, u32[]{:S(2)}, u32[]{:S(2)}) collective-permute-start(bf16[2,2,16,128]{3,2,1,0:T(8,128)(2,1)S(1)} %maximum_select_fusion), channel_id=1, source_target_pairs={{0,96},{16,112},{32,0},{48,16},{64,32},{80,48},{96,64},{112,80},{1... | collective-permute-start | bytes 49160 | tf_op jit(solution)/shard_map/ppermute | solution.py:329
  49.2 0.7 slice_bitcast_fusion.after
  49.9 9.9 %collective-permute-done.3 = bf16[2,2,16,128]{3,2,1,0:T(8,128)(2,1)S(1)} collective-permute-done((bf16[2,2,16,128]{3,2,1,0:T(8,128)(2,1)S(1)}, bf16[2,2,16,128]{3,2,1,0:T(8,128)(2,1)S(1)}, u32[]{:S(2)}, u32[]{:S(2)}) %collective-permute-start.3) | collective-permute-done | bytes 16416 | tf_op jit(solution)/shard_map/ppermute | solution.py:329
  59.8 0.2 collective-permute-done.2
  60.0 0.0 collective-permute-done.4
  60.1 2.1 %all-to-all-done.got = bf16[64,2,64,128]{3,2,1,0:T(8,128)(2,1)S(1)} async-done(((bf16[64,2,64,128]{3,2,1,0:T(8,128)(2,1)}), bf16[64,2,64,128]{3,2,1,0:T(8,128)(2,1)S(1)}, u32[]{:S(2)}, u32[]{:S(2)}) %all-to-all-start) | async-done | bytes 2097184 | tf_op jit(solution)/shard_map/all_to_all | solution.py:368
  62.2 0.0 copy-done.3
  62.2 1.4 %parent.1 = (bf16[2,64,128]{2,1,0:T(8,128)(2,1)}, bf16[64,2,64,128]{3,2,1,0:T(8,128)(2,1)S(1)}) custom-call(bf16[64,2,64,128]{3,2,1,0:T(8,128)(2,1)S(1)} %all-to-all-done.got, bf16[2,64,128]{2,1,0:T(8,128)(2,1)S(1)} %copy-done.3, bf16[2,128,128]{2,1,0:T(8,128)(2,1)S(1)} %bitcast.30, bf16[16,128]{1,0:T(8,128)(2,1)S(1)} %slice_bitcast_fusion.after), custom_call_target="tpu_custom_call" | custom-call | flops 30000000 | bytes 4500000 | tf_op jit(solution)/shard_map/parent/pallas_call | solution.py:227
  63.7 0.0 copy-start.2
  63.7 1.3 %copy-done.2 = bf16[64,2,64,128]{3,2,1,0:T(8,128)(2,1)} copy-done((bf16[64,2,64,128]{3,2,1,0:T(8,128)(2,1)}, bf16[64,2,64,128]{3,2,1,0:T(8,128)(2,1)S(1)}, u32[]{:S(2)}) %copy-start.2) | copy-done | bytes 2097176
  65.0 0.0 copy-start.8
  65.0 8.9 %all-to-all-start.1 = ((bf16[64,2,64,128]{3,2,1,0:T(8,128)(2,1)}), bf16[64,2,64,128]{3,2,1,0:T(8,128)(2,1)S(1)}, u32[]{:S(2)}, u32[]{:S(2)}) async-start(bf16[64,2,64,128]{3,2,1,0:T(8,128)(2,1)} %copy-done.2), calls=%async_computation.1 | async-start | bytes 4194304 | tf_op jit(solution)/shard_map/all_to_all | solution.py:371
  73.9 0.0 copy-done.8
  73.9 0.0 copy-start.4
  73.9 2.8 %copy-done.4 = bf16[48,512,128]{2,1,0:T(8,128)(2,1)S(1)} copy-done((bf16[48,512,128]{2,1,0:T(8,128)(2,1)S(1)}, bf16[48,512,128]{2,1,0:T(8,128)(2,1)}, u32[]{:S(2)}) %copy-start.4) | copy-done | bytes 6291480
  76.6 0.0 copy-start.7
  76.7 1.4 %copy-done.7 = bf16[48,128,128]{2,1,0:T(8,128)(2,1)S(1)} copy-done((bf16[48,128,128]{2,1,0:T(8,128)(2,1)S(1)}, bf16[48,128,128]{2,1,0:T(8,128)(2,1)}, u32[]{:S(2)}) %copy-start.7) | copy-done | bytes 1572888
  78.1 6.0 %leaf.1 = bf16[48,512,128]{2,1,0:T(8,128)(2,1)S(1)} custom-call(bf16[48,512,128]{2,1,0:T(8,128)(2,1)S(1)} %copy-done.4, bf16[48,128,128]{2,1,0:T(8,128)(2,1)S(1)} %copy-done.7, bf16[2,64,128]{2,1,0:T(8,128)(2,1)S(1)} %copy-done.8), custom_call_target="tpu_custom_call" | custom-call | flops 6000000000 | bytes 20000000 | tf_op jit(solution)/shard_map/leaf/pallas_call | solution.py:189
  84.1 0.0 copy-start
  84.1 2.7 %copy-done = bf16[48,512,128]{2,1,0:T(8,128)(2,1)} copy-done((bf16[48,512,128]{2,1,0:T(8,128)(2,1)}, bf16[48,512,128]{2,1,0:T(8,128)(2,1)S(1)}, u32[]{:S(2)}) %copy-start) | copy-done | bytes 6291480
  86.8 15.1 %all-to-all-done.1 = bf16[64,2,64,128]{3,2,1,0:T(8,128)(2,1)S(1)} async-done(((bf16[64,2,64,128]{3,2,1,0:T(8,128)(2,1)}), bf16[64,2,64,128]{3,2,1,0:T(8,128)(2,1)S(1)}, u32[]{:S(2)}, u32[]{:S(2)}) %all-to-all-start.1) | async-done | bytes 2097184 | tf_op jit(solution)/shard_map/all_to_all | solution.py:371
  101.8 2.6 %collective-permute-start.5 = (bf16[4,32,64,128]{3,2,1,0:T(8,128)(2,1)S(1)}, bf16[4,32,64,128]{3,2,1,0:T(8,128)(2,1)S(1)}, u32[]{:S(2)}, u32[]{:S(2)}) collective-permute-start(bf16[4,32,64,128]{3,2,1,0:T(8,128)(2,1)S(1)} %bitcast.28), channel_id=1, source_target_pairs={{0,16},{16,0},{32,48},{48,32},{64,80},{80,64},{96,112},{112,96},{1... | collective-permute-start | bytes 6291464 | tf_op jit(solution)/shard_map/ppermute | solution.py:374
  104.4 6.8 %backward.2.rest_0_ = bf16[48,4,2,64,128]{4,3,2,1,0:T(8,128)(2,1)} custom-call(s32[144]{0:T(256)S(1)} %reshape.189.blocks, s32[1]{0:T(128)} %bitcast.core.which, bf16[48,4,2,64,128]{4,3,2,1,0:T(8,128)(2,1)} %bitcast.26, bf16[48,384,128]{2,1,0:T(8,128)(2,1)} %copy-done.1, bf16[4,32,64,128]{3,2,1,0:T(8,128)(2,1)S(1)} %bitcast.29), custom_call_target="tpu_custom_call" | custom-call | flops 5000000000 | bytes 13000000 | tf_op jit(solution)/shard_map/backward/pallas_call | solution.py:300
  111.2 0.0 collective-permute-done.5.xs
  111.3 6.8 %backward.3 = bf16[48,4,2,64,128]{4,3,2,1,0:T(8,128)(2,1)} custom-call(s32[144]{0:T(256)S(1)} %reshape.189.blocks, s32[1]{0:T(128)S(6)} %sub.12.which, bf16[48,4,2,64,128]{4,3,2,1,0:T(8,128)(2,1)} %bitcast.27, bf16[48,384,128]{2,1,0:T(8,128)(2,1)} %copy-done.1, ...), custom_call_target="tpu_custom_call", output_to_operand_aliasing={{}: (5, {})} | custom-call | flops 5000000000 | bytes 13000000 | tf_op jit(solution)/shard_map/backward/pallas_call | solution.py:300
  (7 shorter events, 0.1 us)
Async XLA Ops:
  15.3 5.3 %collective-permute-start = (bf16[4,32,64,128]{3,2,1,0:T(8,128)(2,1)S(1)}, bf16[4,32,64,128]{3,2,1,0:T(8,128)(2,1)S(1)}, u32[]{:S(2)}, u32[]{:S(2)}) collective-permute-start(bf16[4,32,64,128]{3,2,1,0:T(8,128)(2,1)S(1)} %get-tuple-element.57), channel_id=1, source_target_pairs={{0,16},{16,0},{32,48},{48,32},{64,80},{80,64},{96,112},{112,96},{1... | collective-permute-start | bytes 6291464 | tf_op jit(solution)/shard_map/ppermute | solution.py:367
  22.8 11.4 %copy-start.9 = (bf16[2,16,128]{2,1,0:T(8,128)(2,1)S(1)}, bf16[2,16,128]{2,1,0:T(8,128)(2,1)}, u32[]{:S(2)}) copy-start(bf16[2,16,128]{2,1,0:T(8,128)(2,1)} %param.19) | copy-start | bytes 24580
  22.8 39.4 %all-to-all-start = ((bf16[64,2,64,128]{3,2,1,0:T(8,128)(2,1)}), bf16[64,2,64,128]{3,2,1,0:T(8,128)(2,1)S(1)}, u32[]{:S(2)}, u32[]{:S(2)}) async-start(bf16[64,2,64,128]{3,2,1,0:T(8,128)(2,1)} %bitcast.33), calls=%async_computation | async-start | bytes 4194304 | tf_op jit(solution)/shard_map/all_to_all | solution.py:368
  34.2 28.0 %copy-start.3 = (bf16[2,64,128]{2,1,0:T(8,128)(2,1)S(1)}, bf16[2,64,128]{2,1,0:T(8,128)(2,1)}, u32[]{:S(2)}) copy-start(bf16[2,64,128]{2,1,0:T(8,128)(2,1)} %rhs.6) | copy-start | bytes 98308
  34.2 9.3 %collective-permute-start.1 = (bf16[2,16,128]{2,1,0:T(8,128)(2,1)S(1)}, bf16[2,16,128]{2,1,0:T(8,128)(2,1)S(1)}, u32[]{:S(2)}, u32[]{:S(2)}) collective-permute-start(bf16[2,16,128]{2,1,0:T(8,128)(2,1)S(1)} %copy-done.9), channel_id=1, source_target_pairs={{0,16},{16,0},{32,48},{48,32},{64,80},{80,64},{96,112},{112,96},{1... | collective-permute-start | bytes 24584 | tf_op jit(solution)/shard_map/ppermute | solution.py:324
  34.9 2.3 %copy-start.5 = (bf16[48,3,128,128]{3,2,1,0:T(8,128)(2,1)S(1)}, bf16[48,3,128,128]{3,2,1,0:T(8,128)(2,1)}, u32[]{:S(2)}) copy-start(bf16[48,3,128,128]{3,2,1,0:T(8,128)(2,1)} %off.1) | copy-start | bytes 14155780
  37.3 1.4 %copy-start.6 = (bf16[48,128,128]{2,1,0:T(8,128)(2,1)S(1)}, bf16[48,128,128]{2,1,0:T(8,128)(2,1)}, u32[]{:S(2)}) copy-start(bf16[48,128,128]{2,1,0:T(8,128)(2,1)} %inv.3) | copy-start | bytes 4718596
  41.3 2.2 %copy-start.1 = (bf16[48,384,128]{2,1,0:T(8,128)(2,1)}, bf16[48,384,128]{2,1,0:T(8,128)(2,1)S(1)}, u32[]{:S(2)}) copy-start(bf16[48,384,128]{2,1,0:T(8,128)(2,1)S(1)} %fold.1.folded_hbm) | copy-start | bytes 14155780
  43.5 16.2 %collective-permute-start.3 = (bf16[2,2,16,128]{3,2,1,0:T(8,128)(2,1)S(1)}, bf16[2,2,16,128]{3,2,1,0:T(8,128)(2,1)S(1)}, u32[]{:S(2)}, u32[]{:S(2)}) collective-permute-start(bf16[2,2,16,128]{3,2,1,0:T(8,128)(2,1)S(1)} %maximum_select_fusion), channel_id=1, source_target_pairs={{0,64},{16,80},{32,96},{48,112},{64,0},{80,16},{96,32},{112,48},{1... | collective-permute-start | bytes 49160 | tf_op jit(solution)/shard_map/ppermute | solution.py:329
  46.5 13.5 %collective-permute-start.2 = (bf16[2,2,16,128]{3,2,1,0:T(8,128)(2,1)S(1)}, bf16[2,2,16,128]{3,2,1,0:T(8,128)(2,1)S(1)}, u32[]{:S(2)}, u32[]{:S(2)}) collective-permute-start(bf16[2,2,16,128]{3,2,1,0:T(8,128)(2,1)S(1)} %maximum_select_fusion), channel_id=1, source_target_pairs={{0,32},{16,48},{32,64},{48,80},{64,96},{80,112},{96,0},{112,16},{1... | collective-permute-start | bytes 49160 | tf_op jit(solution)/shard_map/ppermute | solution.py:329
  46.9 13.0 %collective-permute-start.4 = (bf16[2,2,16,128]{3,2,1,0:T(8,128)(2,1)S(1)}, bf16[2,2,16,128]{3,2,1,0:T(8,128)(2,1)S(1)}, u32[]{:S(2)}, u32[]{:S(2)}) collective-permute-start(bf16[2,2,16,128]{3,2,1,0:T(8,128)(2,1)S(1)} %maximum_select_fusion), channel_id=1, source_target_pairs={{0,96},{16,112},{32,0},{48,16},{64,32},{80,48},{96,64},{112,80},{1... | collective-permute-start | bytes 49160 | tf_op jit(solution)/shard_map/ppermute | solution.py:329
  63.7 1.3 %copy-start.2 = (bf16[64,2,64,128]{3,2,1,0:T(8,128)(2,1)}, bf16[64,2,64,128]{3,2,1,0:T(8,128)(2,1)S(1)}, u32[]{:S(2)}) copy-start(bf16[64,2,64,128]{3,2,1,0:T(8,128)(2,1)S(1)} %get-tuple-element.58) | copy-start | bytes 6291460
  65.0 8.9 %copy-start.8 = (bf16[2,64,128]{2,1,0:T(8,128)(2,1)S(1)}, bf16[2,64,128]{2,1,0:T(8,128)(2,1)}, u32[]{:S(2)}) copy-start(bf16[2,64,128]{2,1,0:T(8,128)(2,1)} %get-tuple-element.55.after) | copy-start | bytes 98308
  65.0 36.8 %all-to-all-start.1 = ((bf16[64,2,64,128]{3,2,1,0:T(8,128)(2,1)}), bf16[64,2,64,128]{3,2,1,0:T(8,128)(2,1)S(1)}, u32[]{:S(2)}, u32[]{:S(2)}) async-start(bf16[64,2,64,128]{3,2,1,0:T(8,128)(2,1)} %copy-done.2), calls=%async_computation.1 | async-start | bytes 4194304 | tf_op jit(solution)/shard_map/all_to_all | solution.py:371
  73.9 2.8 %copy-start.4 = (bf16[48,512,128]{2,1,0:T(8,128)(2,1)S(1)}, bf16[48,512,128]{2,1,0:T(8,128)(2,1)}, u32[]{:S(2)}) copy-start(bf16[48,512,128]{2,1,0:T(8,128)(2,1)} %rhs.7) | copy-start | bytes 18874372
  76.6 1.4 %copy-start.7 = (bf16[48,128,128]{2,1,0:T(8,128)(2,1)S(1)}, bf16[48,128,128]{2,1,0:T(8,128)(2,1)}, u32[]{:S(2)}) copy-start(bf16[48,128,128]{2,1,0:T(8,128)(2,1)} %inv.3) | copy-start | bytes 4718596
  84.1 2.7 %copy-start = (bf16[48,512,128]{2,1,0:T(8,128)(2,1)}, bf16[48,512,128]{2,1,0:T(8,128)(2,1)S(1)}, u32[]{:S(2)}) copy-start(bf16[48,512,128]{2,1,0:T(8,128)(2,1)S(1)} %leaf.1) | copy-start | bytes 18874372
  101.8 9.4 %collective-permute-start.5 = (bf16[4,32,64,128]{3,2,1,0:T(8,128)(2,1)S(1)}, bf16[4,32,64,128]{3,2,1,0:T(8,128)(2,1)S(1)}, u32[]{:S(2)}, u32[]{:S(2)}) collective-permute-start(bf16[4,32,64,128]{3,2,1,0:T(8,128)(2,1)S(1)} %bitcast.28), channel_id=1, source_target_pairs={{0,16},{16,0},{32,48},{48,32},{64,80},{80,64},{96,112},{112,96},{1... | collective-permute-start | bytes 6291464 | tf_op jit(solution)/shard_map/ppermute | solution.py:374

commit v3 on v2

--- a/solution.py
+++ b/solution.py
@@ -125,13 +125,13 @@
             pltpu.SemaphoreType.DMA((CORES, heights)),
         ],
         out_shape=[jax.ShapeDtypeStruct(half, BF16)] * 2,
-        compiler_params=params(48),
+        compiler_params=params(32),
         name="forward",
         cost_estimate=cost(7_000_000_000, 19_000_000),
     )(blocks, core, *in_hbm(rhs, inv, off))
 
 
-def fold_kernel(g, fanout, inv, off, out, w_inv):
+def fold_kernel(g, fanout, inv, off, after, out, w_inv):
     width = inv.shape[-1]
 
     @pl.when(pl.program_id(0) == 0)
@@ -147,7 +147,7 @@
             out[i + h] = m[:, h * width : (h + 1) * width]
 
 
-def fold(inv, off):
+def fold(inv, off, after):
     leaves, fanout, width, _ = off.shape
     g = 8
     return pl.pallas_call(
@@ -156,17 +156,18 @@
         in_specs=[
             pl.BlockSpec((g, width, width), lambda s: (s, 0, 0)),
             pl.BlockSpec((g, fanout, width, width), lambda s: (s, 0, 0, 0)),
+            pl.BlockSpec(memory_space=pl.ANY),
         ],
         out_specs=pl.BlockSpec((g, fanout * width, width), lambda s: (s, 0, 0)),
         out_shape=jax.ShapeDtypeStruct((leaves, fanout * width, width), BF16),
         scratch_shapes=[pltpu.VMEM((2, 2 * width, 2 * width), BF16)],
-        compiler_params=params(10),
+        compiler_params=params(54),
         name="fold",
         cost_estimate=cost(4_000_000_000, 15_000_000),
-    )(inv, off)
-
-
-def leaf_kernel(g, rhs, inv, after, out, w_inv):
+    )(inv, off, after)
+
+
+def leaf_kernel(g, rhs, inv, out, w_inv):
     width = inv.shape[-1]
 
     @pl.when(pl.program_id(0) == 0)
@@ -183,7 +184,7 @@
             out[i + h] = z[:, h * width : (h + 1) * width]
 
 
-def leaf(rhs, inv, after):
+def leaf(rhs, inv):
     leaves, nrhs, width = rhs.shape
     g = 8
     return pl.pallas_call(
@@ -192,19 +193,19 @@
         in_specs=[
             pl.BlockSpec((g, nrhs, width), lambda s: (s, 0, 0)),
             pl.BlockSpec((g, width, width), lambda s: (s, 0, 0)),
-            pl.BlockSpec(memory_space=pl.ANY),
         ],
         out_specs=pl.BlockSpec((g, nrhs, width), lambda s: (s, 0, 0)),
         out_shape=jax.ShapeDtypeStruct(rhs.shape, BF16),
         scratch_shapes=[pltpu.VMEM((2, 2 * width, 2 * width), BF16)],
-        compiler_params=params(10),
+        compiler_params=params(54),
         name="leaf",
         cost_estimate=cost(6_000_000_000, 20_000_000),
-    )(rhs, inv, after)
-
-
-def parent_kernel(sources, got, rhs, inv, after, x_out, x_every):
-    own, block_rows, width = rhs.shape
+    )(rhs, inv)
+
+
+def parent_kernel(sources, targets, got, rhs, pieces, place, after, x_out, x_every):
+    own, block_rows, width = x_out.shape
+    side = pieces.shape[0]
     total = got[0].astype(F32)
     for s in range(1, sources):
         total += got[s].astype(F32)
@@ -214,44 +215,52 @@
         left = rest - high.astype(F32)
         mid = left.astype(BF16)
         low = (left - mid.astype(F32)).astype(BF16)
-        w = inv[p]
+        w = jnp.concatenate(
+            [pieces[lax.rem(place[0] - t + side, side), p] for t in range(side)], axis=0
+        )
         y = (mm_t(low, w) + mm_t(mid, w)) + mm_t(high, w)
         x = mm(y.astype(BF16), w).astype(BF16)
         x_out[p] = x
-        for s in range(sources):
+        for s in range(targets):
             x_every[s, p] = x
 
 
-def parent(got, rhs, inv, after):
+def parent(got, rhs, pieces, place, after, targets):
     sources = got.shape[0]
     return pl.pallas_call(
-        functools.partial(parent_kernel, sources),
-        in_specs=[pl.BlockSpec(memory_space=pltpu.VMEM)] * 3 + [pl.BlockSpec(memory_space=pl.ANY)],
+        functools.partial(parent_kernel, sources, targets),
+        in_specs=[pl.BlockSpec(memory_space=pltpu.VMEM)] * 3
+        + [pl.BlockSpec(memory_space=pltpu.SMEM), pl.BlockSpec(memory_space=pl.ANY)],
         out_shape=[
-            jax.ShapeDtypeStruct(rhs.shape, BF16),
-            jax.ShapeDtypeStruct(got.shape, BF16),
+            jax.ShapeDtypeStruct(got.shape[1:], BF16),
+            jax.ShapeDtypeStruct((targets,) + got.shape[1:], BF16),
         ],
         compiler_params=params(16),
         name="parent",
         cost_estimate=cost(30_000_000, 4_500_000),
-    )(got, rhs, inv, after)
-
-
-def backward_kernel(g, fanout, blocks, which, base_hbm, folded_hbm, xs, *rest):
+    )(got, rhs, pieces, place, after)
+
+
+def backward_kernel(g, fanout, n_xs, blocks, which, base_hbm, folded_hbm, *rest):
+    xs = [ref.at[n] for ref in rest[:n_xs] for n in range(ref.shape[0])]
     out_hbm, base, folded, out, w, in_sems, out_sems = rest[-7:]
-    leaves, heights, block_rows, width = base.shape
-    c = which[0]
+    leaves, parts, block_rows, width = base.shape
 
     def fetches(i):
         some = pl.ds(g * i, g)
         return [
-            pltpu.make_async_copy(folded_hbm.at[some], folded.at[some], in_sems.at[0, i]),
-            pltpu.make_async_copy(base_hbm.at[some, :, c], base.at[some], in_sems.at[1, i]),
+            pltpu.make_async_copy(folded_hbm.at[some], folded.at[some], in_sems.at[parts, i])
+        ] + [
+            pltpu.make_async_copy(base_hbm.at[some, which[n]], base.at[some, n], in_sems.at[n, i])
+            for n in range(parts)
         ]
 
-    def store(i):
+    def stores(i):
         some = pl.ds(g * i, g)
-        return pltpu.make_async_copy(out.at[some], out_hbm.at[some, :, c], out_sems.at[i])
+        return [
+            pltpu.make_async_copy(out.at[some, n], out_hbm.at[some, which[n]], out_sems.at[n, i])
+            for n in range(parts)
+        ]
 
     for i in range(leaves // g):
         for copy in fetches(i):
@@ -263,9 +272,7 @@
         diagonal(w, slot, [folded[j], folded[j + 1]])
         x = jnp.concatenate(
             [
-                jnp.concatenate(
-                    [xs[z, blocks[(j + h) * fanout + k]] for z in range(heights)], axis=0
-                )
+                jnp.concatenate([ref[blocks[(j + h) * fanout + k]] for ref in xs], axis=0)
                 for h in range(2)
                 for k in range(fanout)
             ],
@@ -273,10 +280,10 @@
         )
         back = mm(x, w[slot])
         for h in range(2):
-            for z in range(heights):
-                row = z * block_rows
+            for n in range(parts):
+                row = n * block_rows
                 part = back[row : row + block_rows, h * width : (h + 1) * width]
-                out[j + h, z] = (base[j + h, z].astype(F32) - part).astype(BF16)
+                out[j + h, n] = (base[j + h, n].astype(F32) - part).astype(BF16)
 
     @pl.loop(0, leaves // g)
     def _(i):
@@ -284,97 +291,125 @@
             copy.wait()
         for u in range(0, g, 2):
             pair(i * g + u, (u // 2) % w.shape[0])
-        store(i).start()
+        for copy in stores(i):
+            copy.start()
 
     for i in range(leaves // g):
-        store(i).wait()
+        for copy in stores(i):
+            copy.wait()
 
 
 def backward(blocks, which, base, folded, xs, so_far=None):
-    leaves, heights, _, block_rows, width = base.shape
+    leaves, _, block_rows, width = base.shape
     fanout = folded.shape[1] // width
-    half = (leaves, heights, block_rows, width)
+    parts = which.shape[0]
+    some = (leaves, parts, block_rows, width)
     g, slots = B_G, B_S
     more = [] if so_far is None else [so_far]
-    smem, hbm = pl.BlockSpec(memory_space=pltpu.SMEM), pl.BlockSpec(memory_space=pltpu.HBM)
+    smem, hbm, vmem = (
+        pl.BlockSpec(memory_space=m) for m in (pltpu.SMEM, pltpu.HBM, pltpu.VMEM)
+    )
     return pl.pallas_call(
-        functools.partial(backward_kernel, g, fanout),
-        in_specs=[smem, smem, hbm, hbm, pl.BlockSpec(memory_space=pltpu.VMEM)] + [hbm] * len(more),
+        functools.partial(backward_kernel, g, fanout, len(xs)),
+        in_specs=[smem, smem, hbm, hbm] + [vmem] * len(xs) + [hbm] * len(more),
         out_specs=hbm,
         scratch_shapes=[
-            pltpu.VMEM(half, BF16),
+            pltpu.VMEM(some, BF16),
             pltpu.VMEM(folded.shape, BF16),
-            pltpu.VMEM(half, BF16),
+            pltpu.VMEM(some, BF16),
             pltpu.VMEM((slots, 2 * fanout * width, 2 * width), BF16),
-            pltpu.SemaphoreType.DMA((2, leaves // g)),
-            pltpu.SemaphoreType.DMA((leaves // g,)),
+            pltpu.SemaphoreType.DMA((parts + 1, leaves // g)),
+            pltpu.SemaphoreType.DMA((parts, leaves // g)),
         ],
         out_shape=jax.ShapeDtypeStruct(base.shape, BF16),
-        input_output_aliases={5: 0} if more else {},
+        input_output_aliases={4 + len(xs): 0} if more else {},
         compiler_params=params(24),
         name="backward",
         cost_estimate=cost(5_000_000_000, 13_000_000),
-    )(blocks, which, *in_hbm(base, folded), xs, *more)
-
-
-def gather_inverse(par_inv, rows):
-    own, part, width = par_inv.shape
-    heights = rows // CORES
-    place = lax.axis_index("row")
-    across = lax.ppermute(par_inv, "row", [(r, r ^ 1) for r in range(rows)])
-    pair = jnp.where(
-        place % CORES == 0, jnp.stack([par_inv, across]), jnp.stack([across, par_inv])
-    )
-    parts = [pair] + [
-        lax.ppermute(pair, "row", [(r, (r + CORES * s) % rows) for r in range(rows)])
-        for s in range(1, heights)
-    ]
-    z = place // CORES
-    stacked = jnp.stack(parts)
-    whole = jnp.zeros_like(stacked)
-    for h in range(heights):
-        pick = sum(
-            jnp.where((z - h) % heights == s, parts[s].astype(F32), 0.0) for s in range(heights)
-        )
-        whole = whole.at[h].set(pick.astype(BF16))
-    return whole.transpose(2, 0, 1, 3, 4).reshape(own, rows * part, width)
+    )(blocks, which, *in_hbm(base, folded), *xs, *more)
 
 
 def on_device(rows, cols, leaf_rhs, leaf_inv, leaf_off, blocks, par_rhs, par_inv):
     own, block_rows, width = par_rhs.shape
+    leaves, nrhs, _ = leaf_rhs.shape
     parents = own * cols
-    heights = rows // CORES
-    chips = heights * cols
-    core = (lax.axis_index("row") % CORES).astype(jnp.int32).reshape(1)
+    side = rows // CORES
+    deep = cols // side
+    both = ("row", "col")
+
+    def device(u, c, v, y):
+        z, x = (u % side, v) if c == 0 else (v, u % side)
+        return (z * CORES + c) * cols + x * deep + y
+
+    every = [
+        (u, c, v, y)
+        for u in range(side)
+        for c in range(CORES)
+        for v in range(side)
+        for y in range(deep)
+    ]
+    turn = [(device(u, 0, v, y) + (cols if c else 0), device(u, c, v, y)) for u, c, v, y in every]
+    swap = [(r, r ^ 1) for r in range(rows)]
+    row, col = lax.axis_index("row"), lax.axis_index("col")
+    core = (row % CORES).astype(jnp.int32)
+    z, x = (row // CORES).astype(jnp.int32), (col // deep).astype(jnp.int32)
+    u, other_u = jnp.where(core == 0, z, x), jnp.where(core == 0, x, z)
+
+    def along(a, step):
+        return lax.ppermute(
+            a, both, [(device(u, c, v, y), device(u + step, c, v, y)) for u, c, v, y in every]
+        )
+
+    def spread(a, first, stride):
+        groups = [
+            [device(u, c, v, y) for u in range(f, side, stride) for v in range(side) for y in range(deep)]
+            for c in range(CORES)
+            for f in first
+        ]
+        return lax.all_to_all(a, both, 0, 0, axis_index_groups=groups, tiled=True)
+
+    by_core = (leaves, side, CORES, block_rows, width)
+
     flat = blocks.reshape(-1)
-    swap = [(r, r ^ 1) for r in range(rows)]
-    groups = [
-        [(z * CORES + c) * cols + k for z in range(heights) for k in range(cols)]
-        for c in range(CORES)
-    ]
-    spread = functools.partial(
-        lax.all_to_all,
-        axis_name=("row", "col"),
-        split_axis=0,
-        concat_axis=0,
-        axis_index_groups=groups,
-        tiled=True,
+    across = lax.ppermute(par_inv, "row", swap)
+    keep, send = forward(flat, core.reshape(1), leaf_rhs.reshape(by_core), leaf_inv, leaf_off, parents)
+    across, send = lax.optimization_barrier((across, send))
+    low, high = jnp.where(core == 0, par_inv, across), jnp.where(core == 0, across, par_inv)
+    given = lax.ppermute(jnp.concatenate([par_rhs, low, high], axis=1), both, turn)
+    received = lax.ppermute(send, "row", swap)
+    chip = (keep.astype(F32) + received.astype(F32)).astype(BF16)
+    chip, given = lax.optimization_barrier((chip, given))
+    pair = given[:, block_rows:]
+    shifts = [pair] + [along(pair, step) for step in range(1, side)]
+    got = spread(chip.reshape(side * cols, own, block_rows, width), (0,), 1)
+    base = leaf(leaf_rhs, leaf_inv)
+    pieces = jnp.stack(shifts)
+    par_x, targets = parent(
+        got, given[:, :block_rows], pieces, u.reshape(1), base[0, :16], side // 2 * cols
     )
-
-    inverse = gather_inverse(par_inv, rows)
-    by_core = (leaf_rhs.shape[0], heights, CORES, block_rows, width)
-    keep, send = forward(flat, core, leaf_rhs.reshape(by_core), leaf_inv, leaf_off, parents)
-    chip = (keep.astype(F32) + lax.ppermute(send, "row", swap).astype(F32)).astype(BF16)
-    got = spread(chip.reshape(chips, own, block_rows, width))
-    folded = fold(leaf_inv, leaf_off)
-    par_x, every = parent(got, par_rhs, inverse, folded[0, :16])
-    mine = spread(every).reshape(heights, parents, block_rows, width)
-    base = leaf(leaf_rhs, leaf_inv, par_x).reshape(by_core)
-    mine, base = lax.optimization_barrier((mine, base))
-    other = lax.ppermute(mine, "row", swap)
-    half = backward(flat, core, base, folded, mine)
-    leaf_x = backward(flat, 1 - core, base, folded, other, half)
-    return (leaf_x.reshape(leaf_rhs.shape), par_x)
+    near = spread(targets, (0, 1), 2).reshape(side // 2, parents, block_rows, width)
+    folded = fold(leaf_inv, leaf_off, par_x)
+    near, base, folded, x_out = lax.optimization_barrier(
+        (near, base, folded, lax.ppermute(par_x, both, turn))
+    )
+    base = base.reshape(leaves, rows, block_rows, width)
+
+    mine = jnp.where(u < 2, near[:1], near[1:])
+    near_other = lax.ppermute(near, "row", swap)
+    far = [along(mine, -1), along(mine, 1)]
+
+    def places(us, other_us):
+        return jnp.stack(
+            [(a % side) * CORES + core for a in us] + [(a % side) * CORES + 1 - core for a in other_us]
+        ).astype(jnp.int32)
+
+    first = places((u % 2, u % 2 + 2), (other_u % 2, other_u % 2 + 2))
+    second = places((u + 1, u + side - 1), (other_u + 1, other_u + side - 1))
+    half = backward(flat, first, base, folded, [near, near_other])
+    far, half = lax.optimization_barrier((far, half))
+    far_other = [lax.ppermute(a, "row", swap) for a in far]
+    leaf_x = backward(flat, second, base, folded, far + far_other, half)
+    return (leaf_x.reshape(leaf_rhs.shape), x_out)
 
 
 def solution(mesh):

time: 119 us -> 113 us (0.950)
  local copies, waits for them, and re-layouts: 15.7 us -> 2.21 us
  Pallas kernels: 37.5 us -> 46.8 us
  waiting for transfers between devices: 31 us -> 25.2 us
  starting transfers between devices: 30.7 us -> 32.7 us
  other arithmetic: 2.37 us -> 4.1 us
    unnamed x21 -> x8, local copies, waits for them, and re-layouts: 14.9 us -> 1.4 us
    all_to_all x2, waiting for transfers between devices: 17.1 us -> 9.57 us  [spread(): return lax.all_to_all(a, both, 0, 0, axis_index_groups=groups, tiled=True)]
    ppermute x6 -> x12, starting transfers between devices: 10.5 us -> 15.7 us  [the longest x5 8.12 us: along(): lax.ppermute(a, both, [(device(u, c, v, y), device(u + step, c, v, y)) fo...]
    pallas_call x1, Pallas kernels: 2.62 us -> 7.39 us  [fold(): pl.pallas_call(functools.partial(fold_kernel, g, fanout), grid=(leaves //...]
    pallas_call x1, Pallas kernels: 6.03 us -> 9.77 us  [leaf(): pl.pallas_call(functools.partial(leaf_kernel, g), grid=(leaves // g,), in...]
    all_to_all x2, starting transfers between devices: 20.2 us -> 17 us  [spread(): return lax.all_to_all(a, both, 0, 0, axis_index_groups=groups, tiled=True)]
    ppermute x6 -> x12, waiting for transfers between devices: 13.9 us -> 15.6 us  [the longest x5 9.71 us: along(): lax.ppermute(a, both, [(device(u, c, v, y), device(u + step, c, v, y)) fo...]
    convert_element_type x1, other arithmetic: 2.25 us -> 3.87 us  [on_device(): chip = (keep.astype(F32) + received.astype(F32)).astype(BF16)]
  transfers between devices with their start and end apart: 8 -> 14, of which waited for: 5 -> 6; matrix products, arithmetic and copies ran while one was open for 1% -> 5% of each run, Pallas kernels for 13% -> 34%
where the time goes in v3:
time: 113 us; the launch traced here: 112 us
  Pallas kernels  46.8 us (41%)
  starting transfers between devices  32.7 us (29%)
  waiting for transfers between devices  25.2 us (22%)
  other arithmetic  4.1 us (4%)
  local copies, waits for them, and re-layouts  2.21 us (2%)
    all_to_all x2, starting transfers between devices, spread(): return lax.all_to_all(a, both, 0, 0, axis_index_groups=groups, tiled=True)  17 us
    pallas_call x1, Pallas kernels, forward(): pl.pallas_call(functools.partial(forward_kernel, g, fanout), in_specs=[sm...  14.1 us
    pallas_call x2, Pallas kernels, backward(): pl.pallas_call(functools.partial(backward_kernel, g, fanout, len(xs)), in...  13.9 us
    pallas_call x1, Pallas kernels, leaf(): pl.pallas_call(functools.partial(leaf_kernel, g), grid=(leaves // g,), in...  9.77 us
    ppermute x5, waiting for transfers between devices, along(): lax.ppermute(a, both, [(device(u, c, v, y), device(u + step, c, v, y)) fo...  9.71 us
    all_to_all x2, waiting for transfers between devices, spread(): return lax.all_to_all(a, both, 0, 0, axis_index_groups=groups, tiled=True)  9.57 us
    ppermute x5, starting transfers between devices, along(): lax.ppermute(a, both, [(device(u, c, v, y), device(u + step, c, v, y)) fo...  8.12 us
    pallas_call x1, Pallas kernels, fold(): pl.pallas_call(functools.partial(fold_kernel, g, fanout), grid=(leaves //...  7.39 us
  transfers between devices with their start and end apart: 14, of which 6 were waited for; matrix products, arithmetic and copies ran while one was open for 5% of the time, Pallas kernels for 34%

profile of v3, /device:TPU:1, one launch (start us, length us, event | category | flops | bytes accessed | tf_op | source)
XLA Modules:
  0.0 111.9 jit_solution(5497726622907289175)
XLA Ops:
  0.6 1.5 %collective-permute-start = (bf16[2,16,128]{2,1,0:T(8,128)(2,1)}, bf16[2,16,128]{2,1,0:T(8,128)(2,1)S(1)}, u32[]{:S(2)}, u32[]{:S(2)}) collective-permute-start(bf16[2,16,128]{2,1,0:T(8,128)(2,1)} %param.11), channel_id=1, source_target_pairs={{0,16},{16,0},{32,48},{48,32},{64,80},{80,64},{96,112},{112,96},{1... | collective-permute-start | bytes 24584 | tf_op jit(solution)/shard_map/ppermute | solution.py:374
  2.1 0.8 copy.9
  2.9 0.1 reshape.28.blocks
  3.0 0.0 copy-start.2
  3.0 0.0 copy-start.1
  3.1 14.1 %forward.1 = (bf16[4,32,64,128]{3,2,1,0:T(8,128)(2,1)S(1)}, bf16[4,32,64,128]{3,2,1,0:T(8,128)(2,1)}) custom-call(s32[144]{0:T(256)S(1)} %reshape.28.blocks, s32[1]{0:T(128)} %bitcast.4.core, bf16[48,4,2,64,128]{4,3,2,1,0:T(8,128)(2,1)} %bitcast.32, bf16[48,128,128]{2,1,0:T(8,128)(2,1)} %inv.3, bf16[48,3,128,128]{3,2,1,0:T(8,128)(2,1)} %off.1), custom_call_target="tpu_custom_call" | custom-call | flops 7000000000 | bytes 19000000 | tf_op jit(solution)/shard_map/forward/pallas_call | solution.py:112
  17.2 0.0 collective-permute-done
  17.2 0.1 collective-permute-start.1
  17.3 0.0 copy-done.2
  17.3 0.0 copy-done.1
  17.3 0.7 collective-permute-start.2
  18.0 3.8 %collective-permute-done.1 = bf16[4,32,64,128]{3,2,1,0:T(8,128)(2,1)} collective-permute-done((bf16[4,32,64,128]{3,2,1,0:T(8,128)(2,1)}, bf16[4,32,64,128]{3,2,1,0:T(8,128)(2,1)}, u32[]{:S(2)}, u32[]{:S(2)}) %collective-permute-start.1) | collective-permute-done | bytes 2097184 | tf_op jit(solution)/shard_map/ppermute | solution.py:379
  21.8 3.9 %add_convert_fusion = bf16[4,32,64,128]{3,2,1,0:T(8,128)(2,1)} fusion(bf16[4,32,64,128]{3,2,1,0:T(8,128)(2,1)} %collective-permute-done.1, bf16[4,32,64,128]{3,2,1,0:T(8,128)(2,1)S(1)} %get-tuple-element.17), kind=kLoop, calls=%fused_computation | loop fusion | flops 4194304 | bytes 6291456 | tf_op jit(solution)/shard_map/convert_element_type | solution.py:380
  25.6 0.0 collective-permute-done.2
  25.6 11.2 %all-to-all-start = ((bf16[64,2,64,128]{3,2,1,0:T(8,128)(2,1)}), bf16[64,2,64,128]{3,2,1,0:T(8,128)(2,1)S(1)}, u32[]{:S(2)}, u32[]{:S(2)}) async-start(bf16[64,2,64,128]{3,2,1,0:T(8,128)(2,1)} %bitcast.28), calls=%async_computation | async-start | bytes 4194304 | tf_op jit(solution)/shard_map/all_to_all | solution.py:369
  36.9 9.8 %leaf.1 = bf16[48,512,128]{2,1,0:T(8,128)(2,1)} custom-call(bf16[48,512,128]{2,1,0:T(8,128)(2,1)} %rhs.1, bf16[48,128,128]{2,1,0:T(8,128)(2,1)} %inv.3), custom_call_target="tpu_custom_call" | custom-call | flops 6000000000 | bytes 20000000 | tf_op jit(solution)/shard_map/leaf/pallas_call | solution.py:190
  46.6 2.7 %collective-permute-start.4 = (bf16[2,32,128]{2,1,0:T(8,128)(2,1)S(1)}, bf16[2,32,128]{2,1,0:T(8,128)(2,1)S(1)}, u32[]{:S(2)}, u32[]{:S(2)}) collective-permute-start(bf16[2,32,128]{2,1,0:T(8,128)(2,1)S(1)} %get-tuple-element.33), channel_id=1, source_target_pairs={{0,64},{1,65},{2,66},{3,67},{4,68},{5,69},{6,70},{7,71},{8,72},{9,... | collective-permute-start | bytes 49160 | tf_op jit(solution)/shard_map/ppermute | solution.py:359
  49.3 0.4 collective-permute-start.3
  49.7 2.3 %collective-permute-start.5 = (bf16[2,32,128]{2,1,0:T(8,128)(2,1)S(1)}, bf16[2,32,128]{2,1,0:T(8,128)(2,1)S(1)}, u32[]{:S(2)}, u32[]{:S(2)}) collective-permute-start(bf16[2,32,128]{2,1,0:T(8,128)(2,1)S(1)} %get-tuple-element.33), channel_id=1, source_target_pairs={{0,96},{1,97},{2,98},{3,99},{4,100},{5,101},{6,102},{7,103},{8,104... | collective-permute-start | bytes 49160 | tf_op jit(solution)/shard_map/ppermute | solution.py:359
  52.0 0.7 slice_bitcast_fusion.after
  52.7 9.7 %collective-permute-done.4 = bf16[2,32,128]{2,1,0:T(8,128)(2,1)S(1)} collective-permute-done((bf16[2,32,128]{2,1,0:T(8,128)(2,1)S(1)}, bf16[2,32,128]{2,1,0:T(8,128)(2,1)S(1)}, u32[]{:S(2)}, u32[]{:S(2)}) %collective-permute-start.4) | collective-permute-done | bytes 16416 | tf_op jit(solution)/shard_map/ppermute | solution.py:359
  62.4 0.0 collective-permute-done.3
  62.4 0.0 collective-permute-done.5
  62.4 2.3 %all-to-all-done.got = bf16[64,2,64,128]{3,2,1,0:T(8,128)(2,1)S(1)} async-done(((bf16[64,2,64,128]{3,2,1,0:T(8,128)(2,1)}), bf16[64,2,64,128]{3,2,1,0:T(8,128)(2,1)S(1)}, u32[]{:S(2)}, u32[]{:S(2)}) %all-to-all-start) | async-done | bytes 2097184 | tf_op jit(solution)/shard_map/all_to_all | solution.py:369
  64.7 1.7 %parent.1 = (bf16[2,64,128]{2,1,0:T(8,128)(2,1)S(1)}, bf16[32,2,64,128]{3,2,1,0:T(8,128)(2,1)}) custom-call(bf16[64,2,64,128]{3,2,1,0:T(8,128)(2,1)S(1)} %all-to-all-done.got, bf16[2,64,128]{2,1,0:T(8,128)(2,1)S(1)} %slice.15.rhs, bf16[4,2,32,128]{3,2,1,0:T(8,128)(2,1)S(1)} %pad_maximum_fusion.pieces, s32[1]{0:T(128)} %bitcast.11.place, ...), custom_call_target="tpu_custom_call" | custom-call | flops 30000000 | bytes 4500000 | tf_op jit(solution)/shard_map/parent/pallas_call | solution.py:230
  66.4 0.0 copy-start
  66.4 5.8 %all-to-all-start.1 = ((bf16[32,2,64,128]{3,2,1,0:T(8,128)(2,1)}), bf16[32,2,64,128]{3,2,1,0:T(8,128)(2,1)S(1)}, u32[]{:S(2)}, u32[]{:S(2)}) async-start(bf16[32,2,64,128]{3,2,1,0:T(8,128)(2,1)} %get-tuple-element.23), calls=%async_computation.1 | async-start | bytes 2097152 | tf_op jit(solution)/shard_map/all_to_all | solution.py:369
  72.2 0.7 collective-permute-start.6
  72.9 0.0 copy-done
  72.9 7.4 %fold.1.folded_hbm = bf16[48,384,128]{2,1,0:T(8,128)(2,1)} custom-call(bf16[48,128,128]{2,1,0:T(8,128)(2,1)} %inv.3, bf16[48,3,128,128]{3,2,1,0:T(8,128)(2,1)} %off.1, bf16[2,64,128]{2,1,0:T(8,128)(2,1)} %copy-done), custom_call_target="tpu_custom_call" | custom-call | flops 4000000000 | bytes 15000000 | tf_op jit(solution)/shard_map/fold/pallas_call | solution.py:153
  80.3 0.0 collective-permute-done.6
  80.3 7.3 %all-to-all-done.1 = bf16[32,2,64,128]{3,2,1,0:T(8,128)(2,1)S(1)} async-done(((bf16[32,2,64,128]{3,2,1,0:T(8,128)(2,1)}), bf16[32,2,64,128]{3,2,1,0:T(8,128)(2,1)S(1)}, u32[]{:S(2)}, u32[]{:S(2)}) %all-to-all-start.1) | async-done | bytes 1048608 | tf_op jit(solution)/shard_map/all_to_all | solution.py:369
  87.6 3.9 %collective-permute-start.9 = (bf16[2,32,64,128]{3,2,1,0:T(8,128)(2,1)S(1)}, bf16[2,32,64,128]{3,2,1,0:T(8,128)(2,1)S(1)}, u32[]{:S(2)}, u32[]{:S(2)}) collective-permute-start(bf16[2,32,64,128]{3,2,1,0:T(8,128)(2,1)S(1)} %bitcast.22), channel_id=1, source_target_pairs={{0,16},{16,0},{32,48},{48,32},{64,80},{80,64},{96,112},{112,96},{1... | collective-permute-start | bytes 3145736 | tf_op jit(solution)/shard_map/ppermute | solution.py:398
  91.5 0.1 slice_select_fusion
  91.6 0.9 collective-permute-start.8
  92.5 1.8 %collective-permute-start.7 = (bf16[1,32,64,128]{3,2,1,0:T(8,128)(2,1)S(1)}, bf16[1,32,64,128]{3,2,1,0:T(8,128)(2,1)S(1)}, u32[]{:S(2)}, u32[]{:S(2)}) collective-permute-start(bf16[1,32,64,128]{3,2,1,0:T(8,128)(2,1)S(1)} %slice_select_fusion), channel_id=1, source_target_pairs={{0,96},{1,97},{2,98},{3,99},{4,100},{5,101},{6,102},{7,103},{8,104... | collective-permute-start | bytes 1572872 | tf_op jit(solution)/shard_map/ppermute | solution.py:359
  94.3 0.1 pad_add_fusion.1.which
  94.4 0.0 collective-permute-done.9.rest_1_
  94.4 6.9 %backward.2.rest_4_ = bf16[48,8,64,128]{3,2,1,0:T(8,128)(2,1)} custom-call(s32[144]{0:T(256)S(1)} %reshape.28.blocks, s32[4]{0:T(128)S(1)} %pad_add_fusion.1.which, bf16[48,8,64,128]{3,2,1,0:T(8,128)(2,1)} %bitcast.25, bf16[48,384,128]{2,1,0:T(8,128)(2,1)} %fold.1.folded_hbm, bf16[2,32,64,128]{3,2,1,0:T(8,128)(2,1)S(1)} %bitcast.24, ...), custom_call_target="tpu_custom_call" | custom-call | flops 5000000000 | bytes 13000000 | tf_op jit(solution)/shard_map/backward/pallas_call | solution.py:312
  101.3 0.0 collective-permute-done.8.rest_1_
  101.3 0.0 collective-permute-done.7.rest_0_
  101.3 0.7 collective-permute-start.10
  102.0 0.1 collective-permute-start.11
  102.1 0.1 pad_add_fusion.which
  102.2 1.4 %collective-permute-done.10.rest_2_ = bf16[1,32,64,128]{3,2,1,0:T(8,128)(2,1)S(1)} collective-permute-done((bf16[1,32,64,128]{3,2,1,0:T(8,128)(2,1)S(1)}, bf16[1,32,64,128]{3,2,1,0:T(8,128)(2,1)S(1)}, u32[]{:S(2)}, u32[]{:S(2)}) %collective-permute-start.10) | collective-permute-done | bytes 524320 | tf_op jit(solution)/shard_map/ppermute | solution.py:410
  103.6 0.7 collective-permute-done.11.rest_3_
  104.3 6.9 %backward.3 = bf16[48,8,64,128]{3,2,1,0:T(8,128)(2,1)} custom-call(s32[144]{0:T(256)S(1)} %reshape.28.blocks, s32[4]{0:T(128)S(1)} %pad_add_fusion.which, bf16[48,8,64,128]{3,2,1,0:T(8,128)(2,1)} %bitcast.26, bf16[48,384,128]{2,1,0:T(8,128)(2,1)} %fold.1.folded_hbm, ...), custom_call_target="tpu_custom_call", output_to_operand_aliasing={{}: (8, {})} | custom-call | flops 5000000000 | bytes 13000000 | tf_op jit(solution)/shard_map/backward/pallas_call | solution.py:312
  111.3 0.6 copy.12
  (5 shorter events, 0.0 us)
Async XLA Ops:
  0.6 16.5 %collective-permute-start = (bf16[2,16,128]{2,1,0:T(8,128)(2,1)}, bf16[2,16,128]{2,1,0:T(8,128)(2,1)S(1)}, u32[]{:S(2)}, u32[]{:S(2)}) collective-permute-start(bf16[2,16,128]{2,1,0:T(8,128)(2,1)} %param.11), channel_id=1, source_target_pairs={{0,16},{16,0},{32,48},{48,32},{64,80},{80,64},{96,112},{112,96},{1... | collective-permute-start | bytes 24584 | tf_op jit(solution)/shard_map/ppermute | solution.py:374
  3.0 14.3 %copy-start.2 = (bf16[2,16,128]{2,1,0:T(8,128)(2,1)S(1)}, bf16[2,16,128]{2,1,0:T(8,128)(2,1)}, u32[]{:S(2)}) copy-start(bf16[2,16,128]{2,1,0:T(8,128)(2,1)} %param.11) | copy-start | bytes 24580
  3.0 14.3 %copy-start.1 = (bf16[2,64,128]{2,1,0:T(8,128)(2,1)S(1)}, bf16[2,64,128]{2,1,0:T(8,128)(2,1)}, u32[]{:S(2)}) copy-start(bf16[2,64,128]{2,1,0:T(8,128)(2,1)} %param.10) | copy-start | bytes 98308
  17.2 4.6 %collective-permute-start.1 = (bf16[4,32,64,128]{3,2,1,0:T(8,128)(2,1)}, bf16[4,32,64,128]{3,2,1,0:T(8,128)(2,1)}, u32[]{:S(2)}, u32[]{:S(2)}) collective-permute-start(bf16[4,32,64,128]{3,2,1,0:T(8,128)(2,1)} %get-tuple-element.19), channel_id=1, source_target_pairs={{0,16},{16,0},{32,48},{48,32},{64,80},{80,64},{96,112},{112,96},{1... | collective-permute-start | bytes 6291464 | tf_op jit(solution)/shard_map/ppermute | solution.py:379
  17.3 8.3 %collective-permute-start.2 = (bf16[2,96,128]{2,1,0:T(8,128)(2,1)S(1)}, bf16[2,96,128]{2,1,0:T(8,128)(2,1)S(1)}, u32[]{:S(2)}, u32[]{:S(2)}) collective-permute-start(bf16[2,96,128]{2,1,0:T(8,128)(2,1)S(1)} %pad_maximum_fusion.1), channel_id=1, source_target_pairs={{0,0},{1,1},{2,2},{3,3},{4,4},{5,5},{6,6},{7,7},{8,8},{9,9},{10,10... | collective-permute-start | bytes 147464 | tf_op jit(solution)/shard_map/ppermute | solution.py:378
  25.6 39.1 %all-to-all-start = ((bf16[64,2,64,128]{3,2,1,0:T(8,128)(2,1)}), bf16[64,2,64,128]{3,2,1,0:T(8,128)(2,1)S(1)}, u32[]{:S(2)}, u32[]{:S(2)}) async-start(bf16[64,2,64,128]{3,2,1,0:T(8,128)(2,1)} %bitcast.28), calls=%async_computation | async-start | bytes 4194304 | tf_op jit(solution)/shard_map/all_to_all | solution.py:369
  46.6 15.7 %collective-permute-start.4 = (bf16[2,32,128]{2,1,0:T(8,128)(2,1)S(1)}, bf16[2,32,128]{2,1,0:T(8,128)(2,1)S(1)}, u32[]{:S(2)}, u32[]{:S(2)}) collective-permute-start(bf16[2,32,128]{2,1,0:T(8,128)(2,1)S(1)} %get-tuple-element.33), channel_id=1, source_target_pairs={{0,64},{1,65},{2,66},{3,67},{4,68},{5,69},{6,70},{7,71},{8,72},{9,... | collective-permute-start | bytes 49160 | tf_op jit(solution)/shard_map/ppermute | solution.py:359
  49.3 13.1 %collective-permute-start.3 = (bf16[2,32,128]{2,1,0:T(8,128)(2,1)S(1)}, bf16[2,32,128]{2,1,0:T(8,128)(2,1)S(1)}, u32[]{:S(2)}, u32[]{:S(2)}) collective-permute-start(bf16[2,32,128]{2,1,0:T(8,128)(2,1)S(1)} %get-tuple-element.33), channel_id=1, source_target_pairs={{0,32},{1,33},{2,34},{3,35},{4,36},{5,37},{6,38},{7,39},{8,40},{9,... | collective-permute-start | bytes 49160 | tf_op jit(solution)/shard_map/ppermute | solution.py:359
  49.7 12.7 %collective-permute-start.5 = (bf16[2,32,128]{2,1,0:T(8,128)(2,1)S(1)}, bf16[2,32,128]{2,1,0:T(8,128)(2,1)S(1)}, u32[]{:S(2)}, u32[]{:S(2)}) collective-permute-start(bf16[2,32,128]{2,1,0:T(8,128)(2,1)S(1)} %get-tuple-element.33), channel_id=1, source_target_pairs={{0,96},{1,97},{2,98},{3,99},{4,100},{5,101},{6,102},{7,103},{8,104... | collective-permute-start | bytes 49160 | tf_op jit(solution)/shard_map/ppermute | solution.py:359
  66.4 6.5 %copy-start = (bf16[2,64,128]{2,1,0:T(8,128)(2,1)}, bf16[2,64,128]{2,1,0:T(8,128)(2,1)S(1)}, u32[]{:S(2)}) copy-start(bf16[2,64,128]{2,1,0:T(8,128)(2,1)S(1)} %get-tuple-element.24.after) | copy-start | bytes 98308
  66.4 21.1 %all-to-all-start.1 = ((bf16[32,2,64,128]{3,2,1,0:T(8,128)(2,1)}), bf16[32,2,64,128]{3,2,1,0:T(8,128)(2,1)S(1)}, u32[]{:S(2)}, u32[]{:S(2)}) async-start(bf16[32,2,64,128]{3,2,1,0:T(8,128)(2,1)} %get-tuple-element.23), calls=%async_computation.1 | async-start | bytes 2097152 | tf_op jit(solution)/shard_map/all_to_all | solution.py:369
  72.2 8.1 %collective-permute-start.6 = (bf16[2,64,128]{2,1,0:T(8,128)(2,1)S(1)}, bf16[2,64,128]{2,1,0:T(8,128)(2,1)S(1)}, u32[]{:S(2)}, u32[]{:S(2)}) collective-permute-start(bf16[2,64,128]{2,1,0:T(8,128)(2,1)S(1)} %get-tuple-element.24.after), channel_id=1, source_target_pairs={{0,0},{1,1},{2,2},{3,3},{4,4},{5,5},{6,6},{7,7},{8,8},{9,9},{10,10... | collective-permute-start | bytes 98312 | tf_op jit(solution)/shard_map/ppermute | solution.py:393
  87.6 6.8 %collective-permute-start.9 = (bf16[2,32,64,128]{3,2,1,0:T(8,128)(2,1)S(1)}, bf16[2,32,64,128]{3,2,1,0:T(8,128)(2,1)S(1)}, u32[]{:S(2)}, u32[]{:S(2)}) collective-permute-start(bf16[2,32,64,128]{3,2,1,0:T(8,128)(2,1)S(1)} %bitcast.22), channel_id=1, source_target_pairs={{0,16},{16,0},{32,48},{48,32},{64,80},{80,64},{96,112},{112,96},{1... | collective-permute-start | bytes 3145736 | tf_op jit(solution)/shard_map/ppermute | solution.py:398
  91.6 9.8 %collective-permute-start.8 = (bf16[1,32,64,128]{3,2,1,0:T(8,128)(2,1)S(1)}, bf16[1,32,64,128]{3,2,1,0:T(8,128)(2,1)S(1)}, u32[]{:S(2)}, u32[]{:S(2)}) collective-permute-start(bf16[1,32,64,128]{3,2,1,0:T(8,128)(2,1)S(1)} %slice_select_fusion), channel_id=1, source_target_pairs={{0,32},{1,33},{2,34},{3,35},{4,36},{5,37},{6,38},{7,39},{8,40},{9,... | collective-permute-start | bytes 1572872 | tf_op jit(solution)/shard_map/ppermute | solution.py:359
  92.5 8.9 %collective-permute-start.7 = (bf16[1,32,64,128]{3,2,1,0:T(8,128)(2,1)S(1)}, bf16[1,32,64,128]{3,2,1,0:T(8,128)(2,1)S(1)}, u32[]{:S(2)}, u32[]{:S(2)}) collective-permute-start(bf16[1,32,64,128]{3,2,1,0:T(8,128)(2,1)S(1)} %slice_select_fusion), channel_id=1, source_target_pairs={{0,96},{1,97},{2,98},{3,99},{4,100},{5,101},{6,102},{7,103},{8,104... | collective-permute-start | bytes 1572872 | tf_op jit(solution)/shard_map/ppermute | solution.py:359
  101.3 2.2 %collective-permute-start.10 = (bf16[1,32,64,128]{3,2,1,0:T(8,128)(2,1)S(1)}, bf16[1,32,64,128]{3,2,1,0:T(8,128)(2,1)S(1)}, u32[]{:S(2)}, u32[]{:S(2)}) collective-permute-start(bf16[1,32,64,128]{3,2,1,0:T(8,128)(2,1)S(1)} %collective-permute-done.7.rest_0_), channel_id=1, source_target_pairs={{0,16},{16,0},{32,48},{48,32},{64,80},{80,64},{96,112},{112,96},{1... | collective-permute-start | bytes 1572872 | tf_op jit(solution)/shard_map/ppermute | solution.py:410
  102.0 2.3 %collective-permute-start.11 = (bf16[1,32,64,128]{3,2,1,0:T(8,128)(2,1)S(1)}, bf16[1,32,64,128]{3,2,1,0:T(8,128)(2,1)S(1)}, u32[]{:S(2)}, u32[]{:S(2)}) collective-permute-start(bf16[1,32,64,128]{3,2,1,0:T(8,128)(2,1)S(1)} %collective-permute-done.8.rest_1_), channel_id=1, source_target_pairs={{0,16},{16,0},{32,48},{48,32},{64,80},{80,64},{96,112},{112,96},{1... | collective-permute-start | bytes 1572872 | tf_op jit(solution)/shard_map/ppermute | solution.py:410

commit v4 on v3

--- a/solution.py
+++ b/solution.py
@@ -40,13 +40,11 @@
 
 
 def forward_kernel(
-    g, fanout, blocks, core, rhs_hbm, inv_hbm, off_hbm, keep_hbm, send_hbm,
-    rhs, inv, off, acc, staged, w_inv, w_off, in_sems, out_sems,
+    g, fanout, blocks, which, rhs_hbm, inv_hbm, off_hbm, *rest
 ):
+    outs, (rhs, inv, off, acc, staged, w_inv, w_off, in_sems, out_sems) = rest[:-9], rest[-9:]
     leaves = rhs.shape[0]
-    _, heights, parents, block_rows, width = acc.shape
-    half = heights * block_rows
-    me = core[0]
+    parts, parents, block_rows, width = acc.shape
 
     def fetches(i):
         some = pl.ds(g * i, g)
@@ -68,9 +66,7 @@
         diagonal(w_off, slot, [off[j + h].reshape(fanout * width, width) for h in range(2)])
         x = jnp.concatenate(
             [
-                jnp.concatenate(
-                    [rhs[j + h, z, c] for c in (me, 1 - me) for z in range(heights)], axis=0
-                )
+                jnp.concatenate([rhs[j + h, which[n]] for n in range(parts)], axis=0)
                 for h in range(2)
             ],
             axis=1,
@@ -81,10 +77,9 @@
             for k in range(fanout):
                 p = blocks[(j + h) * fanout + k]
                 at = (h * fanout + k) * width
-                for c in range(CORES):
-                    for z in range(heights):
-                        row = c * half + z * block_rows
-                        acc[c, z, p] += part[row : row + block_rows, at : at + width]
+                for n in range(parts):
+                    row = n * block_rows
+                    acc[n, p] += part[row : row + block_rows, at : at + width]
 
     @pl.loop(0, leaves // g)
     def _(i):
@@ -94,44 +89,46 @@
             pair(i * g + u, (u // 2) % w_inv.shape[0])
 
     copies = []
-    for z in range(heights):
-        for c, out in ((1, send_hbm), (0, keep_hbm)):
-            staged[c, z] = acc[c, z].astype(BF16)
-            copies.append(pltpu.make_async_copy(staged.at[c, z], out.at[z], out_sems.at[c, z]))
-            copies[-1].start()
+    each = outs[0].shape[0]
+    for n in range(parts):
+        staged[n] = acc[n].astype(BF16)
+        copies.append(
+            pltpu.make_async_copy(staged.at[n], outs[n // each].at[n % each], out_sems.at[n])
+        )
+        copies[-1].start()
     for copy in copies:
         copy.wait()
 
 
-def forward(blocks, core, rhs, inv, off, parents):
-    leaves, heights, _, block_rows, width = rhs.shape
+def forward(blocks, which, rhs, inv, off, parents, each):
+    leaves, parts, block_rows, width = rhs.shape
     fanout = off.shape[1]
-    half = (heights, parents, block_rows, width)
+    one = (parents, block_rows, width)
     g, slots = F_G, F_S
     smem, hbm = pl.BlockSpec(memory_space=pltpu.SMEM), pl.BlockSpec(memory_space=pltpu.HBM)
     return pl.pallas_call(
         functools.partial(forward_kernel, g, fanout),
         in_specs=[smem, smem, hbm, hbm, hbm],
-        out_specs=[hbm, hbm],
+        out_specs=[hbm] * (parts // each),
         scratch_shapes=[
             pltpu.VMEM(rhs.shape, BF16),
             pltpu.VMEM(inv.shape, BF16),
             pltpu.VMEM(off.shape, BF16),
-            pltpu.VMEM((CORES,) + half, F32),
-            pltpu.VMEM((CORES,) + half, BF16),
+            pltpu.VMEM((parts,) + one, F32),
+            pltpu.VMEM((parts,) + one, BF16),
             pltpu.VMEM((slots, 2 * width, 2 * width), BF16),
             pltpu.VMEM((slots, 2 * fanout * width, 2 * width), BF16),
             pltpu.SemaphoreType.DMA((3, leaves // g)),
-            pltpu.SemaphoreType.DMA((CORES, heights)),
+            pltpu.SemaphoreType.DMA((parts,)),
         ],
-        out_shape=[jax.ShapeDtypeStruct(half, BF16)] * 2,
+        out_shape=[jax.ShapeDtypeStruct((each,) + one, BF16)] * (parts // each),
         compiler_params=params(32),
         name="forward",
         cost_estimate=cost(7_000_000_000, 19_000_000),
-    )(blocks, core, *in_hbm(rhs, inv, off))
-
-
-def fold_kernel(g, fanout, inv, off, after, out, w_inv):
+    )(blocks, which, *in_hbm(rhs, inv, off))
+
+
+def fold_kernel(g, fanout, inv, off, out, w_inv):
     width = inv.shape[-1]
 
     @pl.when(pl.program_id(0) == 0)
@@ -147,7 +144,7 @@
             out[i + h] = m[:, h * width : (h + 1) * width]
 
 
-def fold(inv, off, after):
+def fold(inv, off):
     leaves, fanout, width, _ = off.shape
     g = 8
     return pl.pallas_call(
@@ -156,7 +153,6 @@
         in_specs=[
             pl.BlockSpec((g, width, width), lambda s: (s, 0, 0)),
             pl.BlockSpec((g, fanout, width, width), lambda s: (s, 0, 0, 0)),
-            pl.BlockSpec(memory_space=pl.ANY),
         ],
         out_specs=pl.BlockSpec((g, fanout * width, width), lambda s: (s, 0, 0)),
         out_shape=jax.ShapeDtypeStruct((leaves, fanout * width, width), BF16),
@@ -164,10 +160,10 @@
         compiler_params=params(54),
         name="fold",
         cost_estimate=cost(4_000_000_000, 15_000_000),
-    )(inv, off, after)
-
-
-def leaf_kernel(g, rhs, inv, out, w_inv):
+    )(inv, off)
+
+
+def leaf_kernel(g, rhs, inv, after, out, w_inv):
     width = inv.shape[-1]
 
     @pl.when(pl.program_id(0) == 0)
@@ -184,7 +180,7 @@
             out[i + h] = z[:, h * width : (h + 1) * width]
 
 
-def leaf(rhs, inv):
+def leaf(rhs, inv, after):
     leaves, nrhs, width = rhs.shape
     g = 8
     return pl.pallas_call(
@@ -193,6 +189,7 @@
         in_specs=[
             pl.BlockSpec((g, nrhs, width), lambda s: (s, 0, 0)),
             pl.BlockSpec((g, width, width), lambda s: (s, 0, 0)),
+            pl.BlockSpec(memory_space=pl.ANY),
         ],
         out_specs=pl.BlockSpec((g, nrhs, width), lambda s: (s, 0, 0)),
         out_shape=jax.ShapeDtypeStruct(rhs.shape, BF16),
@@ -200,23 +197,32 @@
         compiler_params=params(54),
         name="leaf",
         cost_estimate=cost(6_000_000_000, 20_000_000),
-    )(rhs, inv)
-
-
-def parent_kernel(sources, targets, got, rhs, pieces, place, after, x_out, x_every):
+    )(rhs, inv, after)
+
+
+def parent_kernel(sources, targets, side, got, given, place, after, x_out, x_every):
     own, block_rows, width = x_out.shape
-    side = pieces.shape[0]
+    part = width // side
     total = got[0].astype(F32)
     for s in range(1, sources):
         total += got[s].astype(F32)
     for p in range(own):
-        rest = rhs[p].astype(F32) - total[p]
+        rest = given[p, :block_rows].astype(F32) - total[p]
         high = rest.astype(BF16)
         left = rest - high.astype(F32)
         mid = left.astype(BF16)
         low = (left - mid.astype(F32)).astype(BF16)
         w = jnp.concatenate(
-            [pieces[lax.rem(place[0] - t + side, side), p] for t in range(side)], axis=0
+            [
+                given[
+                    p,
+                    pl.ds(
+                        pl.multiple_of(block_rows + lax.rem(place[0] - t + side, side) * part, 16), part
+                    ),
+                ]
+                for t in range(side)
+            ],
+            axis=0,
         )
         y = (mm_t(low, w) + mm_t(mid, w)) + mm_t(high, w)
         x = mm(y.astype(BF16), w).astype(BF16)
@@ -225,11 +231,11 @@
             x_every[s, p] = x
 
 
-def parent(got, rhs, pieces, place, after, targets):
+def parent(got, given, side, place, after, targets):
     sources = got.shape[0]
     return pl.pallas_call(
-        functools.partial(parent_kernel, sources, targets),
-        in_specs=[pl.BlockSpec(memory_space=pltpu.VMEM)] * 3
+        functools.partial(parent_kernel, sources, targets, side),
+        in_specs=[pl.BlockSpec(memory_space=pltpu.VMEM)] * 2
         + [pl.BlockSpec(memory_space=pltpu.SMEM), pl.BlockSpec(memory_space=pl.ANY)],
         out_shape=[
             jax.ShapeDtypeStruct(got.shape[1:], BF16),
@@ -238,7 +244,7 @@
         compiler_params=params(16),
         name="parent",
         cost_estimate=cost(30_000_000, 4_500_000),
-    )(got, rhs, pieces, place, after)
+    )(got, given, place, after)
 
 
 def backward_kernel(g, fanout, n_xs, blocks, which, base_hbm, folded_hbm, *rest):
@@ -368,47 +374,63 @@
         ]
         return lax.all_to_all(a, both, 0, 0, axis_index_groups=groups, tiled=True)
 
-    by_core = (leaves, side, CORES, block_rows, width)
-
-    flat = blocks.reshape(-1)
-    across = lax.ppermute(par_inv, "row", swap)
-    keep, send = forward(flat, core.reshape(1), leaf_rhs.reshape(by_core), leaf_inv, leaf_off, parents)
-    across, send = lax.optimization_barrier((across, send))
-    low, high = jnp.where(core == 0, par_inv, across), jnp.where(core == 0, across, par_inv)
-    given = lax.ppermute(jnp.concatenate([par_rhs, low, high], axis=1), both, turn)
-    received = lax.ppermute(send, "row", swap)
-    chip = (keep.astype(F32) + received.astype(F32)).astype(BF16)
-    chip, given = lax.optimization_barrier((chip, given))
-    pair = given[:, block_rows:]
-    shifts = [pair] + [along(pair, step) for step in range(1, side)]
-    got = spread(chip.reshape(side * cols, own, block_rows, width), (0,), 1)
-    base = leaf(leaf_rhs, leaf_inv)
-    pieces = jnp.stack(shifts)
-    par_x, targets = parent(
-        got, given[:, :block_rows], pieces, u.reshape(1), base[0, :16], side // 2 * cols
-    )
-    near = spread(targets, (0, 1), 2).reshape(side // 2, parents, block_rows, width)
-    folded = fold(leaf_inv, leaf_off, par_x)
-    near, base, folded, x_out = lax.optimization_barrier(
-        (near, base, folded, lax.ppermute(par_x, both, turn))
-    )
-    base = base.reshape(leaves, rows, block_rows, width)
-
-    mine = jnp.where(u < 2, near[:1], near[1:])
-    near_other = lax.ppermute(near, "row", swap)
-    far = [along(mine, -1), along(mine, 1)]
+    by_block = (leaves, rows, block_rows, width)
 
     def places(us, other_us):
         return jnp.stack(
             [(a % side) * CORES + core for a in us] + [(a % side) * CORES + 1 - core for a in other_us]
         ).astype(jnp.int32)
 
-    first = places((u % 2, u % 2 + 2), (other_u % 2, other_u % 2 + 2))
-    second = places((u + 1, u + side - 1), (other_u + 1, other_u + side - 1))
-    half = backward(flat, first, base, folded, [near, near_other])
+    near_places = places((u % 2, u % 2 + 2), (other_u % 2, other_u % 2 + 2))
+    far_places = places((u + 1, u + side - 1), (other_u + 1, other_u + side - 1))
+
+    flat = blocks.reshape(-1)
+    across = lax.ppermute(par_inv, "row", swap)
+    keep_far, send_far, keep_near, send_near = forward(
+        flat,
+        jnp.concatenate([far_places, near_places]),
+        leaf_rhs.reshape(by_block),
+        leaf_inv,
+        leaf_off,
+        parents,
+        2,
+    )
+    across, send_far = lax.optimization_barrier((across, send_far))
+    low, high = jnp.where(core == 0, par_inv, across), jnp.where(core == 0, across, par_inv)
+    pair = jnp.concatenate([low, high], axis=1)
+    shifts = [pair] + [
+        lax.ppermute(pair, "row", [(r, (r + CORES * s) % rows) for r in range(rows)])
+        for s in range(1, side)
+    ]
+    far = [
+        (keep_far[n : n + 1].astype(F32) + lax.ppermute(send_far, "row", swap)[n : n + 1].astype(F32)).astype(BF16)
+        for n in range(2)
+    ]
+    received = lax.ppermute(send_near, "row", swap)
+    neighbours = along(far[0], 1).astype(F32) + along(far[1], -1).astype(F32)
+    here = jnp.arange(2, dtype=jnp.int32).reshape(2, 1, 1, 1) == u // 2
+    chip = keep_near.astype(F32) + received.astype(F32) + jnp.where(here, neighbours, 0.0)
+    chip = chip.astype(BF16)
+    chip, shifts = lax.optimization_barrier((chip, shifts))
+    got = spread(chip.reshape(side // 2 * cols, own, block_rows, width), (0, 1), 2)
+    folded = fold(leaf_inv, leaf_off)
+    given = lax.ppermute(jnp.concatenate([par_rhs] + shifts, axis=1), both, turn)
+    par_x, targets = parent(got, given, side, u.reshape(1), folded[0, :16], side // 2 * cols)
+    near = spread(targets, (0, 1), 2).reshape(side // 2, parents, block_rows, width)
+    base = leaf(leaf_rhs, leaf_inv, par_x)
+    near, base, folded, x_out = lax.optimization_barrier(
+        (near, base, folded, lax.ppermute(par_x, both, turn))
+    )
+    base = base.reshape(by_block)
+
+    mine = jnp.where(u < 2, near[:1], near[1:])
+    near_other = lax.ppermute(near, "row", swap)
+    far = [along(mine, -1), along(mine, 1)]
+
+    half = backward(flat, near_places, base, folded, [near, near_other])
     far, half = lax.optimization_barrier((far, half))
     far_other = [lax.ppermute(a, "row", swap) for a in far]
-    leaf_x = backward(flat, second, base, folded, far + far_other, half)
+    leaf_x = backward(flat, far_places, base, folded, far + far_other, half)
     return (leaf_x.reshape(leaf_rhs.shape), x_out)
 
 

time: 113 us -> 110 us (0.973)
  waiting for transfers between devices: 25.2 us -> 21.6 us
  starting transfers between devices: 32.7 us -> 34.4 us
  Pallas kernels: 46.8 us -> 45.5 us
    ppermute x5 -> x4, waiting for transfers between devices: 9.71 us -> 3.01 us  [along(): lax.ppermute(a, both, [(device(u, c, v, y), device(u + step, c, v, y)) fo...]
    ppermute x2 -> x6, starting transfers between devices: 0.77 us -> 6.59 us  [the longest x3 5.33 us: on_device(): lax.ppermute(pair, 'row', [(r, (r + CORES * s) % rows) for r in range(row...]
    all_to_all x2, waiting for transfers between devices: 9.57 us -> 13.2 us  [spread(): return lax.all_to_all(a, both, 0, 0, axis_index_groups=groups, tiled=True)]
    ppermute x1, starting transfers between devices: 3.92 us -> 1.17 us  [on_device(): near_other = lax.ppermute(near, 'row', swap)]
    ppermute x5 -> x4, starting transfers between devices: 8.12 us -> 5.49 us  [along(): lax.ppermute(a, both, [(device(u, c, v, y), device(u + step, c, v, y)) fo...]
    ppermute x2 -> x6, waiting for transfers between devices: 3.76 us -> 3.12 us  [the longest x1 2.49 us: on_device(): lax.ppermute(send_far, 'row', swap)[n:n + 1].astype(F32)]
    convert_element_type x1 -> x2, other arithmetic: 3.87 us -> 4.32 us  [the longest x1 2.72 us: on_device(): chip = chip.astype(BF16)]
  transfers between devices with their start and end apart: 14 -> 17, of which waited for: 6 -> 8; matrix products, arithmetic and copies ran while one was open for 5% -> 6% of each run, Pallas kernels for 34% -> 34%
where the time goes in v4:
time: 110 us; the launch traced here: 109 us
  Pallas kernels  45.5 us (41%)
  starting transfers between devices  34.4 us (31%)
  waiting for transfers between devices  21.6 us (20%)
  other arithmetic  4.71 us (4%)
  local copies, waits for them, and re-layouts  2.32 us (2%)
    all_to_all x2, starting transfers between devices, spread(): return lax.all_to_all(a, both, 0, 0, axis_index_groups=groups, tiled=True)  18.1 us
    pallas_call x2, Pallas kernels, backward(): pl.pallas_call(functools.partial(backward_kernel, g, fanout, len(xs)), in...  13.6 us
    all_to_all x2, waiting for transfers between devices, spread(): return lax.all_to_all(a, both, 0, 0, axis_index_groups=groups, tiled=True)  13.2 us
    pallas_call x1, Pallas kernels, forward(): pl.pallas_call(functools.partial(forward_kernel, g, fanout), in_specs=[sm...  13.1 us
    pallas_call x1, Pallas kernels, leaf(): pl.pallas_call(functools.partial(leaf_kernel, g), grid=(leaves // g,), in...  9.76 us
    pallas_call x1, Pallas kernels, fold(): pl.pallas_call(functools.partial(fold_kernel, g, fanout), grid=(leaves //...  7.4 us
    ppermute x4, starting transfers between devices, along(): lax.ppermute(a, both, [(device(u, c, v, y), device(u + step, c, v, y)) fo...  5.49 us
    ppermute x3, starting transfers between devices, on_device(): lax.ppermute(pair, 'row', [(r, (r + CORES * s) % rows) for r in range(row...  5.33 us
  transfers between devices with their start and end apart: 17, of which 8 were waited for; matrix products, arithmetic and copies ran while one was open for 6% of the time, Pallas kernels for 34%

profile of v4, /device:TPU:1, one launch (start us, length us, event | category | flops | bytes accessed | tf_op | source)
XLA Modules:
  0.0 109.2 jit_solution(8500056022898336702)
XLA Ops:
  0.6 1.5 %collective-permute-start.1 = (bf16[2,16,128]{2,1,0:T(8,128)(2,1)}, bf16[2,16,128]{2,1,0:T(8,128)(2,1)S(1)}, u32[]{:S(2)}, u32[]{:S(2)}) collective-permute-start(bf16[2,16,128]{2,1,0:T(8,128)(2,1)} %param.11), channel_id=1, source_target_pairs={{0,16},{16,0},{32,48},{48,32},{64,80},{80,64},{96,112},{112,96},{1... | collective-permute-start | bytes 24584 | tf_op jit(solution)/shard_map/ppermute | solution.py:388
  2.1 0.8 copy.9
  2.9 0.1 reshape.31.blocks
  3.0 0.1 concatenate.10.which
  3.1 13.1 %forward.1 = (bf16[2,32,64,128]{3,2,1,0:T(8,128)(2,1)S(1)}, bf16[2,32,64,128]{3,2,1,0:T(8,128)(2,1)}, bf16[2,32,64,128]{3,2,1,0:T(8,128)(2,1)S(1)}, bf16[2,32,64,128]{3,2,1,0:T(8,128)(2,1)S(1)}) custom-call(s32[144]{0:T(256)S(1)} %reshape.31.blocks, s32[8]{0:T(128)S(1)} %concatenate.10.which, bf16[48,8,64,128]{3,2,1,0:T(8,128)(2,1)} %bitcast.24, ...), custom_call_target="tpu_custom_call" | custom-call | flops 7000000000 | bytes 19000000 | tf_op jit(solution)/shard_map/forward/pallas_call | solution.py:109
  16.3 0.0 copy-start.1
  16.3 0.0 copy-start.2
  16.3 0.3 collective-permute-start.2
  16.6 0.3 collective-permute-start
  16.9 2.5 %collective-permute-done.2 = bf16[2,32,64,128]{3,2,1,0:T(8,128)(2,1)} collective-permute-done((bf16[2,32,64,128]{3,2,1,0:T(8,128)(2,1)}, bf16[2,32,64,128]{3,2,1,0:T(8,128)(2,1)}, u32[]{:S(2)}, u32[]{:S(2)}) %collective-permute-start.2) | collective-permute-done | bytes 1048608 | tf_op jit(solution)/shard_map/ppermute | solution.py:406
  19.4 1.6 %add_convert_fusion.2 = (bf16[1,32,64,128]{3,2,1,0:T(8,128)(2,1)S(1)}, bf16[1,32,64,128]{3,2,1,0:T(8,128)(2,1)S(1)}) fusion(bf16[2,32,64,128]{3,2,1,0:T(8,128)(2,1)} %collective-permute-done.2, bf16[2,32,64,128]{3,2,1,0:T(8,128)(2,1)S(1)} %get-tuple-element.24), kind=kLoop, calls=%fused_computation.3 | loop fusion | flops 2097152 | bytes 3145728 | tf_op jit(solution)/shard_map/convert_element_type | solution.py:406
  21.0 1.4 %collective-permute-start.3 = (bf16[1,32,64,128]{3,2,1,0:T(8,128)(2,1)S(1)}, bf16[1,32,64,128]{3,2,1,0:T(8,128)(2,1)S(1)}, u32[]{:S(2)}, u32[]{:S(2)}) collective-permute-start(bf16[1,32,64,128]{3,2,1,0:T(8,128)(2,1)S(1)} %get-tuple-element.42), channel_id=1, source_target_pairs={{0,32},{1,33},{2,34},{3,35},{4,36},{5,37},{6,38},{7,39},{8,40},{9,... | collective-permute-start | bytes 1572872 | tf_op jit(solution)/shard_map/ppermute | solution.py:365
  22.3 1.4 %collective-permute-start.4 = (bf16[1,32,64,128]{3,2,1,0:T(8,128)(2,1)S(1)}, bf16[1,32,64,128]{3,2,1,0:T(8,128)(2,1)S(1)}, u32[]{:S(2)}, u32[]{:S(2)}) collective-permute-start(bf16[1,32,64,128]{3,2,1,0:T(8,128)(2,1)S(1)} %get-tuple-element.43), channel_id=1, source_target_pairs={{0,96},{1,97},{2,98},{3,99},{4,100},{5,101},{6,102},{7,103},{8,104... | collective-permute-start | bytes 1572872 | tf_op jit(solution)/shard_map/ppermute | solution.py:365
  23.8 3.9 %collective-permute-start.7 = (bf16[2,32,128]{2,1,0:T(8,128)(2,1)S(1)}, bf16[2,32,128]{2,1,0:T(8,128)(2,1)S(1)}, u32[]{:S(2)}, u32[]{:S(2)}) collective-permute-start(bf16[2,32,128]{2,1,0:T(8,128)(2,1)S(1)} %pad_maximum_fusion), channel_id=1, source_target_pairs={{0,96},{16,112},{32,0},{48,16},{64,32},{80,48},{96,64},{112,80},{1... | collective-permute-start | bytes 49160 | tf_op jit(solution)/shard_map/ppermute | solution.py:402
  27.7 2.9 %collective-permute-done.3 = bf16[1,32,64,128]{3,2,1,0:T(8,128)(2,1)S(1)} collective-permute-done((bf16[1,32,64,128]{3,2,1,0:T(8,128)(2,1)S(1)}, bf16[1,32,64,128]{3,2,1,0:T(8,128)(2,1)S(1)}, u32[]{:S(2)}, u32[]{:S(2)}) %collective-permute-start.3) | collective-permute-done | bytes 524320 | tf_op jit(solution)/shard_map/ppermute | solution.py:365
  30.6 1.4 %collective-permute-start.5 = (bf16[2,32,128]{2,1,0:T(8,128)(2,1)S(1)}, bf16[2,32,128]{2,1,0:T(8,128)(2,1)S(1)}, u32[]{:S(2)}, u32[]{:S(2)}) collective-permute-start(bf16[2,32,128]{2,1,0:T(8,128)(2,1)S(1)} %pad_maximum_fusion), channel_id=1, source_target_pairs={{0,32},{16,48},{32,64},{48,80},{64,96},{80,112},{96,0},{112,16},{1... | collective-permute-start | bytes 49160 | tf_op jit(solution)/shard_map/ppermute | solution.py:402
  32.0 0.0 collective-permute-done.4
  32.0 0.2 add_bitcast_fusion
  32.2 0.0 collective-permute-done
  32.2 2.7 %add_convert_fusion = bf16[2,32,64,128]{3,2,1,0:T(8,128)(2,1)} fusion(bf16[2,32,64,128]{3,2,1,0:T(8,128)(2,1)} %collective-permute-done, bf16[2,32,64,128]{3,2,1,0:T(8,128)(2,1)S(1)} %get-tuple-element.22, f32[32,64,128]{2,1,0:T(8,128)S(1)} %add_bitcast_fusion, pred[2]{0:T(512)(128)(4,1)S(1)} %iota_compare_fusion), kind=kLoop, calls=%fused_computation | loop fusion | flops 3145728 | bytes 4194306 | tf_op jit(solution)/shard_map/convert_element_type | solution.py:413
  34.9 0.6 collective-permute-done.5
  35.5 8.5 %all-to-all-start = ((bf16[32,2,64,128]{3,2,1,0:T(8,128)(2,1)}), bf16[32,2,64,128]{3,2,1,0:T(8,128)(2,1)S(1)}, u32[]{:S(2)}, u32[]{:S(2)}) async-start(bf16[32,2,64,128]{3,2,1,0:T(8,128)(2,1)} %bitcast.10), calls=%async_computation | async-start | bytes 2097152 | tf_op jit(solution)/shard_map/all_to_all | solution.py:375
  44.1 7.4 %fold.1.folded_hbm = bf16[48,384,128]{2,1,0:T(8,128)(2,1)} custom-call(bf16[48,128,128]{2,1,0:T(8,128)(2,1)} %inv.3, bf16[48,3,128,128]{3,2,1,0:T(8,128)(2,1)} %off.1), custom_call_target="tpu_custom_call" | custom-call | flops 4000000000 | bytes 15000000 | tf_op jit(solution)/shard_map/fold/pallas_call | solution.py:150
  51.5 0.7 collective-permute-start.8
  52.2 0.7 slice_bitcast_fusion.after
  52.9 0.0 collective-permute-done.8.given
  52.9 6.4 %all-to-all-done.got = bf16[32,2,64,128]{3,2,1,0:T(8,128)(2,1)S(1)} async-done(((bf16[32,2,64,128]{3,2,1,0:T(8,128)(2,1)}), bf16[32,2,64,128]{3,2,1,0:T(8,128)(2,1)S(1)}, u32[]{:S(2)}, u32[]{:S(2)}) %all-to-all-start) | async-done | bytes 1048608 | tf_op jit(solution)/shard_map/all_to_all | solution.py:375
  59.3 1.6 %parent.1 = (bf16[2,64,128]{2,1,0:T(8,128)(2,1)S(1)}, bf16[32,2,64,128]{3,2,1,0:T(8,128)(2,1)}) custom-call(bf16[32,2,64,128]{3,2,1,0:T(8,128)(2,1)S(1)} %all-to-all-done.got, bf16[2,192,128]{2,1,0:T(8,128)(2,1)S(1)} %collective-permute-done.8.given, s32[1]{0:T(128)} %bitcast.11.place, bf16[16,128]{1,0:T(8,128)(2,1)S(1)} %slice_bitcast_fusion.after), custom_call_target="tpu_custom_call" | custom-call | flops 30000000 | bytes 4500000 | tf_op jit(solution)/shard_map/parent/pallas_call | solution.py:236
  60.9 9.5 %all-to-all-start.1 = ((bf16[32,2,64,128]{3,2,1,0:T(8,128)(2,1)}), bf16[32,2,64,128]{3,2,1,0:T(8,128)(2,1)S(1)}, u32[]{:S(2)}, u32[]{:S(2)}) async-start(bf16[32,2,64,128]{3,2,1,0:T(8,128)(2,1)} %get-tuple-element.33), calls=%async_computation.1 | async-start | bytes 2097152 | tf_op jit(solution)/shard_map/all_to_all | solution.py:375
  70.4 0.7 collective-permute-start.9
  71.1 9.8 %leaf.1 = bf16[48,512,128]{2,1,0:T(8,128)(2,1)} custom-call(bf16[48,512,128]{2,1,0:T(8,128)(2,1)} %rhs.1, bf16[48,128,128]{2,1,0:T(8,128)(2,1)} %inv.3, bf16[2,64,128]{2,1,0:T(8,128)(2,1)} %copy-done), custom_call_target="tpu_custom_call" | custom-call | flops 6000000000 | bytes 20000000 | tf_op jit(solution)/shard_map/leaf/pallas_call | solution.py:186
  80.9 6.8 %all-to-all-done.1 = bf16[32,2,64,128]{3,2,1,0:T(8,128)(2,1)S(1)} async-done(((bf16[32,2,64,128]{3,2,1,0:T(8,128)(2,1)}), bf16[32,2,64,128]{3,2,1,0:T(8,128)(2,1)S(1)}, u32[]{:S(2)}, u32[]{:S(2)}) %all-to-all-start.1) | async-done | bytes 1048608 | tf_op jit(solution)/shard_map/all_to_all | solution.py:375
  87.7 1.2 %collective-permute-start.12 = (bf16[2,32,64,128]{3,2,1,0:T(8,128)(2,1)S(1)}, bf16[2,32,64,128]{3,2,1,0:T(8,128)(2,1)S(1)}, u32[]{:S(2)}, u32[]{:S(2)}) collective-permute-start(bf16[2,32,64,128]{3,2,1,0:T(8,128)(2,1)S(1)} %bitcast.18), channel_id=1, source_target_pairs={{0,16},{16,0},{32,48},{48,32},{64,80},{80,64},{96,112},{112,96},{1... | collective-permute-start | bytes 3145736 | tf_op jit(solution)/shard_map/ppermute | solution.py:427
  88.9 0.1 slice_select_fusion
  88.9 0.5 collective-permute-start.11
  89.4 2.3 %collective-permute-start.10 = (bf16[1,32,64,128]{3,2,1,0:T(8,128)(2,1)S(1)}, bf16[1,32,64,128]{3,2,1,0:T(8,128)(2,1)S(1)}, u32[]{:S(2)}, u32[]{:S(2)}) collective-permute-start(bf16[1,32,64,128]{3,2,1,0:T(8,128)(2,1)S(1)} %slice_select_fusion), channel_id=1, source_target_pairs={{0,96},{1,97},{2,98},{3,99},{4,100},{5,101},{6,102},{7,103},{8,104... | collective-permute-start | bytes 1572872 | tf_op jit(solution)/shard_map/ppermute | solution.py:365
  91.7 0.1 pad_add_fusion.1.which
  91.7 0.0 collective-permute-done.12.rest_1_
  91.7 6.7 %backward.2.rest_4_ = bf16[48,8,64,128]{3,2,1,0:T(8,128)(2,1)} custom-call(s32[144]{0:T(256)S(1)} %reshape.31.blocks, s32[4]{0:T(128)S(1)} %pad_add_fusion.1.which, bf16[48,8,64,128]{3,2,1,0:T(8,128)(2,1)} %bitcast.21, bf16[48,384,128]{2,1,0:T(8,128)(2,1)} %fold.1.folded_hbm, bf16[2,32,64,128]{3,2,1,0:T(8,128)(2,1)S(1)} %bitcast.20, ...), custom_call_target="tpu_custom_call" | custom-call | flops 5000000000 | bytes 13000000 | tf_op jit(solution)/shard_map/backward/pallas_call | solution.py:318
  98.4 0.1 collective-permute-done.11.rest_1_
  98.5 0.0 collective-permute-done.10.rest_0_
  98.5 0.9 collective-permute-start.13
  99.4 0.0 collective-permute-start.14
  99.4 0.1 pad_add_fusion.which
  99.5 1.5 %collective-permute-done.13.rest_2_ = bf16[1,32,64,128]{3,2,1,0:T(8,128)(2,1)S(1)} collective-permute-done((bf16[1,32,64,128]{3,2,1,0:T(8,128)(2,1)S(1)}, bf16[1,32,64,128]{3,2,1,0:T(8,128)(2,1)S(1)}, u32[]{:S(2)}, u32[]{:S(2)}) %collective-permute-start.13) | collective-permute-done | bytes 524320 | tf_op jit(solution)/shard_map/ppermute | solution.py:432
  101.0 0.7 collective-permute-done.14.rest_3_
  101.7 6.9 %backward.3 = bf16[48,8,64,128]{3,2,1,0:T(8,128)(2,1)} custom-call(s32[144]{0:T(256)S(1)} %reshape.31.blocks, s32[4]{0:T(128)S(1)} %pad_add_fusion.which, bf16[48,8,64,128]{3,2,1,0:T(8,128)(2,1)} %bitcast.22, bf16[48,384,128]{2,1,0:T(8,128)(2,1)} %fold.1.folded_hbm, ...), custom_call_target="tpu_custom_call", output_to_operand_aliasing={{}: (8, {})} | custom-call | flops 5000000000 | bytes 13000000 | tf_op jit(solution)/shard_map/backward/pallas_call | solution.py:318
  108.6 0.6 copy.16
  (17 shorter events, 0.1 us)
Async XLA Ops:
  0.6 15.7 %collective-permute-start.1 = (bf16[2,16,128]{2,1,0:T(8,128)(2,1)}, bf16[2,16,128]{2,1,0:T(8,128)(2,1)S(1)}, u32[]{:S(2)}, u32[]{:S(2)}) collective-permute-start(bf16[2,16,128]{2,1,0:T(8,128)(2,1)} %param.11), channel_id=1, source_target_pairs={{0,16},{16,0},{32,48},{48,32},{64,80},{80,64},{96,112},{112,96},{1... | collective-permute-start | bytes 24584 | tf_op jit(solution)/shard_map/ppermute | solution.py:388
  16.3 7.5 %copy-start.1 = (bf16[2,64,128]{2,1,0:T(8,128)(2,1)S(1)}, bf16[2,64,128]{2,1,0:T(8,128)(2,1)}, u32[]{:S(2)}) copy-start(bf16[2,64,128]{2,1,0:T(8,128)(2,1)} %param.10) | copy-start | bytes 98308
  16.3 7.5 %copy-start.2 = (bf16[2,16,128]{2,1,0:T(8,128)(2,1)S(1)}, bf16[2,16,128]{2,1,0:T(8,128)(2,1)}, u32[]{:S(2)}) copy-start(bf16[2,16,128]{2,1,0:T(8,128)(2,1)} %param.11) | copy-start | bytes 24580
  16.3 3.1 %collective-permute-start.2 = (bf16[2,32,64,128]{3,2,1,0:T(8,128)(2,1)}, bf16[2,32,64,128]{3,2,1,0:T(8,128)(2,1)}, u32[]{:S(2)}, u32[]{:S(2)}) collective-permute-start(bf16[2,32,64,128]{3,2,1,0:T(8,128)(2,1)} %get-tuple-element.26), channel_id=1, source_target_pairs={{0,16},{16,0},{32,48},{48,32},{64,80},{80,64},{96,112},{112,96},{1... | collective-permute-start | bytes 3145736 | tf_op jit(solution)/shard_map/ppermute | solution.py:406
  16.6 15.6 %collective-permute-start = (bf16[2,32,64,128]{3,2,1,0:T(8,128)(2,1)S(1)}, bf16[2,32,64,128]{3,2,1,0:T(8,128)(2,1)}, u32[]{:S(2)}, u32[]{:S(2)}) collective-permute-start(bf16[2,32,64,128]{3,2,1,0:T(8,128)(2,1)S(1)} %get-tuple-element.23), channel_id=1, source_target_pairs={{0,16},{16,0},{32,48},{48,32},{64,80},{80,64},{96,112},{112,96},{1... | collective-permute-start | bytes 3145736 | tf_op jit(solution)/shard_map/ppermute | solution.py:409
  21.0 9.6 %collective-permute-start.3 = (bf16[1,32,64,128]{3,2,1,0:T(8,128)(2,1)S(1)}, bf16[1,32,64,128]{3,2,1,0:T(8,128)(2,1)S(1)}, u32[]{:S(2)}, u32[]{:S(2)}) collective-permute-start(bf16[1,32,64,128]{3,2,1,0:T(8,128)(2,1)S(1)} %get-tuple-element.42), channel_id=1, source_target_pairs={{0,32},{1,33},{2,34},{3,35},{4,36},{5,37},{6,38},{7,39},{8,40},{9,... | collective-permute-start | bytes 1572872 | tf_op jit(solution)/shard_map/ppermute | solution.py:365
  22.3 9.7 %collective-permute-start.4 = (bf16[1,32,64,128]{3,2,1,0:T(8,128)(2,1)S(1)}, bf16[1,32,64,128]{3,2,1,0:T(8,128)(2,1)S(1)}, u32[]{:S(2)}, u32[]{:S(2)}) collective-permute-start(bf16[1,32,64,128]{3,2,1,0:T(8,128)(2,1)S(1)} %get-tuple-element.43), channel_id=1, source_target_pairs={{0,96},{1,97},{2,98},{3,99},{4,100},{5,101},{6,102},{7,103},{8,104... | collective-permute-start | bytes 1572872 | tf_op jit(solution)/shard_map/ppermute | solution.py:365
  23.8 11.2 %collective-permute-start.7 = (bf16[2,32,128]{2,1,0:T(8,128)(2,1)S(1)}, bf16[2,32,128]{2,1,0:T(8,128)(2,1)S(1)}, u32[]{:S(2)}, u32[]{:S(2)}) collective-permute-start(bf16[2,32,128]{2,1,0:T(8,128)(2,1)S(1)} %pad_maximum_fusion), channel_id=1, source_target_pairs={{0,96},{16,112},{32,0},{48,16},{64,32},{80,48},{96,64},{112,80},{1... | collective-permute-start | bytes 49160 | tf_op jit(solution)/shard_map/ppermute | solution.py:402
  27.7 7.2 %collective-permute-start.6 = (bf16[2,32,128]{2,1,0:T(8,128)(2,1)S(1)}, bf16[2,32,128]{2,1,0:T(8,128)(2,1)S(1)}, u32[]{:S(2)}, u32[]{:S(2)}) collective-permute-start(bf16[2,32,128]{2,1,0:T(8,128)(2,1)S(1)} %pad_maximum_fusion), channel_id=1, source_target_pairs={{0,64},{16,80},{32,96},{48,112},{64,0},{80,16},{96,32},{112,48},{1... | collective-permute-start | bytes 49160 | tf_op jit(solution)/shard_map/ppermute | solution.py:402
  30.6 5.0 %collective-permute-start.5 = (bf16[2,32,128]{2,1,0:T(8,128)(2,1)S(1)}, bf16[2,32,128]{2,1,0:T(8,128)(2,1)S(1)}, u32[]{:S(2)}, u32[]{:S(2)}) collective-permute-start(bf16[2,32,128]{2,1,0:T(8,128)(2,1)S(1)} %pad_maximum_fusion), channel_id=1, source_target_pairs={{0,32},{16,48},{32,64},{48,80},{64,96},{80,112},{96,0},{112,16},{1... | collective-permute-start | bytes 49160 | tf_op jit(solution)/shard_map/ppermute | solution.py:402
  35.5 23.8 %all-to-all-start = ((bf16[32,2,64,128]{3,2,1,0:T(8,128)(2,1)}), bf16[32,2,64,128]{3,2,1,0:T(8,128)(2,1)S(1)}, u32[]{:S(2)}, u32[]{:S(2)}) async-start(bf16[32,2,64,128]{3,2,1,0:T(8,128)(2,1)} %bitcast.10), calls=%async_computation | async-start | bytes 2097152 | tf_op jit(solution)/shard_map/all_to_all | solution.py:375
  51.5 1.4 %collective-permute-start.8 = (bf16[2,192,128]{2,1,0:T(8,128)(2,1)S(1)}, bf16[2,192,128]{2,1,0:T(8,128)(2,1)S(1)}, u32[]{:S(2)}, u32[]{:S(2)}) collective-permute-start(bf16[2,192,128]{2,1,0:T(8,128)(2,1)S(1)} %constant_dynamic-update-slice_fusion), channel_id=1, source_target_pairs={{0,0},{1,1},{2,2},{3,3},{4,4},{5,5},{6,6},{7,7},{8,8},{9,9},{10,10... | collective-permute-start | bytes 294920 | tf_op jit(solution)/shard_map/ppermute | solution.py:417
  60.9 10.2 %copy-start = (bf16[2,64,128]{2,1,0:T(8,128)(2,1)}, bf16[2,64,128]{2,1,0:T(8,128)(2,1)S(1)}, u32[]{:S(2)}) copy-start(bf16[2,64,128]{2,1,0:T(8,128)(2,1)S(1)} %get-tuple-element.34.after) | copy-start | bytes 98308
  60.9 26.8 %all-to-all-start.1 = ((bf16[32,2,64,128]{3,2,1,0:T(8,128)(2,1)}), bf16[32,2,64,128]{3,2,1,0:T(8,128)(2,1)S(1)}, u32[]{:S(2)}, u32[]{:S(2)}) async-start(bf16[32,2,64,128]{3,2,1,0:T(8,128)(2,1)} %get-tuple-element.33), calls=%async_computation.1 | async-start | bytes 2097152 | tf_op jit(solution)/shard_map/all_to_all | solution.py:375
  70.4 10.4 %collective-permute-start.9 = (bf16[2,64,128]{2,1,0:T(8,128)(2,1)S(1)}, bf16[2,64,128]{2,1,0:T(8,128)(2,1)S(1)}, u32[]{:S(2)}, u32[]{:S(2)}) collective-permute-start(bf16[2,64,128]{2,1,0:T(8,128)(2,1)S(1)} %get-tuple-element.34.after), channel_id=1, source_target_pairs={{0,0},{1,1},{2,2},{3,3},{4,4},{5,5},{6,6},{7,7},{8,8},{9,9},{10,10... | collective-permute-start | bytes 98312 | tf_op jit(solution)/shard_map/ppermute | solution.py:422
  87.7 4.1 %collective-permute-start.12 = (bf16[2,32,64,128]{3,2,1,0:T(8,128)(2,1)S(1)}, bf16[2,32,64,128]{3,2,1,0:T(8,128)(2,1)S(1)}, u32[]{:S(2)}, u32[]{:S(2)}) collective-permute-start(bf16[2,32,64,128]{3,2,1,0:T(8,128)(2,1)S(1)} %bitcast.18), channel_id=1, source_target_pairs={{0,16},{16,0},{32,48},{48,32},{64,80},{80,64},{96,112},{112,96},{1... | collective-permute-start | bytes 3145736 | tf_op jit(solution)/shard_map/ppermute | solution.py:427
  88.9 9.6 %collective-permute-start.11 = (bf16[1,32,64,128]{3,2,1,0:T(8,128)(2,1)S(1)}, bf16[1,32,64,128]{3,2,1,0:T(8,128)(2,1)S(1)}, u32[]{:S(2)}, u32[]{:S(2)}) collective-permute-start(bf16[1,32,64,128]{3,2,1,0:T(8,128)(2,1)S(1)} %slice_select_fusion), channel_id=1, source_target_pairs={{0,32},{1,33},{2,34},{3,35},{4,36},{5,37},{6,38},{7,39},{8,40},{9,... | collective-permute-start | bytes 1572872 | tf_op jit(solution)/shard_map/ppermute | solution.py:365
  89.4 9.1 %collective-permute-start.10 = (bf16[1,32,64,128]{3,2,1,0:T(8,128)(2,1)S(1)}, bf16[1,32,64,128]{3,2,1,0:T(8,128)(2,1)S(1)}, u32[]{:S(2)}, u32[]{:S(2)}) collective-permute-start(bf16[1,32,64,128]{3,2,1,0:T(8,128)(2,1)S(1)} %slice_select_fusion), channel_id=1, source_target_pairs={{0,96},{1,97},{2,98},{3,99},{4,100},{5,101},{6,102},{7,103},{8,104... | collective-permute-start | bytes 1572872 | tf_op jit(solution)/shard_map/ppermute | solution.py:365
  98.5 2.4 %collective-permute-start.13 = (bf16[1,32,64,128]{3,2,1,0:T(8,128)(2,1)S(1)}, bf16[1,32,64,128]{3,2,1,0:T(8,128)(2,1)S(1)}, u32[]{:S(2)}, u32[]{:S(2)}) collective-permute-start(bf16[1,32,64,128]{3,2,1,0:T(8,128)(2,1)S(1)} %collective-permute-done.10.rest_0_), channel_id=1, source_target_pairs={{0,16},{16,0},{32,48},{48,32},{64,80},{80,64},{96,112},{112,96},{1... | collective-permute-start | bytes 1572872 | tf_op jit(solution)/shard_map/ppermute | solution.py:432
  99.4 2.3 %collective-permute-start.14 = (bf16[1,32,64,128]{3,2,1,0:T(8,128)(2,1)S(1)}, bf16[1,32,64,128]{3,2,1,0:T(8,128)(2,1)S(1)}, u32[]{:S(2)}, u32[]{:S(2)}) collective-permute-start(bf16[1,32,64,128]{3,2,1,0:T(8,128)(2,1)S(1)} %collective-permute-done.11.rest_1_), channel_id=1, source_target_pairs={{0,16},{16,0},{32,48},{48,32},{64,80},{80,64},{96,112},{112,96},{1... | collective-permute-start | bytes 1572872 | tf_op jit(solution)/shard_map/ppermute | solution.py:432

commit v5 on v4

--- a/solution.py
+++ b/solution.py
@@ -128,7 +128,7 @@
     )(blocks, which, *in_hbm(rhs, inv, off))
 
 
-def fold_kernel(g, fanout, inv, off, out, w_inv):
+def fold_kernel(g, fanout, inv, off, after, out, w_inv):
     width = inv.shape[-1]
 
     @pl.when(pl.program_id(0) == 0)
@@ -144,7 +144,7 @@
             out[i + h] = m[:, h * width : (h + 1) * width]
 
 
-def fold(inv, off):
+def fold(inv, off, after):
     leaves, fanout, width, _ = off.shape
     g = 8
     return pl.pallas_call(
@@ -153,6 +153,7 @@
         in_specs=[
             pl.BlockSpec((g, width, width), lambda s: (s, 0, 0)),
             pl.BlockSpec((g, fanout, width, width), lambda s: (s, 0, 0, 0)),
+            pl.BlockSpec(memory_space=pl.ANY),
         ],
         out_specs=pl.BlockSpec((g, fanout * width, width), lambda s: (s, 0, 0)),
         out_shape=jax.ShapeDtypeStruct((leaves, fanout * width, width), BF16),
@@ -160,10 +161,10 @@
         compiler_params=params(54),
         name="fold",
         cost_estimate=cost(4_000_000_000, 15_000_000),
-    )(inv, off)
-
-
-def leaf_kernel(g, rhs, inv, after, out, w_inv):
+    )(inv, off, after)
+
+
+def leaf_kernel(g, rhs, inv, out, w_inv):
     width = inv.shape[-1]
 
     @pl.when(pl.program_id(0) == 0)
@@ -180,7 +181,7 @@
             out[i + h] = z[:, h * width : (h + 1) * width]
 
 
-def leaf(rhs, inv, after):
+def leaf(rhs, inv):
     leaves, nrhs, width = rhs.shape
     g = 8
     return pl.pallas_call(
@@ -189,7 +190,6 @@
         in_specs=[
             pl.BlockSpec((g, nrhs, width), lambda s: (s, 0, 0)),
             pl.BlockSpec((g, width, width), lambda s: (s, 0, 0)),
-            pl.BlockSpec(memory_space=pl.ANY),
         ],
         out_specs=pl.BlockSpec((g, nrhs, width), lambda s: (s, 0, 0)),
         out_shape=jax.ShapeDtypeStruct(rhs.shape, BF16),
@@ -197,7 +197,7 @@
         compiler_params=params(54),
         name="leaf",
         cost_estimate=cost(6_000_000_000, 20_000_000),
-    )(rhs, inv, after)
+    )(rhs, inv)
 
 
 def parent_kernel(sources, targets, side, got, given, place, after, x_out, x_every):
@@ -408,16 +408,23 @@
     ]
     received = lax.ppermute(send_near, "row", swap)
     neighbours = along(far[0], 1).astype(F32) + along(far[1], -1).astype(F32)
-    here = jnp.arange(2, dtype=jnp.int32).reshape(2, 1, 1, 1) == u // 2
-    chip = keep_near.astype(F32) + received.astype(F32) + jnp.where(here, neighbours, 0.0)
-    chip = chip.astype(BF16)
+    chip = jnp.concatenate(
+        [
+            (
+                keep_near[n : n + 1].astype(F32)
+                + received[n : n + 1].astype(F32)
+                + jnp.where(u // 2 == n, neighbours, 0.0)
+            ).astype(BF16)
+            for n in range(2)
+        ]
+    )
     chip, shifts = lax.optimization_barrier((chip, shifts))
     got = spread(chip.reshape(side // 2 * cols, own, block_rows, width), (0, 1), 2)
-    folded = fold(leaf_inv, leaf_off)
+    base = leaf(leaf_rhs, leaf_inv)
     given = lax.ppermute(jnp.concatenate([par_rhs] + shifts, axis=1), both, turn)
-    par_x, targets = parent(got, given, side, u.reshape(1), folded[0, :16], side // 2 * cols)
+    par_x, targets = parent(got, given, side, u.reshape(1), base[0, :16], side // 2 * cols)
     near = spread(targets, (0, 1), 2).reshape(side // 2, parents, block_rows, width)
-    base = leaf(leaf_rhs, leaf_inv, par_x)
+    folded = fold(leaf_inv, leaf_off, par_x)
     near, base, folded, x_out = lax.optimization_barrier(
         (near, base, folded, lax.ppermute(par_x, both, turn))
     )

time: 110 us -> 109 us (level)
  waiting for transfers between devices: 21.6 us -> 19.5 us
  starting transfers between devices: 34.4 us -> 36.1 us
    all_to_all x2, starting transfers between devices: 18.1 us -> 21.4 us  [spread(): return lax.all_to_all(a, both, 0, 0, axis_index_groups=groups, tiled=True)]
    ppermute x1, starting transfers between devices: 1.17 us -> 0.01 us  [on_device(): near_other = lax.ppermute(near, 'row', swap)]
  transfers between devices with their start and end apart: 17 -> 17, of which waited for: 8 -> 7; matrix products, arithmetic and copies ran while one was open for 6% -> 6% of each run, Pallas kernels for 34% -> 34%
where the time goes in v5:
time: 109 us; the launch traced here: 108 us
  Pallas kernels  45.1 us (41%)
  starting transfers between devices  36.1 us (33%)
  waiting for transfers between devices  19.5 us (18%)
  other arithmetic  4.51 us (4%)
  local copies, waits for them, and re-layouts  2.32 us (2%)
    all_to_all x2, starting transfers between devices, spread(): return lax.all_to_all(a, both, 0, 0, axis_index_groups=groups, tiled=True)  21.4 us
    pallas_call x2, Pallas kernels, backward(): pl.pallas_call(functools.partial(backward_kernel, g, fanout, len(xs)), in...  13.6 us
    pallas_call x1, Pallas kernels, forward(): pl.pallas_call(functools.partial(forward_kernel, g, fanout), in_specs=[sm...  12.7 us
    all_to_all x2, waiting for transfers between devices, spread(): return lax.all_to_all(a, both, 0, 0, axis_index_groups=groups, tiled=True)  12.6 us
    pallas_call x1, Pallas kernels, leaf(): pl.pallas_call(functools.partial(leaf_kernel, g), grid=(leaves // g,), in...  9.75 us
    pallas_call x1, Pallas kernels, fold(): pl.pallas_call(functools.partial(fold_kernel, g, fanout), grid=(leaves //...  7.41 us
    ppermute x4, starting transfers between devices, along(): lax.ppermute(a, both, [(device(u, c, v, y), device(u + step, c, v, y)) fo...  5.42 us
    ppermute x3, starting transfers between devices, on_device(): lax.ppermute(pair, 'row', [(r, (r + CORES * s) % rows) for r in range(row...  4.61 us
  transfers between devices with their start and end apart: 17, of which 7 were waited for; matrix products, arithmetic and copies ran while one was open for 6% of the time, Pallas kernels for 34%

profile of v5, /device:TPU:1, one launch (start us, length us, event | category | flops | bytes accessed | tf_op | source)
XLA Modules:
  0.0 108.3 jit_solution(8358341689800203021)
XLA Ops:
  0.6 1.5 %collective-permute-start.1 = (bf16[2,16,128]{2,1,0:T(8,128)(2,1)}, bf16[2,16,128]{2,1,0:T(8,128)(2,1)S(1)}, u32[]{:S(2)}, u32[]{:S(2)}) collective-permute-start(bf16[2,16,128]{2,1,0:T(8,128)(2,1)} %param.11), channel_id=1, source_target_pairs={{0,16},{16,0},{32,48},{48,32},{64,80},{80,64},{96,112},{112,96},{1... | collective-permute-start | bytes 24584 | tf_op jit(solution)/shard_map/ppermute | solution.py:388
  2.1 0.8 copy.9
  2.9 0.1 reshape.25.blocks
  3.0 0.1 concatenate.13.which
  3.1 12.7 %forward.1 = (bf16[2,32,64,128]{3,2,1,0:T(8,128)(2,1)S(1)}, bf16[2,32,64,128]{3,2,1,0:T(8,128)(2,1)S(1)}, bf16[2,32,64,128]{3,2,1,0:T(8,128)(2,1)S(1)}, bf16[2,32,64,128]{3,2,1,0:T(8,128)(2,1)S(1)}) custom-call(s32[144]{0:T(256)S(1)} %reshape.25.blocks, s32[8]{0:T(128)S(1)} %concatenate.13.which, bf16[48,8,64,128]{3,2,1,0:T(8,128)(2,1)} %bitcast.22, ...), custom_call_target="tpu_custom_call" | custom-call | flops 7000000000 | bytes 19000000 | tf_op jit(solution)/shard_map/forward/pallas_call | solution.py:109
  15.8 0.0 collective-permute-done.1
  15.8 0.3 collective-permute-start.2
  16.1 0.3 collective-permute-start
  16.4 2.1 %collective-permute-done.2 = bf16[2,32,64,128]{3,2,1,0:T(8,128)(2,1)S(1)} collective-permute-done((bf16[2,32,64,128]{3,2,1,0:T(8,128)(2,1)S(1)}, bf16[2,32,64,128]{3,2,1,0:T(8,128)(2,1)S(1)}, u32[]{:S(2)}, u32[]{:S(2)}) %collective-permute-start.2) | collective-permute-done | bytes 1048608 | tf_op jit(solution)/shard_map/ppermute | solution.py:406
  18.6 1.4 %add_convert_fusion.3 = (bf16[1,32,64,128]{3,2,1,0:T(8,128)(2,1)}, bf16[1,32,64,128]{3,2,1,0:T(8,128)(2,1)}) fusion(bf16[2,32,64,128]{3,2,1,0:T(8,128)(2,1)S(1)} %collective-permute-done.2, bf16[2,32,64,128]{3,2,1,0:T(8,128)(2,1)S(1)} %get-tuple-element.24), kind=kLoop, calls=%fused_computation.5 | loop fusion | flops 2097152 | bytes 3145728 | tf_op jit(solution)/shard_map/convert_element_type | solution.py:406
  19.9 1.3 %collective-permute-start.3 = (bf16[1,32,64,128]{3,2,1,0:T(8,128)(2,1)}, bf16[1,32,64,128]{3,2,1,0:T(8,128)(2,1)}, u32[]{:S(2)}, u32[]{:S(2)}) collective-permute-start(bf16[1,32,64,128]{3,2,1,0:T(8,128)(2,1)} %get-tuple-element.44), channel_id=1, source_target_pairs={{0,32},{1,33},{2,34},{3,35},{4,36},{5,37},{6,38},{7,39},{8,40},{9,... | collective-permute-start | bytes 1572872 | tf_op jit(solution)/shard_map/ppermute | solution.py:365
  21.2 1.4 %collective-permute-start.4 = (bf16[1,32,64,128]{3,2,1,0:T(8,128)(2,1)}, bf16[1,32,64,128]{3,2,1,0:T(8,128)(2,1)}, u32[]{:S(2)}, u32[]{:S(2)}) collective-permute-start(bf16[1,32,64,128]{3,2,1,0:T(8,128)(2,1)} %get-tuple-element.45), channel_id=1, source_target_pairs={{0,96},{1,97},{2,98},{3,99},{4,100},{5,101},{6,102},{7,103},{8,104... | collective-permute-start | bytes 1572872 | tf_op jit(solution)/shard_map/ppermute | solution.py:365
  22.6 3.9 %collective-permute-start.7 = (bf16[2,32,128]{2,1,0:T(8,128)(2,1)S(1)}, bf16[2,32,128]{2,1,0:T(8,128)(2,1)S(1)}, u32[]{:S(2)}, u32[]{:S(2)}) collective-permute-start(bf16[2,32,128]{2,1,0:T(8,128)(2,1)S(1)} %pad_maximum_fusion.1), channel_id=1, source_target_pairs={{0,96},{16,112},{32,0},{48,16},{64,32},{80,48},{96,64},{112,80},{1... | collective-permute-start | bytes 49160 | tf_op jit(solution)/shard_map/ppermute | solution.py:402
  26.6 0.0 collective-permute-start.6
  26.6 0.7 collective-permute-start.5
  27.3 2.5 %collective-permute-done.3 = bf16[1,32,64,128]{3,2,1,0:T(8,128)(2,1)} collective-permute-done((bf16[1,32,64,128]{3,2,1,0:T(8,128)(2,1)}, bf16[1,32,64,128]{3,2,1,0:T(8,128)(2,1)}, u32[]{:S(2)}, u32[]{:S(2)}) %collective-permute-start.3) | collective-permute-done | bytes 524320 | tf_op jit(solution)/shard_map/ppermute | solution.py:365
  29.8 0.1 collective-permute-done.4
  29.9 1.9 %add_convert_fusion.1 = (bf16[1,32,64,128]{3,2,1,0:T(8,128)(2,1)S(1)}, bf16[1,32,64,128]{3,2,1,0:T(8,128)(2,1)S(1)}) fusion(bf16[1,32,64,128]{3,2,1,0:T(8,128)(2,1)} %collective-permute-done.4, bf16[1,32,64,128]{3,2,1,0:T(8,128)(2,1)} %collective-permute-done.3, bf16[2,32,64,128]{3,2,1,0:T(8,128)(2,1)S(1)} %collective-permute-done, ...), kind=kLoop, calls=%fused_computation.2 | loop fusion | flops 3932160 | bytes 4194306 | tf_op jit(solution)/shard_map/convert_element_type | solution.py:417
  31.7 1.1 pad_maximum_fusion
  32.8 0.0 collective-permute-done.7
  32.8 0.0 collective-permute-done.6
  32.8 0.0 collective-permute-done.5
  32.8 10.2 %all-to-all-start = ((bf16[32,2,64,128]{3,2,1,0:T(8,128)(2,1)}), bf16[32,2,64,128]{3,2,1,0:T(8,128)(2,1)S(1)}, u32[]{:S(2)}, u32[]{:S(2)}) async-start(bf16[32,2,64,128]{3,2,1,0:T(8,128)(2,1)} %bitcast.9), calls=%async_computation | async-start | bytes 2097152 | tf_op jit(solution)/shard_map/all_to_all | solution.py:375
  43.0 9.8 %leaf.1 = bf16[48,512,128]{2,1,0:T(8,128)(2,1)} custom-call(bf16[48,512,128]{2,1,0:T(8,128)(2,1)} %rhs.1, bf16[48,128,128]{2,1,0:T(8,128)(2,1)} %inv.3), custom_call_target="tpu_custom_call" | custom-call | flops 6000000000 | bytes 20000000 | tf_op jit(solution)/shard_map/leaf/pallas_call | solution.py:187
  52.8 0.7 collective-permute-start.8
  53.5 0.7 slice_bitcast_fusion.after
  54.2 0.0 collective-permute-done.8.given
  54.2 3.8 %all-to-all-done.got = bf16[32,2,64,128]{3,2,1,0:T(8,128)(2,1)S(1)} async-done(((bf16[32,2,64,128]{3,2,1,0:T(8,128)(2,1)}), bf16[32,2,64,128]{3,2,1,0:T(8,128)(2,1)S(1)}, u32[]{:S(2)}, u32[]{:S(2)}) %all-to-all-start) | async-done | bytes 1048608 | tf_op jit(solution)/shard_map/all_to_all | solution.py:375
  58.0 1.6 %parent.1 = (bf16[2,64,128]{2,1,0:T(8,128)(2,1)S(1)}, bf16[32,2,64,128]{3,2,1,0:T(8,128)(2,1)}) custom-call(bf16[32,2,64,128]{3,2,1,0:T(8,128)(2,1)S(1)} %all-to-all-done.got, bf16[2,192,128]{2,1,0:T(8,128)(2,1)S(1)} %collective-permute-done.8.given, s32[1]{0:T(128)} %bitcast.10.place, bf16[16,128]{1,0:T(8,128)(2,1)S(1)} %slice_bitcast_fusion.after), custom_call_target="tpu_custom_call" | custom-call | flops 30000000 | bytes 4500000 | tf_op jit(solution)/shard_map/parent/pallas_call | solution.py:236
  59.6 11.2 %all-to-all-start.1 = ((bf16[32,2,64,128]{3,2,1,0:T(8,128)(2,1)}), bf16[32,2,64,128]{3,2,1,0:T(8,128)(2,1)S(1)}, u32[]{:S(2)}, u32[]{:S(2)}) async-start(bf16[32,2,64,128]{3,2,1,0:T(8,128)(2,1)} %get-tuple-element.33), calls=%async_computation.1 | async-start | bytes 2097152 | tf_op jit(solution)/shard_map/all_to_all | solution.py:375
  70.8 0.7 collective-permute-start.9
  71.5 7.4 %fold.1.folded_hbm = bf16[48,384,128]{2,1,0:T(8,128)(2,1)} custom-call(bf16[48,128,128]{2,1,0:T(8,128)(2,1)} %inv.3, bf16[48,3,128,128]{3,2,1,0:T(8,128)(2,1)} %off.1, bf16[2,64,128]{2,1,0:T(8,128)(2,1)} %copy-done), custom_call_target="tpu_custom_call" | custom-call | flops 4000000000 | bytes 15000000 | tf_op jit(solution)/shard_map/fold/pallas_call | solution.py:150
  78.9 0.0 collective-permute-done.9
  78.9 8.8 %all-to-all-done.1 = bf16[32,2,64,128]{3,2,1,0:T(8,128)(2,1)S(1)} async-done(((bf16[32,2,64,128]{3,2,1,0:T(8,128)(2,1)}), bf16[32,2,64,128]{3,2,1,0:T(8,128)(2,1)S(1)}, u32[]{:S(2)}, u32[]{:S(2)}) %all-to-all-start.1) | async-done | bytes 1048608 | tf_op jit(solution)/shard_map/all_to_all | solution.py:375
  87.7 0.1 slice_select_fusion
  87.7 0.4 collective-permute-start.11
  88.1 2.4 %collective-permute-start.10 = (bf16[1,32,64,128]{3,2,1,0:T(8,128)(2,1)S(1)}, bf16[1,32,64,128]{3,2,1,0:T(8,128)(2,1)S(1)}, u32[]{:S(2)}, u32[]{:S(2)}) collective-permute-start(bf16[1,32,64,128]{3,2,1,0:T(8,128)(2,1)S(1)} %slice_select_fusion), channel_id=1, source_target_pairs={{0,96},{1,97},{2,98},{3,99},{4,100},{5,101},{6,102},{7,103},{8,104... | collective-permute-start | bytes 1572872 | tf_op jit(solution)/shard_map/ppermute | solution.py:365
  90.5 0.1 pad_add_fusion.1.which
  90.5 6.9 %backward.2.rest_4_ = bf16[48,8,64,128]{3,2,1,0:T(8,128)(2,1)} custom-call(s32[144]{0:T(256)S(1)} %reshape.25.blocks, s32[4]{0:T(128)S(1)} %pad_add_fusion.1.which, bf16[48,8,64,128]{3,2,1,0:T(8,128)(2,1)} %bitcast.19, bf16[48,384,128]{2,1,0:T(8,128)(2,1)} %fold.1.folded_hbm, bf16[2,32,64,128]{3,2,1,0:T(8,128)(2,1)S(1)} %bitcast.18, ...), custom_call_target="tpu_custom_call" | custom-call | flops 5000000000 | bytes 13000000 | tf_op jit(solution)/shard_map/backward/pallas_call | solution.py:318
  97.5 0.0 collective-permute-done.11.rest_1_
  97.5 0.0 collective-permute-done.10.rest_0_
  97.5 1.2 %collective-permute-start.13 = (bf16[1,32,64,128]{3,2,1,0:T(8,128)(2,1)S(1)}, bf16[1,32,64,128]{3,2,1,0:T(8,128)(2,1)S(1)}, u32[]{:S(2)}, u32[]{:S(2)}) collective-permute-start(bf16[1,32,64,128]{3,2,1,0:T(8,128)(2,1)S(1)} %collective-permute-done.10.rest_0_), channel_id=1, source_target_pairs={{0,16},{16,0},{32,48},{48,32},{64,80},{80,64},{96,112},{112,96},{1... | collective-permute-start | bytes 1572872 | tf_op jit(solution)/shard_map/ppermute | solution.py:439
  98.7 0.1 collective-permute-start.14
  98.8 0.1 pad_add_fusion.which
  98.8 1.4 %collective-permute-done.13.rest_2_ = bf16[1,32,64,128]{3,2,1,0:T(8,128)(2,1)S(1)} collective-permute-done((bf16[1,32,64,128]{3,2,1,0:T(8,128)(2,1)S(1)}, bf16[1,32,64,128]{3,2,1,0:T(8,128)(2,1)S(1)}, u32[]{:S(2)}, u32[]{:S(2)}) %collective-permute-start.13) | collective-permute-done | bytes 524320 | tf_op jit(solution)/shard_map/ppermute | solution.py:439
  100.2 0.7 collective-permute-done.14.rest_3_
  101.0 6.7 %backward.3 = bf16[48,8,64,128]{3,2,1,0:T(8,128)(2,1)} custom-call(s32[144]{0:T(256)S(1)} %reshape.25.blocks, s32[4]{0:T(128)S(1)} %pad_add_fusion.which, bf16[48,8,64,128]{3,2,1,0:T(8,128)(2,1)} %bitcast.20, bf16[48,384,128]{2,1,0:T(8,128)(2,1)} %fold.1.folded_hbm, ...), custom_call_target="tpu_custom_call", output_to_operand_aliasing={{}: (8, {})} | custom-call | flops 5000000000 | bytes 13000000 | tf_op jit(solution)/shard_map/backward/pallas_call | solution.py:318
  107.6 0.6 copy.16
  (16 shorter events, 0.1 us)
Async XLA Ops:
  0.6 15.2 %collective-permute-start.1 = (bf16[2,16,128]{2,1,0:T(8,128)(2,1)}, bf16[2,16,128]{2,1,0:T(8,128)(2,1)S(1)}, u32[]{:S(2)}, u32[]{:S(2)}) collective-permute-start(bf16[2,16,128]{2,1,0:T(8,128)(2,1)} %param.11), channel_id=1, source_target_pairs={{0,16},{16,0},{32,48},{48,32},{64,80},{80,64},{96,112},{112,96},{1... | collective-permute-start | bytes 24584 | tf_op jit(solution)/shard_map/ppermute | solution.py:388
  3.1 19.5 %copy-start.1 = (bf16[2,64,128]{2,1,0:T(8,128)(2,1)S(1)}, bf16[2,64,128]{2,1,0:T(8,128)(2,1)}, u32[]{:S(2)}) copy-start(bf16[2,64,128]{2,1,0:T(8,128)(2,1)} %param.10) | copy-start | bytes 98308
  3.1 19.5 %copy-start.2 = (bf16[2,16,128]{2,1,0:T(8,128)(2,1)S(1)}, bf16[2,16,128]{2,1,0:T(8,128)(2,1)}, u32[]{:S(2)}) copy-start(bf16[2,16,128]{2,1,0:T(8,128)(2,1)} %param.11) | copy-start | bytes 24580
  15.8 2.7 %collective-permute-start.2 = (bf16[2,32,64,128]{3,2,1,0:T(8,128)(2,1)S(1)}, bf16[2,32,64,128]{3,2,1,0:T(8,128)(2,1)S(1)}, u32[]{:S(2)}, u32[]{:S(2)}) collective-permute-start(bf16[2,32,64,128]{3,2,1,0:T(8,128)(2,1)S(1)} %get-tuple-element.26), channel_id=1, source_target_pairs={{0,16},{16,0},{32,48},{48,32},{64,80},{80,64},{96,112},{112,96},{1... | collective-permute-start | bytes 3145736 | tf_op jit(solution)/shard_map/ppermute | solution.py:406
  16.1 10.4 %collective-permute-start = (bf16[2,32,64,128]{3,2,1,0:T(8,128)(2,1)S(1)}, bf16[2,32,64,128]{3,2,1,0:T(8,128)(2,1)S(1)}, u32[]{:S(2)}, u32[]{:S(2)}) collective-permute-start(bf16[2,32,64,128]{3,2,1,0:T(8,128)(2,1)S(1)} %get-tuple-element.23), channel_id=1, source_target_pairs={{0,16},{16,0},{32,48},{48,32},{64,80},{80,64},{96,112},{112,96},{1... | collective-permute-start | bytes 3145736 | tf_op jit(solution)/shard_map/ppermute | solution.py:409
  19.9 9.9 %collective-permute-start.3 = (bf16[1,32,64,128]{3,2,1,0:T(8,128)(2,1)}, bf16[1,32,64,128]{3,2,1,0:T(8,128)(2,1)}, u32[]{:S(2)}, u32[]{:S(2)}) collective-permute-start(bf16[1,32,64,128]{3,2,1,0:T(8,128)(2,1)} %get-tuple-element.44), channel_id=1, source_target_pairs={{0,32},{1,33},{2,34},{3,35},{4,36},{5,37},{6,38},{7,39},{8,40},{9,... | collective-permute-start | bytes 1572872 | tf_op jit(solution)/shard_map/ppermute | solution.py:365
  21.2 8.6 %collective-permute-start.4 = (bf16[1,32,64,128]{3,2,1,0:T(8,128)(2,1)}, bf16[1,32,64,128]{3,2,1,0:T(8,128)(2,1)}, u32[]{:S(2)}, u32[]{:S(2)}) collective-permute-start(bf16[1,32,64,128]{3,2,1,0:T(8,128)(2,1)} %get-tuple-element.45), channel_id=1, source_target_pairs={{0,96},{1,97},{2,98},{3,99},{4,100},{5,101},{6,102},{7,103},{8,104... | collective-permute-start | bytes 1572872 | tf_op jit(solution)/shard_map/ppermute | solution.py:365
  22.6 10.1 %collective-permute-start.7 = (bf16[2,32,128]{2,1,0:T(8,128)(2,1)S(1)}, bf16[2,32,128]{2,1,0:T(8,128)(2,1)S(1)}, u32[]{:S(2)}, u32[]{:S(2)}) collective-permute-start(bf16[2,32,128]{2,1,0:T(8,128)(2,1)S(1)} %pad_maximum_fusion.1), channel_id=1, source_target_pairs={{0,96},{16,112},{32,0},{48,16},{64,32},{80,48},{96,64},{112,80},{1... | collective-permute-start | bytes 49160 | tf_op jit(solution)/shard_map/ppermute | solution.py:402
  26.6 6.2 %collective-permute-start.6 = (bf16[2,32,128]{2,1,0:T(8,128)(2,1)S(1)}, bf16[2,32,128]{2,1,0:T(8,128)(2,1)S(1)}, u32[]{:S(2)}, u32[]{:S(2)}) collective-permute-start(bf16[2,32,128]{2,1,0:T(8,128)(2,1)S(1)} %pad_maximum_fusion.1), channel_id=1, source_target_pairs={{0,64},{16,80},{32,96},{48,112},{64,0},{80,16},{96,32},{112,48},{1... | collective-permute-start | bytes 49160 | tf_op jit(solution)/shard_map/ppermute | solution.py:402
  26.6 6.2 %collective-permute-start.5 = (bf16[2,32,128]{2,1,0:T(8,128)(2,1)S(1)}, bf16[2,32,128]{2,1,0:T(8,128)(2,1)S(1)}, u32[]{:S(2)}, u32[]{:S(2)}) collective-permute-start(bf16[2,32,128]{2,1,0:T(8,128)(2,1)S(1)} %pad_maximum_fusion.1), channel_id=1, source_target_pairs={{0,32},{16,48},{32,64},{48,80},{64,96},{80,112},{96,0},{112,16},{1... | collective-permute-start | bytes 49160 | tf_op jit(solution)/shard_map/ppermute | solution.py:402
  32.8 25.2 %all-to-all-start = ((bf16[32,2,64,128]{3,2,1,0:T(8,128)(2,1)}), bf16[32,2,64,128]{3,2,1,0:T(8,128)(2,1)S(1)}, u32[]{:S(2)}, u32[]{:S(2)}) async-start(bf16[32,2,64,128]{3,2,1,0:T(8,128)(2,1)} %bitcast.9), calls=%async_computation | async-start | bytes 2097152 | tf_op jit(solution)/shard_map/all_to_all | solution.py:375
  52.8 1.4 %collective-permute-start.8 = (bf16[2,192,128]{2,1,0:T(8,128)(2,1)S(1)}, bf16[2,192,128]{2,1,0:T(8,128)(2,1)S(1)}, u32[]{:S(2)}, u32[]{:S(2)}) collective-permute-start(bf16[2,192,128]{2,1,0:T(8,128)(2,1)S(1)} %constant_dynamic-update-slice_fusion), channel_id=1, source_target_pairs={{0,0},{1,1},{2,2},{3,3},{4,4},{5,5},{6,6},{7,7},{8,8},{9,9},{10,10... | collective-permute-start | bytes 294920 | tf_op jit(solution)/shard_map/ppermute | solution.py:424
  59.6 11.8 %copy-start = (bf16[2,64,128]{2,1,0:T(8,128)(2,1)}, bf16[2,64,128]{2,1,0:T(8,128)(2,1)S(1)}, u32[]{:S(2)}) copy-start(bf16[2,64,128]{2,1,0:T(8,128)(2,1)S(1)} %get-tuple-element.34.after) | copy-start | bytes 98308
  59.6 28.0 %all-to-all-start.1 = ((bf16[32,2,64,128]{3,2,1,0:T(8,128)(2,1)}), bf16[32,2,64,128]{3,2,1,0:T(8,128)(2,1)S(1)}, u32[]{:S(2)}, u32[]{:S(2)}) async-start(bf16[32,2,64,128]{3,2,1,0:T(8,128)(2,1)} %get-tuple-element.33), calls=%async_computation.1 | async-start | bytes 2097152 | tf_op jit(solution)/shard_map/all_to_all | solution.py:375
  70.8 8.1 %collective-permute-start.9 = (bf16[2,64,128]{2,1,0:T(8,128)(2,1)S(1)}, bf16[2,64,128]{2,1,0:T(8,128)(2,1)S(1)}, u32[]{:S(2)}, u32[]{:S(2)}) collective-permute-start(bf16[2,64,128]{2,1,0:T(8,128)(2,1)S(1)} %get-tuple-element.34.after), channel_id=1, source_target_pairs={{0,0},{1,1},{2,2},{3,3},{4,4},{5,5},{6,6},{7,7},{8,8},{9,9},{10,10... | collective-permute-start | bytes 98312 | tf_op jit(solution)/shard_map/ppermute | solution.py:429
  87.7 2.9 %collective-permute-start.12 = (bf16[2,32,64,128]{3,2,1,0:T(8,128)(2,1)S(1)}, bf16[2,32,64,128]{3,2,1,0:T(8,128)(2,1)S(1)}, u32[]{:S(2)}, u32[]{:S(2)}) collective-permute-start(bf16[2,32,64,128]{3,2,1,0:T(8,128)(2,1)S(1)} %bitcast.16), channel_id=1, source_target_pairs={{0,16},{16,0},{32,48},{48,32},{64,80},{80,64},{96,112},{112,96},{1... | collective-permute-start | bytes 3145736 | tf_op jit(solution)/shard_map/ppermute | solution.py:434
  87.7 9.8 %collective-permute-start.11 = (bf16[1,32,64,128]{3,2,1,0:T(8,128)(2,1)S(1)}, bf16[1,32,64,128]{3,2,1,0:T(8,128)(2,1)S(1)}, u32[]{:S(2)}, u32[]{:S(2)}) collective-permute-start(bf16[1,32,64,128]{3,2,1,0:T(8,128)(2,1)S(1)} %slice_select_fusion), channel_id=1, source_target_pairs={{0,32},{1,33},{2,34},{3,35},{4,36},{5,37},{6,38},{7,39},{8,40},{9,... | collective-permute-start | bytes 1572872 | tf_op jit(solution)/shard_map/ppermute | solution.py:365
  88.1 9.4 %collective-permute-start.10 = (bf16[1,32,64,128]{3,2,1,0:T(8,128)(2,1)S(1)}, bf16[1,32,64,128]{3,2,1,0:T(8,128)(2,1)S(1)}, u32[]{:S(2)}, u32[]{:S(2)}) collective-permute-start(bf16[1,32,64,128]{3,2,1,0:T(8,128)(2,1)S(1)} %slice_select_fusion), channel_id=1, source_target_pairs={{0,96},{1,97},{2,98},{3,99},{4,100},{5,101},{6,102},{7,103},{8,104... | collective-permute-start | bytes 1572872 | tf_op jit(solution)/shard_map/ppermute | solution.py:365
  97.5 2.7 %collective-permute-start.13 = (bf16[1,32,64,128]{3,2,1,0:T(8,128)(2,1)S(1)}, bf16[1,32,64,128]{3,2,1,0:T(8,128)(2,1)S(1)}, u32[]{:S(2)}, u32[]{:S(2)}) collective-permute-start(bf16[1,32,64,128]{3,2,1,0:T(8,128)(2,1)S(1)} %collective-permute-done.10.rest_0_), channel_id=1, source_target_pairs={{0,16},{16,0},{32,48},{48,32},{64,80},{80,64},{96,112},{112,96},{1... | collective-permute-start | bytes 1572872 | tf_op jit(solution)/shard_map/ppermute | solution.py:439
  98.7 2.3 %collective-permute-start.14 = (bf16[1,32,64,128]{3,2,1,0:T(8,128)(2,1)S(1)}, bf16[1,32,64,128]{3,2,1,0:T(8,128)(2,1)S(1)}, u32[]{:S(2)}, u32[]{:S(2)}) collective-permute-start(bf16[1,32,64,128]{3,2,1,0:T(8,128)(2,1)S(1)} %collective-permute-done.11.rest_1_), channel_id=1, source_target_pairs={{0,16},{16,0},{32,48},{48,32},{64,80},{80,64},{96,112},{112,96},{1... | collective-permute-start | bytes 1572872 | tf_op jit(solution)/shard_map/ppermute | solution.py:439
